TPU v7x, 32 devices: a whole 2x2x4 slice. The times are simulated.
32 devices in a mesh: leaf: 32 (over z, y, x, core).
Axes of the slice: x: 2, y: 2, z: 4, core: 2. Of those that a mesh axis runs over, the one named last changes fastest.
Arguments:
- coords: float32 [3, 16384], P(None, 'leaf'), may hold values from 0 to 32, as said below
- weights: float32 [16384, 256], P('leaf'), may hold values from -6 to 6
- near_mask: int32 [32, 4], P('leaf'), may hold values 0 or 1
- leaf_inverse: float32 [16384, 512], P('leaf'), may hold values from -0.25 to 0.25
- up_basis: float32 [4, 16384, 512], P(None, 'leaf'), may hold values from -0.25 to 0.25
- coupling: float32 [4, 16384, 1024], P(None, 'leaf'), may hold values from -0.1875 to 0.1875
- down_basis: float32 [4, 16384, 512], P(None, 'leaf'), may hold values from -0.125 to 0.125
Outputs:
- solution: float32 [16384, 256], P('leaf')
Inputs may be any that keep to these rules, and one draw needn't show every extreme that they name: The points of leaf i have i * 512 / 1024 <= coords[0] <= (i + 1) * 512 / 1024; their other two coordinates lie in [0, 32).
All inputs are finite; a program needn't handle non-finite values. No bound on the sum of `near_mask` on one device may be relied on, other than what follows from the above.
Results may differ from a plain program's by a relative error of at most 0.0003.
Values sent between devices are 32-bit elements; how exact they have to be, the bound alone decides.
No kernel may reach another device: no remote copies, remote signals or barrier semaphores. Data moves between devices by JAX's collectives and lax.ppermute only.
A program may use at most 64 MiB of HBM per device.

v0:
```python
import math

import jax
import jax.numpy as jnp
from jax import lax
from jax.sharding import PartitionSpec as P

LEVELS = 4


OFFSETS = (-2, -1, 1, 2)


def from_partner(x, axis, bit):
    return lax.ppermute(x, axis, [(i, i ^ 1 << bit) for i in range(lax.axis_size(axis))])


def passed_along(value, axis, steps):
    count = lax.axis_size(axis)
    first, last = (max(0, -steps), min(count, count - steps))
    return lax.ppermute(value, axis, [(source, source + steps) for source in range(first, last)])


def gauss(left, right):
    dist = jnp.zeros((left.shape[1], right.shape[1]), jnp.float32)
    for coord in range(3):
        diff = left[coord][:, None] - right[coord][None, :]
        dist = dist + diff * diff
    return jnp.exp(-0.5 * dist)


def kernel_tile(own_points, other_points, values):
    return jnp.dot(
        gauss(own_points, other_points),
        values,
        precision=lax.Precision.HIGHEST,
        preferred_element_type=jnp.float32,
    )


def level_step(iterate, level, up_basis, coupling, down_basis):
    skeleton = lax.dot_general(
        up_basis[level],
        iterate,
        (((0,), (0,)), ((), ())),
        precision=lax.Precision.HIGHEST,
        preferred_element_type=jnp.float32,
    )
    for lower in range(level):
        skeleton = skeleton + from_partner(skeleton, "leaf", lower)
    partner = from_partner(skeleton, "leaf", level)
    stacked = jnp.concatenate([skeleton, partner], axis=0)
    correction = jnp.dot(
        coupling[level],
        stacked,
        precision=lax.Precision.HIGHEST,
        preferred_element_type=jnp.float32,
    ) * (1.0 / math.sqrt(2.0 ** (level + 1)))
    return iterate - jnp.dot(
        down_basis[level],
        correction,
        precision=lax.Precision.HIGHEST,
        preferred_element_type=jnp.float32,
    )


def per_device(coords, weights, near_mask, leaf_inverse, up_basis, coupling, down_basis):
    total = kernel_tile(coords, coords, weights)
    for slot, offset in enumerate(OFFSETS):
        other_points, other_values = passed_along((coords, weights), "leaf", -offset)
        total = total + near_mask[0, slot].astype(jnp.float32) * kernel_tile(
            coords, other_points, other_values
        )
    near = total * 0.5
    iterate = jnp.dot(
        leaf_inverse, near, precision=lax.Precision.HIGHEST, preferred_element_type=jnp.float32
    )
    for level in range(LEVELS):
        iterate = level_step(iterate, level, up_basis, coupling, down_basis)
    return iterate


def solution(mesh):
    in_specs = (
        P(None, "leaf"),
        P("leaf", None),
        P("leaf", None),
        P("leaf", None),
        P(None, "leaf", None),
        P(None, "leaf", None),
        P(None, "leaf", None),
    )
    out_specs = P("leaf", None)
    return jax.shard_map(
        per_device, mesh=mesh, in_specs=in_specs, out_specs=out_specs, check_vma=False
    )
```

profile of v0, /device:TPU:0, one launch (start us, length us, event | category | flops | bytes accessed | tf_op | source)
XLA Modules:
  0.0 162.4 jit_solution(7256304585391315059)
XLA Ops:
  0.0 1.4 collective-permute-start.4
  1.4 3.0 %collective-permute-start.2 = (f32[3,512]{1,0:T(4,128)}, f32[3,512]{1,0:T(4,128)S(1)}, u32[]{:S(2)}, u32[]{:S(2)}) collective-permute-start(f32[3,512]{1,0:T(4,128)} %param.7), channel_id=1, source_target_pairs={{0,1},{1,2},{2,3},{3,4},{4,5},{5,6},{6,7},{7,8},{8,9},{9,10},{10,1... | collective-permute-start | bytes 18440 | tf_op jit(solution)/shard_map/ppermute | solution.py:21
  4.5 1.3 collective-permute-start.5
  5.8 5.1 %collective-permute-start.3 = (f32[512,256]{1,0:T(8,128)}, f32[512,256]{1,0:T(8,128)S(1)}, u32[]{:S(2)}, u32[]{:S(2)}) collective-permute-start(f32[512,256]{1,0:T(8,128)} %param.8), channel_id=1, source_target_pairs={{0,1},{1,2},{2,3},{3,4},{4,5},{5,6},{6,7},{7,8},{8,9},{9,10},{10,1... | collective-permute-start | bytes 1572872 | tf_op jit(solution)/shard_map/ppermute | solution.py:21
  10.9 1.3 collective-permute-start.6
  12.2 0.8 fusion.156
  13.0 2.4 %fusion.98 = f32[512,256]{1,0:T(8,128)S(1)} fusion(f32[512,256]{1,0:T(8,128)} %param.8, f32[512]{0:T(512)S(1)} %bitcast.95, f32[512]{0:T(512)S(1)} %bitcast.100, f32[512]{0:T(512)S(1)} %bitcast.90), kind=kOutput, calls=%fused_computation.102 | convolution fusion | flops 807665664 | bytes 1054720 | tf_op jit(solution)/shard_map/dot_general | solution.py:33
  15.4 1.5 fusion.158
  19.4 1.3 collective-permute-start.7
  20.8 5.5 %collective-permute-start = (f32[3,512]{1,0:T(4,128)}, f32[3,512]{1,0:T(4,128)S(1)}, u32[]{:S(2)}, u32[]{:S(2)}) collective-permute-start(f32[3,512]{1,0:T(4,128)} %param.7), channel_id=1, source_target_pairs={{0,2},{1,3},{2,4},{3,5},{4,6},{5,7},{6,8},{7,9},{8,10},{9,11},{10,... | collective-permute-start | bytes 18440 | tf_op jit(solution)/shard_map/ppermute | solution.py:21
  26.3 4.9 %collective-permute-start.1 = (f32[512,256]{1,0:T(8,128)}, f32[512,256]{1,0:T(8,128)S(1)}, u32[]{:S(2)}, u32[]{:S(2)}) collective-permute-start(f32[512,256]{1,0:T(8,128)} %param.8), channel_id=1, source_target_pairs={{0,2},{1,3},{2,4},{3,5},{4,6},{5,7},{6,8},{7,9},{8,10},{9,11},{10,... | collective-permute-start | bytes 1572872 | tf_op jit(solution)/shard_map/ppermute | solution.py:21
  31.2 1.4 convolution_multiply_fusion.1
  32.6 1.4 convolution_multiply_fusion.2
  33.9 1.3 collective-permute-done.7
  35.3 1.4 convolution_multiply_fusion
  36.6 15.0 %collective-permute-done.1 = f32[512,256]{1,0:T(8,128)S(1)} collective-permute-done((f32[512,256]{1,0:T(8,128)}, f32[512,256]{1,0:T(8,128)S(1)}, u32[]{:S(2)}, u32[]{:S(2)}) %collective-permute-start.1) | collective-permute-done | bytes 524320 | tf_op jit(solution)/shard_map/ppermute | solution.py:21
  51.6 1.4 fusion.29
  53.1 1.9 %fusion.159 = f32[256,512]{1,0:T(8,128)S(1)} fusion(f32[512,256]{1,0:T(8,128)S(1)} %fusion.29, f32[512,512]{1,0:T(8,128)S(1)} %copy-done), kind=kOutput, calls=%fused_computation.163 | convolution fusion | flops 805306368 | bytes 2097152 | tf_op jit(solution)/shard_map/dot_general | solution.py:75
  55.0 1.1 convolution_bitcast_fusion.3
  56.1 0.2 collective-permute-start.8
  56.3 1.8 %collective-permute-done.8 = f32[512,256]{0,1:T(8,128)S(1)} collective-permute-done((f32[512,256]{0,1:T(8,128)S(1)}, f32[512,256]{0,1:T(8,128)S(1)}, u32[]{:S(2)}, u32[]{:S(2)}) %collective-permute-start.8) | collective-permute-done | bytes 524320 | tf_op jit(solution)/shard_map/ppermute | solution.py:15
  58.1 1.9 %fusion.12 = f32[256,512]{1,0:T(8,128)S(1)} fusion(f32[4,512,1024]{2,1,0:T(8,128)S(1)} %bitcast.89, f32[512,256]{0,1:T(8,128)S(1)} %collective-permute-done.8, f32[512,256]{0,1:T(8,128)S(1)} %convolution_bitcast_fusion.3), kind=kOutput, calls=%fused_computation.12 | convolution fusion | flops 1611005952 | bytes 3670016 | tf_op jit(solution)/shard_map/dot_general | solution.py:53
  60.0 1.1 convolution_subtract_fusion.3
  61.1 1.2 convolution_bitcast_fusion.2
  62.3 0.2 collective-permute-start.9
  62.6 1.8 %collective-permute-done.9 = f32[512,256]{0,1:T(8,128)S(1)} collective-permute-done((f32[512,256]{0,1:T(8,128)S(1)}, f32[512,256]{0,1:T(8,128)S(1)}, u32[]{:S(2)}, u32[]{:S(2)}) %collective-permute-start.9) | collective-permute-done | bytes 524320 | tf_op jit(solution)/shard_map/ppermute | solution.py:15
  64.4 2.4 %collective-permute-start.10 = (f32[512,256]{0,1:T(8,128)S(1)}, f32[512,256]{0,1:T(8,128)S(1)}, u32[]{:S(2)}, u32[]{:S(2)}) collective-permute-start(f32[512,256]{0,1:T(8,128)S(1)} %add.74), channel_id=1, source_target_pairs={{0,2},{1,3},{2,0},{3,1},{4,6},{5,7},{6,4},{7,5},{8,10},{9,11},{10,... | collective-permute-start | bytes 1572872 | tf_op jit(solution)/shard_map/ppermute | solution.py:15
  66.9 12.2 %collective-permute-done.10 = f32[512,256]{0,1:T(8,128)S(1)} collective-permute-done((f32[512,256]{0,1:T(8,128)S(1)}, f32[512,256]{0,1:T(8,128)S(1)}, u32[]{:S(2)}, u32[]{:S(2)}) %collective-permute-start.10) | collective-permute-done | bytes 524320 | tf_op jit(solution)/shard_map/ppermute | solution.py:15
  79.1 1.9 %fusion.15 = f32[256,512]{1,0:T(8,128)S(1)} fusion(f32[4,512,1024]{2,1,0:T(8,128)S(1)} %bitcast.89, f32[512,256]{0,1:T(8,128)S(1)} %collective-permute-done.10, f32[512,256]{0,1:T(8,128)S(1)} %add.74), kind=kOutput, calls=%fused_computation.13 | convolution fusion | flops 1611005952 | bytes 3670016 | tf_op jit(solution)/shard_map/dot_general | solution.py:53
  81.0 1.1 convolution_subtract_fusion.2
  82.1 1.1 convolution_bitcast_fusion.1
  83.2 1.9 %collective-permute-done.11 = f32[512,256]{0,1:T(8,128)S(1)} collective-permute-done((f32[512,256]{0,1:T(8,128)S(1)}, f32[512,256]{0,1:T(8,128)S(1)}, u32[]{:S(2)}, u32[]{:S(2)}) %collective-permute-start.11) | collective-permute-done | bytes 524320 | tf_op jit(solution)/shard_map/ppermute | solution.py:15
  85.2 1.8 %collective-permute-start.12 = (f32[512,256]{0,1:T(8,128)S(1)}, f32[512,256]{0,1:T(8,128)S(1)}, u32[]{:S(2)}, u32[]{:S(2)}) collective-permute-start(f32[512,256]{0,1:T(8,128)S(1)} %add.75), channel_id=1, source_target_pairs={{0,2},{1,3},{2,0},{3,1},{4,6},{5,7},{6,4},{7,5},{8,10},{9,11},{10,... | collective-permute-start | bytes 1572872 | tf_op jit(solution)/shard_map/ppermute | solution.py:15
  87.0 12.2 %collective-permute-done.12 = f32[512,256]{0,1:T(8,128)S(1)} collective-permute-done((f32[512,256]{0,1:T(8,128)S(1)}, f32[512,256]{0,1:T(8,128)S(1)}, u32[]{:S(2)}, u32[]{:S(2)}) %collective-permute-start.12) | collective-permute-done | bytes 524320 | tf_op jit(solution)/shard_map/ppermute | solution.py:15
  99.4 13.1 %collective-permute-done.13 = f32[512,256]{0,1:T(8,128)S(1)} collective-permute-done((f32[512,256]{0,1:T(8,128)S(1)}, f32[512,256]{0,1:T(8,128)S(1)}, u32[]{:S(2)}, u32[]{:S(2)}) %collective-permute-start.13) | collective-permute-done | bytes 524320 | tf_op jit(solution)/shard_map/ppermute | solution.py:15
  112.5 1.9 %fusion.18 = f32[256,512]{1,0:T(8,128)S(1)} fusion(f32[4,512,1024]{2,1,0:T(8,128)S(1)} %bitcast.89, f32[512,256]{0,1:T(8,128)S(1)} %collective-permute-done.13, f32[512,256]{0,1:T(8,128)S(1)} %add.76), kind=kOutput, calls=%fused_computation.14 | convolution fusion | flops 1611005952 | bytes 3670016 | tf_op jit(solution)/shard_map/dot_general | solution.py:53
  114.5 1.1 convolution_subtract_fusion.1
  115.5 1.1 convolution_bitcast_fusion
  116.7 1.9 %collective-permute-done.14 = f32[512,256]{0,1:T(8,128)S(1)} collective-permute-done((f32[512,256]{0,1:T(8,128)S(1)}, f32[512,256]{0,1:T(8,128)S(1)}, u32[]{:S(2)}, u32[]{:S(2)}) %collective-permute-start.14) | collective-permute-done | bytes 524320 | tf_op jit(solution)/shard_map/ppermute | solution.py:15
  118.7 1.8 %collective-permute-start.15 = (f32[512,256]{0,1:T(8,128)S(1)}, f32[512,256]{0,1:T(8,128)S(1)}, u32[]{:S(2)}, u32[]{:S(2)}) collective-permute-start(f32[512,256]{0,1:T(8,128)S(1)} %add.77), channel_id=1, source_target_pairs={{0,2},{1,3},{2,0},{3,1},{4,6},{5,7},{6,4},{7,5},{8,10},{9,11},{10,... | collective-permute-start | bytes 1572872 | tf_op jit(solution)/shard_map/ppermute | solution.py:15
  120.5 12.2 %collective-permute-done.15 = f32[512,256]{0,1:T(8,128)S(1)} collective-permute-done((f32[512,256]{0,1:T(8,128)S(1)}, f32[512,256]{0,1:T(8,128)S(1)}, u32[]{:S(2)}, u32[]{:S(2)}) %collective-permute-start.15) | collective-permute-done | bytes 524320 | tf_op jit(solution)/shard_map/ppermute | solution.py:15
  132.8 0.4 collective-permute-start.16
  133.1 12.9 %collective-permute-done.16 = f32[512,256]{0,1:T(8,128)S(1)} collective-permute-done((f32[512,256]{0,1:T(8,128)S(1)}, f32[512,256]{0,1:T(8,128)S(1)}, u32[]{:S(2)}, u32[]{:S(2)}) %collective-permute-start.16) | collective-permute-done | bytes 524320 | tf_op jit(solution)/shard_map/ppermute | solution.py:15
  146.1 1.7 %collective-permute-start.17 = (f32[512,256]{0,1:T(8,128)S(1)}, f32[512,256]{0,1:T(8,128)S(1)}, u32[]{:S(2)}, u32[]{:S(2)}) collective-permute-start(f32[512,256]{0,1:T(8,128)S(1)} %add.79), channel_id=1, source_target_pairs={{0,8},{1,9},{2,10},{3,11},{4,12},{5,13},{6,14},{7,15},{8,0},{9,1},... | collective-permute-start | bytes 1572872 | tf_op jit(solution)/shard_map/ppermute | solution.py:15
  147.7 10.6 %collective-permute-done.17 = f32[512,256]{0,1:T(8,128)S(1)} collective-permute-done((f32[512,256]{0,1:T(8,128)S(1)}, f32[512,256]{0,1:T(8,128)S(1)}, u32[]{:S(2)}, u32[]{:S(2)}) %collective-permute-start.17) | collective-permute-done | bytes 524320 | tf_op jit(solution)/shard_map/ppermute | solution.py:15
  158.4 1.9 %fusion.21 = f32[256,512]{1,0:T(8,128)S(1)} fusion(f32[4,512,1024]{2,1,0:T(8,128)S(1)} %bitcast.89, f32[512,256]{0,1:T(8,128)S(1)} %collective-permute-done.17, f32[512,256]{0,1:T(8,128)S(1)} %add.79), kind=kOutput, calls=%fused_computation.15 | convolution fusion | flops 1611005952 | bytes 3670016 | tf_op jit(solution)/shard_map/dot_general | solution.py:53
  160.3 1.1 fusion.24
  161.4 1.0 copy.8
  (30 shorter events, 0.8 us)
Async XLA Ops:
  0.0 53.1 %copy-start = (f32[512,512]{1,0:T(8,128)S(1)}, f32[512,512]{1,0:T(8,128)}, u32[]{:S(2)}) copy-start(f32[512,512]{1,0:T(8,128)} %param.10) | copy-start | bytes 3145732
  0.0 19.4 %collective-permute-start.4 = (f32[3,512]{1,0:T(4,128)}, f32[3,512]{1,0:T(4,128)S(1)}, u32[]{:S(2)}, u32[]{:S(2)}) collective-permute-start(f32[3,512]{1,0:T(4,128)} %param.7), channel_id=1, source_target_pairs={{1,0},{2,1},{3,2},{4,3},{5,4},{6,5},{7,6},{8,7},{9,8},{10,9},{11,1... | collective-permute-start | bytes 18440 | tf_op jit(solution)/shard_map/ppermute | solution.py:21
  1.4 19.3 %collective-permute-start.2 = (f32[3,512]{1,0:T(4,128)}, f32[3,512]{1,0:T(4,128)S(1)}, u32[]{:S(2)}, u32[]{:S(2)}) collective-permute-start(f32[3,512]{1,0:T(4,128)} %param.7), channel_id=1, source_target_pairs={{0,1},{1,2},{2,3},{3,4},{4,5},{5,6},{6,7},{7,8},{8,9},{9,10},{10,1... | collective-permute-start | bytes 18440 | tf_op jit(solution)/shard_map/ppermute | solution.py:21
  4.5 26.7 %collective-permute-start.5 = (f32[512,256]{1,0:T(8,128)}, f32[512,256]{1,0:T(8,128)S(1)}, u32[]{:S(2)}, u32[]{:S(2)}) collective-permute-start(f32[512,256]{1,0:T(8,128)} %param.8), channel_id=1, source_target_pairs={{1,0},{2,1},{3,2},{4,3},{5,4},{6,5},{7,6},{8,7},{9,8},{10,9},{11,1... | collective-permute-start | bytes 1572872 | tf_op jit(solution)/shard_map/ppermute | solution.py:21
  5.8 26.8 %collective-permute-start.3 = (f32[512,256]{1,0:T(8,128)}, f32[512,256]{1,0:T(8,128)S(1)}, u32[]{:S(2)}, u32[]{:S(2)}) collective-permute-start(f32[512,256]{1,0:T(8,128)} %param.8), channel_id=1, source_target_pairs={{0,1},{1,2},{2,3},{3,4},{4,5},{5,6},{6,7},{7,8},{8,9},{9,10},{10,1... | collective-permute-start | bytes 1572872 | tf_op jit(solution)/shard_map/ppermute | solution.py:21
  10.9 15.4 %collective-permute-start.6 = (f32[3,512]{1,0:T(4,128)}, f32[3,512]{1,0:T(4,128)S(1)}, u32[]{:S(2)}, u32[]{:S(2)}) collective-permute-start(f32[3,512]{1,0:T(4,128)} %param.7), channel_id=1, source_target_pairs={{2,0},{3,1},{4,2},{5,3},{6,4},{7,5},{8,6},{9,7},{10,8},{11,9},{12,... | collective-permute-start | bytes 18440 | tf_op jit(solution)/shard_map/ppermute | solution.py:21
  19.4 15.8 %collective-permute-start.7 = (f32[512,256]{1,0:T(8,128)}, f32[512,256]{1,0:T(8,128)S(1)}, u32[]{:S(2)}, u32[]{:S(2)}) collective-permute-start(f32[512,256]{1,0:T(8,128)} %param.8), channel_id=1, source_target_pairs={{2,0},{3,1},{4,2},{5,3},{6,4},{7,5},{8,6},{9,7},{10,8},{11,9},{12,... | collective-permute-start | bytes 1572872 | tf_op jit(solution)/shard_map/ppermute | solution.py:21
  20.8 10.4 %collective-permute-start = (f32[3,512]{1,0:T(4,128)}, f32[3,512]{1,0:T(4,128)S(1)}, u32[]{:S(2)}, u32[]{:S(2)}) collective-permute-start(f32[3,512]{1,0:T(4,128)} %param.7), channel_id=1, source_target_pairs={{0,2},{1,3},{2,4},{3,5},{4,6},{5,7},{6,8},{7,9},{8,10},{9,11},{10,... | collective-permute-start | bytes 18440 | tf_op jit(solution)/shard_map/ppermute | solution.py:21
  26.3 25.4 %collective-permute-start.1 = (f32[512,256]{1,0:T(8,128)}, f32[512,256]{1,0:T(8,128)S(1)}, u32[]{:S(2)}, u32[]{:S(2)}) collective-permute-start(f32[512,256]{1,0:T(8,128)} %param.8), channel_id=1, source_target_pairs={{0,2},{1,3},{2,4},{3,5},{4,6},{5,7},{6,8},{7,9},{8,10},{9,11},{10,... | collective-permute-start | bytes 1572872 | tf_op jit(solution)/shard_map/ppermute | solution.py:21
  31.2 26.9 %slice-start = ((s8[8388608]{0:T(1024)(128)(4,1)}), s8[4194304]{0:T(1024)(128)(4,1)S(1)}, s32[]{:S(2)}) async-start(s8[8388608]{0:T(1024)(128)(4,1)} %bitcast.88), calls=%async_computation | async-start | bytes 8388608
  35.3 19.8 %copy-start.1 = (f32[4,512,512]{2,1,0:T(8,128)S(1)}, f32[4,512,512]{2,1,0:T(8,128)}, u32[]{:S(2)}) copy-start(f32[4,512,512]{2,1,0:T(8,128)} %param.11) | copy-start | bytes 12582916
  35.3 22.8 %slice-start.1 = ((s8[8388608]{0:T(1024)(128)(4,1)}), s8[4194304]{0:T(1024)(128)(4,1)S(1)}, s32[]{:S(2)}) async-start(s8[8388608]{0:T(1024)(128)(4,1)} %bitcast.88), calls=%async_computation.1 | async-start | bytes 8388608
  53.1 6.9 %copy-start.2 = (f32[4,512,512]{2,1,0:T(8,128)S(1)}, f32[4,512,512]{2,1,0:T(8,128)}, u32[]{:S(2)}) copy-start(f32[4,512,512]{2,1,0:T(8,128)} %param.13) | copy-start | bytes 12582916
  56.1 2.0 %collective-permute-start.8 = (f32[512,256]{0,1:T(8,128)S(1)}, f32[512,256]{0,1:T(8,128)S(1)}, u32[]{:S(2)}, u32[]{:S(2)}) collective-permute-start(f32[512,256]{0,1:T(8,128)S(1)} %convolution_bitcast_fusion.3), channel_id=1, source_target_pairs={{0,1},{1,0},{2,3},{3,2},{4,5},{5,4},{6,7},{7,6},{8,9},{9,8},{10,11... | collective-permute-start | bytes 1572872 | tf_op jit(solution)/shard_map/ppermute | solution.py:15
  62.3 2.0 %collective-permute-start.9 = (f32[512,256]{0,1:T(8,128)S(1)}, f32[512,256]{0,1:T(8,128)S(1)}, u32[]{:S(2)}, u32[]{:S(2)}) collective-permute-start(f32[512,256]{0,1:T(8,128)S(1)} %convolution_bitcast_fusion.2), channel_id=1, source_target_pairs={{0,1},{1,0},{2,3},{3,2},{4,5},{5,4},{6,7},{7,6},{8,9},{9,8},{10,11... | collective-permute-start | bytes 1572872 | tf_op jit(solution)/shard_map/ppermute | solution.py:15
  64.4 14.7 %collective-permute-start.10 = (f32[512,256]{0,1:T(8,128)S(1)}, f32[512,256]{0,1:T(8,128)S(1)}, u32[]{:S(2)}, u32[]{:S(2)}) collective-permute-start(f32[512,256]{0,1:T(8,128)S(1)} %add.74), channel_id=1, source_target_pairs={{0,2},{1,3},{2,0},{3,1},{4,6},{5,7},{6,4},{7,5},{8,10},{9,11},{10,... | collective-permute-start | bytes 1572872 | tf_op jit(solution)/shard_map/ppermute | solution.py:15
  83.2 2.0 %collective-permute-start.11 = (f32[512,256]{0,1:T(8,128)S(1)}, f32[512,256]{0,1:T(8,128)S(1)}, u32[]{:S(2)}, u32[]{:S(2)}) collective-permute-start(f32[512,256]{0,1:T(8,128)S(1)} %convolution_bitcast_fusion.1), channel_id=1, source_target_pairs={{0,1},{1,0},{2,3},{3,2},{4,5},{5,4},{6,7},{7,6},{8,9},{9,8},{10,11... | collective-permute-start | bytes 1572872 | tf_op jit(solution)/shard_map/ppermute | solution.py:15
  85.2 14.0 %collective-permute-start.12 = (f32[512,256]{0,1:T(8,128)S(1)}, f32[512,256]{0,1:T(8,128)S(1)}, u32[]{:S(2)}, u32[]{:S(2)}) collective-permute-start(f32[512,256]{0,1:T(8,128)S(1)} %add.75), channel_id=1, source_target_pairs={{0,2},{1,3},{2,0},{3,1},{4,6},{5,7},{6,4},{7,5},{8,10},{9,11},{10,... | collective-permute-start | bytes 1572872 | tf_op jit(solution)/shard_map/ppermute | solution.py:15
  99.3 13.2 %collective-permute-start.13 = (f32[512,256]{0,1:T(8,128)S(1)}, f32[512,256]{0,1:T(8,128)S(1)}, u32[]{:S(2)}, u32[]{:S(2)}) collective-permute-start(f32[512,256]{0,1:T(8,128)S(1)} %add.76), channel_id=1, source_target_pairs={{0,4},{1,5},{2,6},{3,7},{4,0},{5,1},{6,2},{7,3},{8,12},{9,13},{10,... | collective-permute-start | bytes 1572872 | tf_op jit(solution)/shard_map/ppermute | solution.py:15
  116.6 2.0 %collective-permute-start.14 = (f32[512,256]{0,1:T(8,128)S(1)}, f32[512,256]{0,1:T(8,128)S(1)}, u32[]{:S(2)}, u32[]{:S(2)}) collective-permute-start(f32[512,256]{0,1:T(8,128)S(1)} %convolution_bitcast_fusion), channel_id=1, source_target_pairs={{0,1},{1,0},{2,3},{3,2},{4,5},{5,4},{6,7},{7,6},{8,9},{9,8},{10,11... | collective-permute-start | bytes 1572872 | tf_op jit(solution)/shard_map/ppermute | solution.py:15
  118.7 14.0 %collective-permute-start.15 = (f32[512,256]{0,1:T(8,128)S(1)}, f32[512,256]{0,1:T(8,128)S(1)}, u32[]{:S(2)}, u32[]{:S(2)}) collective-permute-start(f32[512,256]{0,1:T(8,128)S(1)} %add.77), channel_id=1, source_target_pairs={{0,2},{1,3},{2,0},{3,1},{4,6},{5,7},{6,4},{7,5},{8,10},{9,11},{10,... | collective-permute-start | bytes 1572872 | tf_op jit(solution)/shard_map/ppermute | solution.py:15
  132.8 13.2 %collective-permute-start.16 = (f32[512,256]{0,1:T(8,128)S(1)}, f32[512,256]{0,1:T(8,128)S(1)}, u32[]{:S(2)}, u32[]{:S(2)}) collective-permute-start(f32[512,256]{0,1:T(8,128)S(1)} %add.78), channel_id=1, source_target_pairs={{0,4},{1,5},{2,6},{3,7},{4,0},{5,1},{6,2},{7,3},{8,12},{9,13},{10,... | collective-permute-start | bytes 1572872 | tf_op jit(solution)/shard_map/ppermute | solution.py:15
  146.1 12.3 %collective-permute-start.17 = (f32[512,256]{0,1:T(8,128)S(1)}, f32[512,256]{0,1:T(8,128)S(1)}, u32[]{:S(2)}, u32[]{:S(2)}) collective-permute-start(f32[512,256]{0,1:T(8,128)S(1)} %add.79), channel_id=1, source_target_pairs={{0,8},{1,9},{2,10},{3,11},{4,12},{5,13},{6,14},{7,15},{8,0},{9,1},... | collective-permute-start | bytes 1572872 | tf_op jit(solution)/shard_map/ppermute | solution.py:15
where the time goes:
time: 163 us; the launch traced here: 162 us
  waiting for transfers between devices  97 us (60%)
  starting transfers between devices  32.5 us (20%)
  matrix products  26.2 us (16%)
  local copies, waits for them, and re-layouts  3.34 us (2%)
  between operations  2.93 us (2%)
    ppermute x10, waiting for transfers between devices, from_partner(): lax.ppermute(x, axis, [(i, i ^ 1 << bit) for i in range(lax.axis_size(axi...  80.6 us
    ppermute x8, starting transfers between devices, passed_along(): lax.ppermute(value, axis, [(source, source + steps) for source in range(f...  23.8 us
    ppermute x8, waiting for transfers between devices, passed_along(): lax.ppermute(value, axis, [(source, source + steps) for source in range(f...  16.3 us
    ppermute x10, starting transfers between devices, from_partner(): lax.ppermute(x, axis, [(i, i ^ 1 << bit) for i in range(lax.axis_size(axi...  8.68 us
    dot_general x5, matrix products, kernel_tile(): jnp.dot(gauss(own_points, other_points), values, precision=lax.Precision....  7.89 us
    dot_general x4, matrix products, level_step(): jnp.dot(coupling[level], stacked, precision=lax.Precision.HIGHEST, prefer...  7.73 us
    dot_general x4, matrix products, level_step(): lax.dot_general(up_basis[level], iterate, (((0,), (0,)), ((), ())), preci...  4.41 us
    dot_general x4, matrix products, level_step(): jnp.dot(down_basis[level], correction, precision=lax.Precision.HIGHEST, p...  4.24 us
  transfers between devices with their start and end apart: 18, of which 12 were waited for; matrix products, arithmetic and copies ran while one was open for 5% of the time, Pallas kernels for 0%

commit v1 on v0

v1 whole, which is shorter than its diff:
```python
import math

import jax
import jax.numpy as jnp
from jax import lax
from jax.sharding import PartitionSpec as P

LEVELS = 4
CHUNKS = 2


def exchange(x, bit):
    count = lax.axis_size("leaf")
    return lax.ppermute(x, "leaf", [(i, i ^ bit) for i in range(count)])


def relay(x):
    count = lax.axis_size("leaf")
    return lax.ppermute(
        x, "leaf", [(i, (i + (-4 if i & 2 else 4)) % count) for i in range(count)]
    )


def product(left, right, contract=1):
    return lax.dot_general(
        left,
        right,
        (((contract,), (0,)), ((), ())),
        precision=lax.Precision.HIGH,
        preferred_element_type=jnp.float32,
    )


def tile(own, message, flag, rows):
    dist = jnp.zeros((own.shape[0], rows), jnp.float32)
    for coord in range(3):
        diff = own[:, coord][:, None] - message[rows + coord][None, :]
        dist = dist + diff * diff
    return flag * product(jnp.exp(-0.5 * dist), message[:rows])


def near_field(coords, weights, near_mask):
    me, count = lax.axis_index("leaf"), lax.axis_size("leaf")
    core, upper = me & 1, (me >> 1) & 1
    rows = weights.shape[0] // CHUNKS
    own = coords.T

    def flag(offset):
        slot = jnp.where(offset < 0, offset + 2, offset + 1)
        inside = (me + offset >= 0) & (me + offset < count)
        return jnp.where(inside, near_mask[0, slot], 0).astype(jnp.float32)

    one, two = 1 - 2 * core, 2 - 4 * upper
    messages = [
        jnp.concatenate(
            [
                weights[k * rows : (k + 1) * rows],
                coords[:, k * rows : (k + 1) * rows],
                jnp.zeros((5, rows), jnp.float32),
            ]
        )
        for k in range(CHUNKS)
    ]
    across = [exchange(m, 2) for m in messages]
    beside = [exchange(m, 1) for m in messages]
    passed = [relay(m) for m in across]
    crossed = [exchange(jnp.where(upper == core, a, p), 1) for a, p in zip(across, passed)]
    total = 0.0
    for m in messages:
        total = total + tile(own, m, 1.0, rows)
    for parts, offset in ((beside, one), (across, two), (passed, -two), (crossed, -one)):
        for m in parts:
            total = total + tile(own, m, flag(offset), rows)
    return total * 0.5


def level_step(iterate, level, up_basis, coupling, down_basis):
    core = lax.axis_index("leaf") & 1
    skeleton = product(up_basis[level], iterate, 0)
    half = skeleton.shape[0] // 2
    low, high = skeleton[:half], skeleton[half:]
    if level == 0:
        block, partner = skeleton, exchange(skeleton, 1)
    else:
        mine = jnp.where(core == 0, low, high) + exchange(jnp.where(core == 0, high, low), 1)
        for lower in range(1, level):
            mine = mine + exchange(mine, 1 << lower)
        theirs = exchange(mine, 1 << level)

        def whole(part):
            other = exchange(part, 1)
            return jnp.where(
                core == 0, jnp.concatenate([part, other]), jnp.concatenate([other, part])
            )

        block, partner = whole(mine), whole(theirs)
    rank = skeleton.shape[0]
    factor = coupling[level]
    correction = (product(factor[:, :rank], block) + product(factor[:, rank:], partner)) * (
        1.0 / math.sqrt(2.0 ** (level + 1))
    )
    return iterate - product(down_basis[level], correction)


def per_device(coords, weights, near_mask, leaf_inverse, up_basis, coupling, down_basis):
    near = near_field(coords, weights, near_mask)
    iterate = product(leaf_inverse, near)
    for level in range(LEVELS):
        iterate = level_step(iterate, level, up_basis, coupling, down_basis)
    return iterate


def solution(mesh):
    in_specs = (
        P(None, "leaf"),
        P("leaf", None),
        P("leaf", None),
        P("leaf", None),
        P(None, "leaf", None),
        P(None, "leaf", None),
        P(None, "leaf", None),
    )
    return jax.shard_map(
        per_device, mesh=mesh, in_specs=in_specs, out_specs=P("leaf", None), check_vma=False
    )
```

time: 163 us -> 106 us (0.65)
  waiting for transfers between devices: 97 us -> 62.2 us
  starting transfers between devices: 32.5 us -> 12.5 us
  matrix products: 26.2 us -> 21.9 us
  local copies, waits for them, and re-layouts: 3.34 us -> 5.37 us
    ppermute x18 -> x24, waiting for transfers between devices: 97 us -> 62.2 us  [the longest x22 56 us: exchange(): return lax.ppermute(x, 'leaf', [(i, i ^ bit) for i in range(count)])]
    ppermute x18 -> x24, starting transfers between devices: 32.5 us -> 12.5 us  [the longest x22 8.62 us: exchange(): return lax.ppermute(x, 'leaf', [(i, i ^ bit) for i in range(count)])]
    dot_general x18 -> x27, matrix products: 26.2 us -> 21.9 us  [product(): lax.dot_general(left, right, (((contract,), (0,)), ((), ())), precision=l...]
    squeeze x0 -> x1, local copies, waits for them, and re-layouts: none -> 1.65 us  [level_step(): factor = coupling[level]]
  transfers between devices with their start and end apart: 18 -> 24, of which waited for: 12 -> 17; matrix products, arithmetic and copies ran while one was open for 5% -> 10% of each run, Pallas kernels for 0% -> 0%
where the time goes in v1:
time: 106 us; the launch traced here: 105 us
  waiting for transfers between devices  62.2 us (59%)
  matrix products  21.9 us (21%)
  starting transfers between devices  12.5 us (12%)
  local copies, waits for them, and re-layouts  5.37 us (5%)
  between operations  3.02 us (3%)
    ppermute x22, waiting for transfers between devices, exchange(): return lax.ppermute(x, 'leaf', [(i, i ^ bit) for i in range(count)])  56 us
    dot_general x27, matrix products, product(): lax.dot_general(left, right, (((contract,), (0,)), ((), ())), precision=l...  21.9 us
    ppermute x22, starting transfers between devices, exchange(): return lax.ppermute(x, 'leaf', [(i, i ^ bit) for i in range(count)])  8.62 us
    ppermute x2, waiting for transfers between devices, relay(): lax.ppermute(x, 'leaf', [(i, (i + (-4 if i & 2 else 4)) % count) for i in...  6.14 us
    ppermute x2, starting transfers between devices, relay(): lax.ppermute(x, 'leaf', [(i, (i + (-4 if i & 2 else 4)) % count) for i in...  3.85 us
  transfers between devices with their start and end apart: 24, of which 17 were waited for; matrix products, arithmetic and copies ran while one was open for 10% of the time, Pallas kernels for 0%

profile of v1, /device:TPU:0, one launch (start us, length us, event | category | flops | bytes accessed | tf_op | source)
XLA Modules:
  0.0 105.5 jit_solution(4960236795763118571)
XLA Ops:
  0.0 0.8 fusion.286
  0.8 1.1 %fusion.276 = (f32[256,256]{1,0:T(8,128)S(1)}, f32[256,256]{1,0:T(8,128)S(1)}) fusion(f32[512,256]{1,0:T(8,128)} %param.8), kind=kLoop, calls=%fused_computation.320 | loop fusion | bytes 1048576 | tf_op jit(solution)/shard_map/slice | solution.py:57
  2.1 3.0 %collective-permute-start.2 = (f32[264,256]{1,0:T(8,128)S(1)}, f32[264,256]{1,0:T(8,128)S(1)}, u32[]{:S(2)}, u32[]{:S(2)}) collective-permute-start(f32[264,256]{1,0:T(8,128)S(1)} %get-tuple-element.46), channel_id=1, source_target_pairs={{0,2},{1,3},{2,0},{3,1},{4,6},{5,7},{6,4},{7,5},{8,10},{9,11},{10,... | collective-permute-start | bytes 811016 | tf_op jit(solution)/shard_map/ppermute | solution.py:14
  6.9 0.7 constant_dynamic-slice_fusion.3
  10.0 2.4 %collective-permute-done.2 = f32[264,256]{1,0:T(8,128)S(1)} collective-permute-done((f32[264,256]{1,0:T(8,128)S(1)}, f32[264,256]{1,0:T(8,128)S(1)}, u32[]{:S(2)}, u32[]{:S(2)}) %collective-permute-start.2) | collective-permute-done | bytes 270368 | tf_op jit(solution)/shard_map/ppermute | solution.py:14
  12.4 2.1 %collective-permute-start.4 = (f32[264,256]{1,0:T(8,128)S(1)}, f32[264,256]{1,0:T(8,128)S(1)}, u32[]{:S(2)}, u32[]{:S(2)}) collective-permute-start(f32[264,256]{1,0:T(8,128)S(1)} %collective-permute-done.2), channel_id=1, source_target_pairs={{0,4},{1,5},{2,30},{3,31},{4,8},{5,9},{6,2},{7,3},{8,12},{9,13},{1... | collective-permute-start | bytes 811016 | tf_op jit(solution)/shard_map/ppermute | solution.py:19
  14.5 2.9 %collective-permute-done.3 = f32[264,256]{1,0:T(8,128)S(1)} collective-permute-done((f32[264,256]{1,0:T(8,128)S(1)}, f32[264,256]{1,0:T(8,128)S(1)}, u32[]{:S(2)}, u32[]{:S(2)}) %collective-permute-start.3) | collective-permute-done | bytes 270368 | tf_op jit(solution)/shard_map/ppermute | solution.py:14
  17.4 1.8 %collective-permute-start.5 = (f32[264,256]{1,0:T(8,128)S(1)}, f32[264,256]{1,0:T(8,128)S(1)}, u32[]{:S(2)}, u32[]{:S(2)}) collective-permute-start(f32[264,256]{1,0:T(8,128)S(1)} %collective-permute-done.3), channel_id=1, source_target_pairs={{0,4},{1,5},{2,30},{3,31},{4,8},{5,9},{6,2},{7,3},{8,12},{9,13},{1... | collective-permute-start | bytes 811016 | tf_op jit(solution)/shard_map/ppermute | solution.py:19
  19.8 0.6 convolution_multiply_fusion.4
  20.3 0.6 fusion.13
  20.9 0.6 fusion.12
  22.1 5.7 %collective-permute-done.5 = f32[264,256]{1,0:T(8,128)S(1)} collective-permute-done((f32[264,256]{1,0:T(8,128)S(1)}, f32[264,256]{1,0:T(8,128)S(1)}, u32[]{:S(2)}, u32[]{:S(2)}) %collective-permute-start.5) | collective-permute-done | bytes 270368 | tf_op jit(solution)/shard_map/ppermute | solution.py:19
  28.5 0.9 collective-permute-done.7
  30.6 0.6 fusion.9
  31.3 1.1 %fusion.288 = f32[256,512]{1,0:T(8,128)S(1)} fusion(f32[512,256]{1,0:T(8,128)S(1)} %fusion.9, f32[512,512]{1,0:T(8,128)S(1)} %copy-done), kind=kOutput, calls=%fused_computation.332 | convolution fusion | flops 402653184 | bytes 2097152 | tf_op jit(solution)/shard_map/dot_general | solution.py:25
  32.4 2.7 %fusion.33 = f32[256,512]{1,0:T(8,128)} fusion(f32[256,512]{1,0:T(8,128)S(1)} %fusion.288, f32[4,512,512]{2,1,0:T(8,128)} %param.11), kind=kOutput, calls=%fused_computation.57 | convolution fusion | flops 402653184 | bytes 2097152 | tf_op jit(solution)/shard_map/dot_general | solution.py:25
  35.2 1.7 %slice_bitcast_fusion = (f32[512,1024]{1,0:T(8,128)S(1)}, f32[512,1024]{1,0:T(8,128)S(1)}, f32[512,1024]{1,0:T(8,128)S(1)}, f32[512,1024]{1,0:T(8,128)S(1)}) fusion(f32[4,512,1024]{2,1,0:T(8,128)S(1)} %bitcast.92), kind=kLoop, calls=%fused_computation | loop fusion | bytes 16777216 | tf_op jit(solution)/shard_map/squeeze | solution.py:98
  36.8 1.7 %fusion.24 = f32[256,512]{1,0:T(8,128)S(1)} fusion(f32[256,512]{1,0:T(8,128)} %fusion.33, f32[512,1024]{1,0:T(8,128)S(1)} %get-tuple-element.7), kind=kOutput, calls=%fused_computation.48 | convolution fusion | flops 402653184 | bytes 2097152 | tf_op jit(solution)/shard_map/dot_general | solution.py:25
  38.6 1.8 %fusion.1 = f32[256,512]{1,0:T(8,128)S(1)} fusion(f32[256,512]{1,0:T(8,128)S(1)} %fusion.24, f32[512,256]{0,1:T(8,128)} %collective-permute-done.8, f32[512,1024]{1,0:T(8,128)S(1)} %get-tuple-element.7), kind=kOutput, calls=%fused_computation.13 | convolution fusion | flops 402915328 | bytes 2621440 | tf_op jit(solution)/shard_map/dot_general | solution.py:25
  40.4 0.7 convolution_subtract_fusion.3
  41.1 0.6 convolution_bitcast_fusion.2
  42.2 1.2 %collective-permute-done.9 = f32[256,256]{0,1:T(8,128)S(1)} collective-permute-done((f32[256,256]{0,1:T(8,128)S(1)}, f32[256,256]{0,1:T(8,128)S(1)}, u32[]{:S(2)}, u32[]{:S(2)}) %collective-permute-start.9) | collective-permute-done | bytes 262176 | tf_op jit(solution)/shard_map/ppermute | solution.py:14
  43.5 1.1 %collective-permute-start.11 = (f32[256,256]{0,1:T(8,128)S(1)}, f32[256,256]{0,1:T(8,128)S(1)}, u32[]{:S(2)}, u32[]{:S(2)}) collective-permute-start(f32[256,256]{0,1:T(8,128)S(1)} %select_add_fusion.2), channel_id=1, source_target_pairs={{0,2},{1,3},{2,0},{3,1},{4,6},{5,7},{6,4},{7,5},{8,10},{9,11},{10,... | collective-permute-start | bytes 786440 | tf_op jit(solution)/shard_map/ppermute | solution.py:14
  44.6 7.5 %collective-permute-done.11 = f32[256,256]{0,1:T(8,128)S(1)} collective-permute-done((f32[256,256]{0,1:T(8,128)S(1)}, f32[256,256]{0,1:T(8,128)S(1)}, u32[]{:S(2)}, u32[]{:S(2)}) %collective-permute-start.11) | collective-permute-done | bytes 262176 | tf_op jit(solution)/shard_map/ppermute | solution.py:14
  52.1 0.7 fusion.21
  52.8 0.9 collective-permute-done.12
  53.6 0.7 fusion.2
  54.3 0.7 convolution_subtract_fusion.2
  55.0 0.9 convolution_bitcast_fusion.1
  56.1 1.4 %collective-permute-done.13 = f32[256,256]{0,1:T(8,128)S(1)} collective-permute-done((f32[256,256]{0,1:T(8,128)S(1)}, f32[256,256]{0,1:T(8,128)S(1)}, u32[]{:S(2)}, u32[]{:S(2)}) %collective-permute-start.13) | collective-permute-done | bytes 262176 | tf_op jit(solution)/shard_map/ppermute | solution.py:14
  57.5 1.1 %collective-permute-start.14 = (f32[256,256]{0,1:T(8,128)S(1)}, f32[256,256]{0,1:T(8,128)S(1)}, u32[]{:S(2)}, u32[]{:S(2)}) collective-permute-start(f32[256,256]{0,1:T(8,128)S(1)} %select_add_fusion.1), channel_id=1, source_target_pairs={{0,2},{1,3},{2,0},{3,1},{4,6},{5,7},{6,4},{7,5},{8,10},{9,11},{10,... | collective-permute-start | bytes 786440 | tf_op jit(solution)/shard_map/ppermute | solution.py:14
  58.6 7.3 %collective-permute-done.14 = f32[256,256]{0,1:T(8,128)S(1)} collective-permute-done((f32[256,256]{0,1:T(8,128)S(1)}, f32[256,256]{0,1:T(8,128)S(1)}, u32[]{:S(2)}, u32[]{:S(2)}) %collective-permute-start.14) | collective-permute-done | bytes 262176 | tf_op jit(solution)/shard_map/ppermute | solution.py:14
  66.1 7.4 %collective-permute-done.16 = f32[256,256]{0,1:T(8,128)S(1)} collective-permute-done((f32[256,256]{0,1:T(8,128)S(1)}, f32[256,256]{0,1:T(8,128)S(1)}, u32[]{:S(2)}, u32[]{:S(2)}) %collective-permute-start.16) | collective-permute-done | bytes 262176 | tf_op jit(solution)/shard_map/ppermute | solution.py:14
  73.6 0.7 fusion.18
  74.2 0.9 collective-permute-done.17
  75.1 0.7 fusion.3
  75.8 0.7 convolution_subtract_fusion.1
  76.4 0.7 convolution_bitcast_fusion
  77.3 1.4 %collective-permute-done.18 = f32[256,256]{0,1:T(8,128)S(1)} collective-permute-done((f32[256,256]{0,1:T(8,128)S(1)}, f32[256,256]{0,1:T(8,128)S(1)}, u32[]{:S(2)}, u32[]{:S(2)}) %collective-permute-start.18) | collective-permute-done | bytes 262176 | tf_op jit(solution)/shard_map/ppermute | solution.py:14
  78.8 1.1 %collective-permute-start.19 = (f32[256,256]{0,1:T(8,128)S(1)}, f32[256,256]{0,1:T(8,128)S(1)}, u32[]{:S(2)}, u32[]{:S(2)}) collective-permute-start(f32[256,256]{0,1:T(8,128)S(1)} %select_add_fusion), channel_id=1, source_target_pairs={{0,2},{1,3},{2,0},{3,1},{4,6},{5,7},{6,4},{7,5},{8,10},{9,11},{10,... | collective-permute-start | bytes 786440 | tf_op jit(solution)/shard_map/ppermute | solution.py:14
  79.9 7.3 %collective-permute-done.19 = f32[256,256]{0,1:T(8,128)S(1)} collective-permute-done((f32[256,256]{0,1:T(8,128)S(1)}, f32[256,256]{0,1:T(8,128)S(1)}, u32[]{:S(2)}, u32[]{:S(2)}) %collective-permute-start.19) | collective-permute-done | bytes 262176 | tf_op jit(solution)/shard_map/ppermute | solution.py:14
  87.6 7.2 %collective-permute-done.20 = f32[256,256]{0,1:T(8,128)S(1)} collective-permute-done((f32[256,256]{0,1:T(8,128)S(1)}, f32[256,256]{0,1:T(8,128)S(1)}, u32[]{:S(2)}, u32[]{:S(2)}) %collective-permute-start.20) | collective-permute-done | bytes 262176 | tf_op jit(solution)/shard_map/ppermute | solution.py:14
  95.0 6.5 %collective-permute-done.22 = f32[256,256]{0,1:T(8,128)S(1)} collective-permute-done((f32[256,256]{0,1:T(8,128)S(1)}, f32[256,256]{0,1:T(8,128)S(1)}, u32[]{:S(2)}, u32[]{:S(2)}) %collective-permute-start.22) | collective-permute-done | bytes 262176 | tf_op jit(solution)/shard_map/ppermute | solution.py:14
  101.5 0.7 fusion.15
  102.2 0.9 collective-permute-done.23
  103.1 0.7 fusion.4
  103.8 0.7 fusion
  104.5 1.0 copy.8
  (73 shorter events, 7.0 us)
Async XLA Ops:
  0.0 31.3 %copy-start = (f32[512,512]{1,0:T(8,128)S(1)}, f32[512,512]{1,0:T(8,128)}, u32[]{:S(2)}) copy-start(f32[512,512]{1,0:T(8,128)} %param.10) | copy-start | bytes 3145732
  0.0 5.6 %copy-start.4 = (f32[3,512]{1,0:T(4,128)S(1)}, f32[3,512]{1,0:T(4,128)}, u32[]{:S(2)}) copy-start(f32[3,512]{1,0:T(4,128)} %param.7) | copy-start | bytes 18436
  0.0 5.6 %copy-start.3 = (f32[512,256]{1,0:T(8,128)S(1)}, f32[512,256]{1,0:T(8,128)}, u32[]{:S(2)}) copy-start(f32[512,256]{1,0:T(8,128)} %param.8) | copy-start | bytes 1572868
  2.0 4.9 %copy-start.5 = (s32[1,4]{1,0:T(1,128)S(1)}, s32[1,4]{1,0:T(1,128)}, u32[]{:S(2)}) copy-start(s32[1,4]{1,0:T(1,128)} %param.9) | copy-start | bytes 52
  2.1 10.3 %collective-permute-start.2 = (f32[264,256]{1,0:T(8,128)S(1)}, f32[264,256]{1,0:T(8,128)S(1)}, u32[]{:S(2)}, u32[]{:S(2)}) collective-permute-start(f32[264,256]{1,0:T(8,128)S(1)} %get-tuple-element.46), channel_id=1, source_target_pairs={{0,2},{1,3},{2,0},{3,1},{4,6},{5,7},{6,4},{7,5},{8,10},{9,11},{10,... | collective-permute-start | bytes 811016 | tf_op jit(solution)/shard_map/ppermute | solution.py:14
  5.1 14.1 %collective-permute-start = (f32[264,256]{1,0:T(8,128)S(1)}, f32[264,256]{1,0:T(8,128)S(1)}, u32[]{:S(2)}, u32[]{:S(2)}) collective-permute-start(f32[264,256]{1,0:T(8,128)S(1)} %get-tuple-element.46), channel_id=1, source_target_pairs={{0,1},{1,0},{2,3},{3,2},{4,5},{5,4},{6,7},{7,6},{8,9},{9,8},{10,11... | collective-permute-start | bytes 811016 | tf_op jit(solution)/shard_map/ppermute | solution.py:14
  5.1 12.3 %collective-permute-start.3 = (f32[264,256]{1,0:T(8,128)S(1)}, f32[264,256]{1,0:T(8,128)S(1)}, u32[]{:S(2)}, u32[]{:S(2)}) collective-permute-start(f32[264,256]{1,0:T(8,128)S(1)} %get-tuple-element.47), channel_id=1, source_target_pairs={{0,2},{1,3},{2,0},{3,1},{4,6},{5,7},{6,4},{7,5},{8,10},{9,11},{10,... | collective-permute-start | bytes 811016 | tf_op jit(solution)/shard_map/ppermute | solution.py:14
  5.3 13.9 %collective-permute-start.1 = (f32[264,256]{1,0:T(8,128)S(1)}, f32[264,256]{1,0:T(8,128)S(1)}, u32[]{:S(2)}, u32[]{:S(2)}) collective-permute-start(f32[264,256]{1,0:T(8,128)S(1)} %get-tuple-element.47), channel_id=1, source_target_pairs={{0,1},{1,0},{2,3},{3,2},{4,5},{5,4},{6,7},{7,6},{8,9},{9,8},{10,11... | collective-permute-start | bytes 811016 | tf_op jit(solution)/shard_map/ppermute | solution.py:14
  12.4 9.6 %collective-permute-start.4 = (f32[264,256]{1,0:T(8,128)S(1)}, f32[264,256]{1,0:T(8,128)S(1)}, u32[]{:S(2)}, u32[]{:S(2)}) collective-permute-start(f32[264,256]{1,0:T(8,128)S(1)} %collective-permute-done.2), channel_id=1, source_target_pairs={{0,4},{1,5},{2,30},{3,31},{4,8},{5,9},{6,2},{7,3},{8,12},{9,13},{1... | collective-permute-start | bytes 811016 | tf_op jit(solution)/shard_map/ppermute | solution.py:19
  17.4 10.4 %collective-permute-start.5 = (f32[264,256]{1,0:T(8,128)S(1)}, f32[264,256]{1,0:T(8,128)S(1)}, u32[]{:S(2)}, u32[]{:S(2)}) collective-permute-start(f32[264,256]{1,0:T(8,128)S(1)} %collective-permute-done.3), channel_id=1, source_target_pairs={{0,4},{1,5},{2,30},{3,31},{4,8},{5,9},{6,2},{7,3},{8,12},{9,13},{1... | collective-permute-start | bytes 811016 | tf_op jit(solution)/shard_map/ppermute | solution.py:19
  20.9 14.2 %slice-start = ((s8[8388608]{0:T(1024)(128)(4,1)}), s8[4194304]{0:T(1024)(128)(4,1)S(1)}, s32[]{:S(2)}) async-start(s8[8388608]{0:T(1024)(128)(4,1)} %bitcast.91), calls=%async_computation | async-start | bytes 8388608
  22.0 6.5 %collective-permute-start.6 = (f32[264,256]{1,0:T(8,128)S(1)}, f32[264,256]{1,0:T(8,128)S(1)}, u32[]{:S(2)}, u32[]{:S(2)}) collective-permute-start(f32[264,256]{1,0:T(8,128)S(1)} %broadcast_select_fusion.1), channel_id=1, source_target_pairs={{0,1},{1,0},{2,3},{3,2},{4,5},{5,4},{6,7},{7,6},{8,9},{9,8},{10,11... | collective-permute-start | bytes 811016 | tf_op jit(solution)/shard_map/ppermute | solution.py:14
  27.8 1.6 %collective-permute-start.7 = (f32[264,256]{1,0:T(8,128)S(1)}, f32[264,256]{1,0:T(8,128)S(1)}, u32[]{:S(2)}, u32[]{:S(2)}) collective-permute-start(f32[264,256]{1,0:T(8,128)S(1)} %broadcast_select_fusion), channel_id=1, source_target_pairs={{0,1},{1,0},{2,3},{3,2},{4,5},{5,4},{6,7},{7,6},{8,9},{9,8},{10,11... | collective-permute-start | bytes 811016 | tf_op jit(solution)/shard_map/ppermute | solution.py:14
  30.0 5.1 %slice-start.1 = ((s8[8388608]{0:T(1024)(128)(4,1)}), s8[4194304]{0:T(1024)(128)(4,1)S(1)}, s32[]{:S(2)}) async-start(s8[8388608]{0:T(1024)(128)(4,1)} %bitcast.91), calls=%async_computation.1 | async-start | bytes 8388608
  35.0 3.5 %collective-permute-start.8 = (f32[512,256]{0,1:T(8,128)}, f32[512,256]{0,1:T(8,128)}, u32[]{:S(2)}, u32[]{:S(2)}) collective-permute-start(f32[512,256]{0,1:T(8,128)} %bitcast.40), channel_id=1, source_target_pairs={{0,1},{1,0},{2,3},{3,2},{4,5},{5,4},{6,7},{7,6},{8,9},{9,8},{10,11... | collective-permute-start | bytes 1572872 | tf_op jit(solution)/shard_map/ppermute | solution.py:14
  35.2 5.2 %copy-start.2 = (f32[4,512,512]{2,1,0:T(8,128)S(1)}, f32[4,512,512]{2,1,0:T(8,128)}, u32[]{:S(2)}) copy-start(f32[4,512,512]{2,1,0:T(8,128)} %param.13) | copy-start | bytes 12582916
  38.5 2.5 %copy-start.1 = (f32[4,512,512]{2,1,0:T(8,128)S(1)}, f32[4,512,512]{2,1,0:T(8,128)}, u32[]{:S(2)}) copy-start(f32[4,512,512]{2,1,0:T(8,128)} %param.11) | copy-start | bytes 12582916
  41.8 1.6 %collective-permute-start.9 = (f32[256,256]{0,1:T(8,128)S(1)}, f32[256,256]{0,1:T(8,128)S(1)}, u32[]{:S(2)}, u32[]{:S(2)}) collective-permute-start(f32[256,256]{0,1:T(8,128)S(1)} %slice_select_fusion.2), channel_id=1, source_target_pairs={{0,1},{1,0},{2,3},{3,2},{4,5},{5,4},{6,7},{7,6},{8,9},{9,8},{10,11... | collective-permute-start | bytes 786440 | tf_op jit(solution)/shard_map/ppermute | solution.py:14
  43.5 8.7 %collective-permute-start.11 = (f32[256,256]{0,1:T(8,128)S(1)}, f32[256,256]{0,1:T(8,128)S(1)}, u32[]{:S(2)}, u32[]{:S(2)}) collective-permute-start(f32[256,256]{0,1:T(8,128)S(1)} %select_add_fusion.2), channel_id=1, source_target_pairs={{0,2},{1,3},{2,0},{3,1},{4,6},{5,7},{6,4},{7,5},{8,10},{9,11},{10,... | collective-permute-start | bytes 786440 | tf_op jit(solution)/shard_map/ppermute | solution.py:14
  44.5 7.6 %collective-permute-start.10 = (f32[256,256]{0,1:T(8,128)S(1)}, f32[256,256]{0,1:T(8,128)S(1)}, u32[]{:S(2)}, u32[]{:S(2)}) collective-permute-start(f32[256,256]{0,1:T(8,128)S(1)} %select_add_fusion.2), channel_id=1, source_target_pairs={{0,1},{1,0},{2,3},{3,2},{4,5},{5,4},{6,7},{7,6},{8,9},{9,8},{10,11... | collective-permute-start | bytes 786440 | tf_op jit(solution)/shard_map/ppermute | solution.py:14
  52.1 1.5 %collective-permute-start.12 = (f32[256,256]{0,1:T(8,128)S(1)}, f32[256,256]{0,1:T(8,128)S(1)}, u32[]{:S(2)}, u32[]{:S(2)}) collective-permute-start(f32[256,256]{0,1:T(8,128)S(1)} %collective-permute-done.11), channel_id=1, source_target_pairs={{0,1},{1,0},{2,3},{3,2},{4,5},{5,4},{6,7},{7,6},{8,9},{9,8},{10,11... | collective-permute-start | bytes 786440 | tf_op jit(solution)/shard_map/ppermute | solution.py:14
  55.9 1.6 %collective-permute-start.13 = (f32[256,256]{0,1:T(8,128)S(1)}, f32[256,256]{0,1:T(8,128)S(1)}, u32[]{:S(2)}, u32[]{:S(2)}) collective-permute-start(f32[256,256]{0,1:T(8,128)S(1)} %slice_select_fusion.1), channel_id=1, source_target_pairs={{0,1},{1,0},{2,3},{3,2},{4,5},{5,4},{6,7},{7,6},{8,9},{9,8},{10,11... | collective-permute-start | bytes 786440 | tf_op jit(solution)/shard_map/ppermute | solution.py:14
  57.5 8.4 %collective-permute-start.14 = (f32[256,256]{0,1:T(8,128)S(1)}, f32[256,256]{0,1:T(8,128)S(1)}, u32[]{:S(2)}, u32[]{:S(2)}) collective-permute-start(f32[256,256]{0,1:T(8,128)S(1)} %select_add_fusion.1), channel_id=1, source_target_pairs={{0,2},{1,3},{2,0},{3,1},{4,6},{5,7},{6,4},{7,5},{8,10},{9,11},{10,... | collective-permute-start | bytes 786440 | tf_op jit(solution)/shard_map/ppermute | solution.py:14
  66.0 7.6 %collective-permute-start.16 = (f32[256,256]{0,1:T(8,128)S(1)}, f32[256,256]{0,1:T(8,128)S(1)}, u32[]{:S(2)}, u32[]{:S(2)}) collective-permute-start(f32[256,256]{0,1:T(8,128)S(1)} %add.246), channel_id=1, source_target_pairs={{0,4},{1,5},{2,6},{3,7},{4,0},{5,1},{6,2},{7,3},{8,12},{9,13},{10,... | collective-permute-start | bytes 786440 | tf_op jit(solution)/shard_map/ppermute | solution.py:14
  66.1 7.5 %collective-permute-start.15 = (f32[256,256]{0,1:T(8,128)S(1)}, f32[256,256]{0,1:T(8,128)S(1)}, u32[]{:S(2)}, u32[]{:S(2)}) collective-permute-start(f32[256,256]{0,1:T(8,128)S(1)} %add.246), channel_id=1, source_target_pairs={{0,1},{1,0},{2,3},{3,2},{4,5},{5,4},{6,7},{7,6},{8,9},{9,8},{10,11... | collective-permute-start | bytes 786440 | tf_op jit(solution)/shard_map/ppermute | solution.py:14
  73.6 1.5 %collective-permute-start.17 = (f32[256,256]{0,1:T(8,128)S(1)}, f32[256,256]{0,1:T(8,128)S(1)}, u32[]{:S(2)}, u32[]{:S(2)}) collective-permute-start(f32[256,256]{0,1:T(8,128)S(1)} %collective-permute-done.16), channel_id=1, source_target_pairs={{0,1},{1,0},{2,3},{3,2},{4,5},{5,4},{6,7},{7,6},{8,9},{9,8},{10,11... | collective-permute-start | bytes 786440 | tf_op jit(solution)/shard_map/ppermute | solution.py:14
  77.1 1.6 %collective-permute-start.18 = (f32[256,256]{0,1:T(8,128)S(1)}, f32[256,256]{0,1:T(8,128)S(1)}, u32[]{:S(2)}, u32[]{:S(2)}) collective-permute-start(f32[256,256]{0,1:T(8,128)S(1)} %slice_select_fusion), channel_id=1, source_target_pairs={{0,1},{1,0},{2,3},{3,2},{4,5},{5,4},{6,7},{7,6},{8,9},{9,8},{10,11... | collective-permute-start | bytes 786440 | tf_op jit(solution)/shard_map/ppermute | solution.py:14
  78.8 8.4 %collective-permute-start.19 = (f32[256,256]{0,1:T(8,128)S(1)}, f32[256,256]{0,1:T(8,128)S(1)}, u32[]{:S(2)}, u32[]{:S(2)}) collective-permute-start(f32[256,256]{0,1:T(8,128)S(1)} %select_add_fusion), channel_id=1, source_target_pairs={{0,2},{1,3},{2,0},{3,1},{4,6},{5,7},{6,4},{7,5},{8,10},{9,11},{10,... | collective-permute-start | bytes 786440 | tf_op jit(solution)/shard_map/ppermute | solution.py:14
  87.2 7.6 %collective-permute-start.20 = (f32[256,256]{0,1:T(8,128)S(1)}, f32[256,256]{0,1:T(8,128)S(1)}, u32[]{:S(2)}, u32[]{:S(2)}) collective-permute-start(f32[256,256]{0,1:T(8,128)S(1)} %add.249), channel_id=1, source_target_pairs={{0,4},{1,5},{2,6},{3,7},{4,0},{5,1},{6,2},{7,3},{8,12},{9,13},{10,... | collective-permute-start | bytes 786440 | tf_op jit(solution)/shard_map/ppermute | solution.py:14
  94.9 6.7 %collective-permute-start.22 = (f32[256,256]{0,1:T(8,128)S(1)}, f32[256,256]{0,1:T(8,128)S(1)}, u32[]{:S(2)}, u32[]{:S(2)}) collective-permute-start(f32[256,256]{0,1:T(8,128)S(1)} %add.250), channel_id=1, source_target_pairs={{0,8},{1,9},{2,10},{3,11},{4,12},{5,13},{6,14},{7,15},{8,0},{9,1},... | collective-permute-start | bytes 786440 | tf_op jit(solution)/shard_map/ppermute | solution.py:14
  95.0 6.6 %collective-permute-start.21 = (f32[256,256]{0,1:T(8,128)S(1)}, f32[256,256]{0,1:T(8,128)S(1)}, u32[]{:S(2)}, u32[]{:S(2)}) collective-permute-start(f32[256,256]{0,1:T(8,128)S(1)} %add.250), channel_id=1, source_target_pairs={{0,1},{1,0},{2,3},{3,2},{4,5},{5,4},{6,7},{7,6},{8,9},{9,8},{10,11... | collective-permute-start | bytes 786440 | tf_op jit(solution)/shard_map/ppermute | solution.py:14
  101.5 1.5 %collective-permute-start.23 = (f32[256,256]{0,1:T(8,128)S(1)}, f32[256,256]{0,1:T(8,128)S(1)}, u32[]{:S(2)}, u32[]{:S(2)}) collective-permute-start(f32[256,256]{0,1:T(8,128)S(1)} %collective-permute-done.22), channel_id=1, source_target_pairs={{0,1},{1,0},{2,3},{3,2},{4,5},{5,4},{6,7},{7,6},{8,9},{9,8},{10,11... | collective-permute-start | bytes 786440 | tf_op jit(solution)/shard_map/ppermute | solution.py:14

commit v2 on v0

v2 whole, which is shorter than its diff:
```python
import functools
import math
from typing import Any, NamedTuple

import jax
import jax.numpy as jnp
from jax import lax
from jax.experimental import pallas as pl
from jax.experimental.pallas import tpu as pltpu
from jax.sharding import PartitionSpec as P

LEVELS = 4
CHUNKS = 2
PAD = 8
F32, BF16 = jnp.float32, jnp.bfloat16
VMEM, WINDOW_VMEM = 24 * 2**20, 48 * 2**20
ALL = slice(None)


def permute(x, target):
    count = lax.axis_size("leaf")
    return lax.ppermute(x, "leaf", [(i, target(i) % count) for i in range(count)])


def exchange(x, bit):
    return permute(x, lambda i: i ^ bit)


def after(x, *earlier):
    return lax.optimization_barrier((x, *earlier))[0]


def split(x):
    high = x.astype(BF16)
    return high, (x - high.astype(F32)).astype(BF16)


def product(left, right):
    def dot(a, b):
        return jnp.dot(a, b, preferred_element_type=F32)

    (left_high, left_low), (right_high, right_low) = left, right
    rows, columns = left_high.shape[0], right_high.shape[1]
    count = 2 if columns <= 256 else 1
    got = []
    for k in range(count):
        at = slice(k * rows // count, (k + 1) * rows // count)
        high, low = left_high[at], left_low[at]
        got.append(dot(high, right_high) + (dot(high, right_low) + dot(low, right_high)))
    return jnp.concatenate(got) if count > 1 else got[0]


def parts(refs, index=...):
    return tuple(ref[index] for ref in refs)


def put(refs, index, values):
    for ref, value in zip(refs, values):
        ref[index] = value


def two_parts(*shape):
    return [(shape, BF16)] * 2


class Window(NamedTuple):
    array: Any
    index: tuple
    shape: tuple


class Arriving:
    def __init__(self, copy, ref):
        self.copy, self.ref, self.here = copy, ref, False

    def __call__(self):
        if not self.here:
            self.copy.wait()
            self.here = True
        return self.ref[...]


def call(body, outs, *args):
    windows = [arg for arg in args if isinstance(arg, Window)]
    arrays = [arg.array if isinstance(arg, Window) else arg for arg in args]

    def kernel(*refs):
        ins, rest = list(refs[: len(args)]), refs[len(args) :]
        results, buffers, semaphores = rest[: len(outs)], rest[len(outs) : -1], rest[-1]
        arriving = []
        for k, arg in enumerate(args):
            if isinstance(arg, Window):
                at = len(arriving)
                copy = pltpu.make_async_copy(ins[k].at[arg.index], buffers[at], semaphores.at[at])
                copy.start()
                ins[k] = Arriving(copy, buffers[at])
                arriving.append(ins[k])
        body(*ins, *results)
        for window in arriving:
            if not window.here:
                window.copy.wait()

    def spec(arg):
        if isinstance(arg, Window):
            return pl.BlockSpec(memory_space=pltpu.HBM)
        return pl.BlockSpec(memory_space=pltpu.SMEM if arg.dtype == jnp.int32 else pltpu.VMEM)

    return pl.pallas_call(
        kernel,
        in_specs=[spec(arg) for arg in args],
        out_specs=[pl.BlockSpec(memory_space=pltpu.VMEM) for _ in outs],
        out_shape=[jax.ShapeDtypeStruct(*out) for out in outs],
        scratch_shapes=[pltpu.VMEM(w.shape, w.array.dtype) for w in windows]
        + [pltpu.SemaphoreType.DMA((max(1, len(windows)),))],
        compiler_params=pltpu.CompilerParams(vmem_limit_bytes=(WINDOW_VMEM if windows else VMEM)),
        cost_estimate=pl.CostEstimate(flops=0, bytes_accessed=0, transcendentals=0),
    )(*arrays)


def pack_body(k, coords, weights, message, points=None):
    rows = message.shape[0] - PAD
    where = coords()
    message[rows : rows + PAD, :] = jnp.zeros((PAD, message.shape[1]), F32)
    message[rows : rows + 3, :] = where[:, k * rows : (k + 1) * rows]
    if points is not None:
        points[...] = jnp.zeros(points.shape, F32)
        points[0:3, :] = where
    message[0:rows, :] = weights()


def flag_of(mask, offset):
    me, count = lax.axis_index("leaf"), lax.axis_size("leaf")
    slot = jnp.where(offset < 0, offset + 2, offset + 1)
    at = me + offset
    return jnp.where((at >= 0) & (at < count), mask[0, slot], 0).astype(F32)


KINDS = ("beside", "across", "passed", "crossed")


def tile(points, message, flag=None):
    rows = message.shape[0] - PAD
    own = points[...].T
    dist = jnp.zeros((own.shape[0], rows), F32)
    for coord in range(3):
        diff = own[:, coord : coord + 1] - message[rows + coord : rows + coord + 1, :]
        dist = dist + diff * diff
    values = message[0:rows, :]
    if flag is not None:
        values = values * flag
    return product(split(jnp.exp(-0.5 * dist)), split(values))


def own_body(points, mask, *refs):
    messages, total, flags = refs[:-2], refs[-2], refs[-1]
    me = lax.axis_index("leaf")
    one, two = 1 - 2 * (me & 1), 2 - 4 * ((me >> 1) & 1)
    flags[...] = jnp.zeros(flags.shape, F32)
    for k, offset in enumerate((one, two, -two, -one)):
        flags[k : k + 1, :] = jnp.full((1, flags.shape[1]), flag_of(mask, offset))
    acc = tile(points, messages[0])
    for message in messages[1:]:
        acc = acc + tile(points, message)
    total[...] = acc


def add_body(kinds, total, points, flags, *rest):
    messages, out = rest[:-1], rest[-1]
    acc = total[...]
    for kind, message in zip(kinds, messages):
        k = KINDS.index(kind)
        acc = acc + tile(points, message, flags[k : k + 1, :])
    out[...] = acc


def start_body(total, points, flags, message, start_high, start_low, near_high, near_low, skeleton):
    k = KINDS.index("crossed")
    near = split(0.5 * (total[...] + tile(points, message, flags[k : k + 1, :])))
    skeleton[...] = product(parts((start_high, start_low)), near)
    put((near_high, near_low), ..., near)


def scale_of(level):
    return 1.0 / math.sqrt(2.0 ** (level + 1))


def halves_by_core(value, mine, other):
    core, half = lax.axis_index("leaf") & 1, mine.shape[0]
    low, high = value[0:half], value[half : 2 * half]
    mine[...] = jnp.where(core == 0, low, high)
    other[...] = jnp.where(core == 0, high, low)


def open_body(up, inverse, start_high, start_low, inverse_high, inverse_low):
    up_parts = split(up().T)
    inverse_parts = split(inverse())
    put((inverse_high, inverse_low), ..., inverse_parts)
    put((start_high, start_low), ..., split(product(up_parts, inverse_parts)))


def fold_body(level, ahead, split_rows, *refs):
    _, down, coupling = refs[0:3]
    refs = refs[3:]
    if ahead:
        up, refs = refs[0], refs[1:]
    down_parts = split(down())
    put(refs[0:2], ..., down_parts)
    step = split(product(down_parts, split(coupling())) * scale_of(level))
    half = step[0].shape[1] // 2
    columns = [(ALL, slice(k * half, (k + 1) * half)) for k in range(2)]
    for k in range(2):
        put(refs[2:4], k, (step[0][columns[k]], step[1][columns[k]]))
    if ahead:
        up_parts = split(up().T)
        put(refs[4:6], ..., up_parts)
        jump = product(up_parts, step)
        if split_rows:
            halves_by_core(jump, refs[6], refs[7])
        else:
            jump = split(jump)
            for k in range(2):
                put(refs[6:8], k, (jump[0][columns[k]], jump[1][columns[k]]))


def fold(level, up_basis, coupling, down_basis, earlier, split_rows):
    points, rank = up_basis.shape[1:]
    half = rank // 2
    ahead = level + 1 < LEVELS
    ups = [Window(up_basis, (level + 1,), (points, rank))] * ahead
    outs = two_parts(points, rank) + two_parts(2, points, half)
    if ahead:
        outs = outs + two_parts(rank, points)
        outs = outs + ([((half, rank), F32)] * 2 if split_rows else two_parts(2, rank, half))
    got = call(
        functools.partial(fold_body, level, ahead, split_rows),
        outs,
        earlier,
        Window(down_basis, (level,), (points, rank)),
        Window(coupling, (level, ALL, slice(rank, 2 * rank)), (rank, rank)),
        *ups,
    )
    return got[0:2], got[2:4], got[4:6], got[6:8]


def settle_first_body(near_high, near_low, skeleton, inverse_high, inverse_low, coupling, down_high, down_low, up_high, up_low, iterate, mine, other):
    weights = split(coupling())
    value = product(parts((inverse_high, inverse_low)), parts((near_high, near_low)))
    middle = product(weights, split(skeleton[...]))
    value = value - product(parts((down_high, down_low)), split(middle * scale_of(0)))
    iterate[...] = value
    halves_by_core(product(parts((up_high, up_low)), split(value)), mine, other)


def settle_body(level, count, ahead, split_rows, *refs):
    base_iterate, old_high, old_low = refs[0:3]
    theirs, refs = refs[3 : 3 + count], refs[3 + count :]
    mine, other, coupling, down_high, down_low = refs[0:5]
    core = lax.axis_index("leaf") & 1
    half = mine.shape[0]
    value = base_iterate[...]
    if count == 1:
        pieces = [(k, theirs[0][k * half : (k + 1) * half, :]) for k in range(2)]
    else:
        pieces = [(core, theirs[0][...]), (1 - core, theirs[1][...])]
    for k, piece in pieces:
        value = value - product(parts((old_high, old_low), k), split(piece))
    low = jnp.where(core == 0, mine[...], other[...])
    high = jnp.where(core == 0, other[...], mine[...])
    middle = product(split(coupling()), split(jnp.concatenate([low, high])))
    value = value - product(parts((down_high, down_low)), split(middle * scale_of(level)))
    if ahead:
        up_high, up_low, iterate = refs[5:8]
        base = product(parts((up_high, up_low)), split(value))
        if split_rows:
            halves_by_core(base, refs[8], refs[9])
        else:
            refs[8][...] = base
    else:
        iterate = refs[5]
    iterate[...] = value


def settle(level, iterate, old, theirs, mine, other, coupling, downs, ups, split_rows):
    points, columns = iterate.shape
    half, rank = mine.shape[0], coupling.shape[2] // 2
    ahead = len(ups) > 0
    outs = [((points, columns), F32)]
    if ahead:
        outs = outs + ([((half, columns), F32)] * 2 if split_rows else [((rank, columns), F32)])
    return call(
        functools.partial(settle_body, level, len(theirs), ahead, split_rows),
        outs,
        iterate,
        *old,
        *theirs,
        mine,
        other,
        Window(coupling, (level, ALL, slice(0, rank)), (rank, rank)),
        *downs,
        *ups,
    )


def join_body(jump_mine, jump_sent, base_mine, base_sent, jump_high, jump_low, base):
    half = base.shape[0]
    for k in range(2):
        at = ALL, slice(k * half, (k + 1) * half)
        put((jump_high, jump_low), k, split(jump_mine[at] + jump_sent[at]))
    base[...] = base_mine[...] + base_sent[...]


def join(jump, base):
    half, rank = jump[0].shape
    columns = base[0].shape[1]
    return call(
        join_body, two_parts(2, half, half) + [((half, columns), F32)], *jump, *base
    )


def sub_body(side, base, factor_high, factor_low, value, out):
    core = lax.axis_index("leaf") & 1
    at = core if side == 0 else 1 - core
    out[...] = base[...] - product(parts((factor_high, factor_low), at), split(value[...]))


def rows_body(turn, base, factor_high, factor_low, value, out):
    core = lax.axis_index("leaf") & 1
    half = out.shape[0]
    rows = pl.ds(pl.multiple_of((1 - core if turn else core) * half, half), half)
    out[...] = base[rows, :] - product(
        parts((factor_high, factor_low), (1 - core, rows)), split(value[...])
    )


def rows_of(turn, base, factor, value):
    rows, columns = base.shape
    return call(functools.partial(rows_body, turn), [((rows // 2, columns), F32)], base, *factor, value)[0]


def sub(side, base, factor, value):
    return call(functools.partial(sub_body, side), [(base.shape, F32)], base, *factor, value)[0]


def sub_whole_body(*refs):
    jump, value, out = refs[-3:]
    acc = refs[0][...]
    for ref in refs[1:-3]:
        acc = acc + ref[...]
    out[...] = acc - product(split(jump[...]), split(value[...]))


def sub_whole(bases, jump, value):
    return call(sub_whole_body, [(bases[0].shape, F32)], *bases, jump, value)[0]


def per_device(coords, weights, near_mask, leaf_inverse, up_basis, coupling, down_basis):
    points, columns = weights.shape
    rank = up_basis.shape[2]
    rows = points // CHUNKS
    me = lax.axis_index("leaf")
    same = (me & 1) == ((me >> 1) & 1)
    bases = up_basis, coupling, down_basis

    def pack(k):
        outs = [((rows + PAD, columns), F32)] + [((8, points), F32)] * (k == 0)
        return call(
            functools.partial(pack_body, k),
            outs,
            Window(coords, (ALL, ALL), (3, points)),
            Window(weights, (slice(k * rows, (k + 1) * rows),), (rows, columns)),
        )

    message, where = pack(0)
    messages = [message, pack(1)[0]]
    across = [exchange(messages[0], 2)]
    far = permute(messages[1], lambda i: i + 4 if i & 2 else i - 4)
    across = across + [exchange(messages[1], 2)]
    beside = [exchange(m, 1) for m in messages]

    total, flags = call(
        own_body,
        [((points, columns), F32), ((8, columns), F32)],
        where,
        near_mask,
        *messages,
    )
    opening = call(
        open_body,
        two_parts(rank, points) + two_parts(points, points),
        Window(up_basis, (0,), (points, rank)),
        Window(leaf_inverse, (ALL,), (points, points)),
    )

    def add(total, **kinds):
        return call(
            functools.partial(add_body, [k for k, v in kinds.items() for _ in v]),
            [((points, columns), F32)],
            total,
            where,
            flags,
            *[m for v in kinds.values() for m in v],
        )[0]

    total = add(total, beside=beside)
    across[0] = after(across[0], total)
    passed = [permute(across[0], lambda i: i - 4 if i & 2 else i + 4)]
    passed = passed + [exchange(far, 2)]
    downs, factor, ups, jump = fold(0, *bases, total, True)
    jump_sent = exchange(jump[1], 1)
    total = add(total, across=across)
    crossed = [exchange(jnp.where(same, across[0], after(passed[0], total, *opening, *factor)), 1)]
    total = add(total, passed=passed[:1])
    far = after(passed[1], total)
    crossed = crossed + [exchange(jnp.where(same, across[1], far), 1)]
    total = add(total, passed=[far], crossed=crossed[:1])
    *near, skeleton = call(
        start_body,
        two_parts(points, columns) + [((rank, columns), F32)],
        total,
        where,
        flags,
        crossed[1],
        *opening[0:2],
    )

    half = rank // 2
    partner = exchange(skeleton, 1)
    iterate, base_mine, base_other = call(
        settle_first_body,
        [((points, columns), F32)] + [((half, columns), F32)] * 2,
        *near,
        skeleton,
        *opening[2:4],
        Window(coupling, (0, ALL, slice(0, rank)), (rank, rank)),
        *downs,
        *ups,
    )
    base = sub_whole((base_mine, exchange(base_other, 1)), jump_sent, skeleton)
    partner = after(partner, base)
    mine = sub_whole((base,), jump[0], partner)
    theirs = [partner]

    for level in range(1, LEVELS):
        ahead, joined = level + 1 < LEVELS, level == 2
        downs, next_factor, ups, jump = fold(level, *bases, mine, joined)
        pending = (*downs, *next_factor, *ups, *jump)
        for even, odd in {1: (), 2: ((2, 2),), 3: ((4, 2), (2, 4))}[level]:
            got = permute(mine, lambda i: i ^ (odd if i & 1 else even))
            mine = mine + after(got, *pending)
            pending = ()
        arriving = exchange(mine, 1 << level)
        other = exchange(mine, 1)
        if joined:
            jump = jump[0], exchange(jump[1], 1)
        iterate, *base = settle(
            level, iterate, factor, theirs, mine, other, coupling, downs, ups, joined
        )
        factor = next_factor
        arriving = after(arriving, iterate, *base)
        theirs = [arriving, exchange(arriving, 1)]
        if joined:
            base_other = after(base[1], arriving)
            *jump, base = join(jump, (base[0], exchange(base_other, 1)))
            mine = sub(1, sub(0, base, jump, theirs[0]), jump, theirs[1])
        elif ahead:
            base = sub(0, base[0], jump, theirs[0])
            mine = rows_of(0, base, jump, theirs[1]) + exchange(
                rows_of(1, base, jump, theirs[1]), 1
            )
    return sub(1, sub(0, iterate, factor, theirs[0]), factor, theirs[1])


def solution(mesh):
    in_specs = (
        P(None, "leaf"),
        P("leaf", None),
        P("leaf", None),
        P("leaf", None),
        P(None, "leaf", None),
        P(None, "leaf", None),
        P(None, "leaf", None),
    )
    return jax.shard_map(
        per_device, mesh=mesh, in_specs=in_specs, out_specs=P("leaf", None), check_vma=False
    )
```

time: 163 us -> 96.4 us (0.59)
  waiting for transfers between devices: 97 us -> 33.8 us
  Pallas kernels: 0 us -> 39.5 us
  matrix products: 26.2 us -> 0 us
  starting transfers between devices: 32.5 us -> 17 us
  between operations: 2.93 us -> 0.61 us
    ppermute x18 -> x27, waiting for transfers between devices: 97 us -> 33.8 us  [permute(): lax.ppermute(x, 'leaf', [(i, target(i) % count) for i in range(count)])]
    pallas_call x0 -> x27, Pallas kernels: none -> 39.5 us  [call(): pl.pallas_call(kernel, in_specs=[spec(arg) for arg in args], out_specs=[p...]
    dot_general x18 -> x0, matrix products: 26.2 us -> none  [the longest x5 7.89 us: kernel_tile(): jnp.dot(gauss(own_points, other_points), values, precision=lax.Precision....]
    ppermute x18 -> x27, starting transfers between devices: 32.5 us -> 17 us  [permute(): lax.ppermute(x, 'leaf', [(i, target(i) % count) for i in range(count)])]
    unnamed x10 -> x20, local copies, waits for them, and re-layouts: 0.03 us -> 4.82 us
    slice x6 -> x0, local copies, waits for them, and re-layouts: 2.32 us -> none  [the longest x1 1.48 us: per_device(): near_mask[0, slot].astype(jnp.float32)]
  transfers between devices with their start and end apart: 18 -> 27, of which waited for: 12 -> 15; matrix products, arithmetic and copies ran while one was open for 5% -> 0% of each run, Pallas kernels for 0% -> 39%
where the time goes in v2:
time: 96.4 us; the launch traced here: 96 us
  Pallas kernels  39.5 us (41%)
  waiting for transfers between devices  33.8 us (35%)
  starting transfers between devices  17 us (18%)
  local copies, waits for them, and re-layouts  4.82 us (5%)
    pallas_call x27, Pallas kernels, call(): pl.pallas_call(kernel, in_specs=[spec(arg) for arg in args], out_specs=[p...  39.5 us
    ppermute x27, waiting for transfers between devices, permute(): lax.ppermute(x, 'leaf', [(i, target(i) % count) for i in range(count)])  33.8 us
    ppermute x27, starting transfers between devices, permute(): lax.ppermute(x, 'leaf', [(i, target(i) % count) for i in range(count)])  17 us
    unnamed x20, local copies, waits for them, and re-layouts  4.82 us
  transfers between devices with their start and end apart: 27, of which 15 were waited for; matrix products, arithmetic and copies ran while one was open for 0% of the time, Pallas kernels for 39%

profile of v2, /device:TPU:0, one launch (start us, length us, event | category | flops | bytes accessed | tf_op | source)
XLA Modules:
  0.0 96.0 jit_solution(440427768898084480)
XLA Ops:
  0.0 1.0 %copy-done = f32[512,256]{1,0:T(8,128)S(1)} copy-done((f32[512,256]{1,0:T(8,128)S(1)}, f32[512,256]{1,0:T(8,128)}, u32[]{:S(2)}) %copy-start) | copy-done | bytes 524312
  1.0 0.7 copy-done.8
  1.8 0.5 collective-permute-start
  2.5 2.9 %collective-permute-start.2 = (f32[264,256]{1,0:T(8,128)S(1)}, f32[264,256]{1,0:T(8,128)S(1)}, u32[]{:S(2)}, u32[]{:S(2)}) collective-permute-start(f32[264,256]{1,0:T(8,128)S(1)} %get-tuple-element.66.refs_2_), channel_id=1, source_target_pairs={{0,2},{1,3},{2,0},{3,1},{4,6},{5,7},{6,4},{7,5},{8,10},{9,11},{10,... | collective-permute-start | bytes 811016 | tf_op jit(solution)/shard_map/ppermute | solution.py:22
  5.5 4.6 %collective-permute-start.5 = (f32[264,256]{1,0:T(8,128)S(1)}, f32[264,256]{1,0:T(8,128)}, u32[]{:S(2)}, u32[]{:S(2)}) collective-permute-start(f32[264,256]{1,0:T(8,128)S(1)} %shard_map.74.refs_3_), channel_id=1, source_target_pairs={{0,28},{1,29},{2,6},{3,7},{4,0},{5,1},{6,10},{7,11},{8,4},{9,5},{1... | collective-permute-start | bytes 811016 | tf_op jit(solution)/shard_map/ppermute | solution.py:22
  10.0 0.7 copy-done.9
  10.7 1.7 %shard_map.75 = (f32[512,256]{1,0:T(8,128)S(1)}, f32[8,256]{1,0:T(8,128)S(1)}) custom-call(f32[8,512]{1,0:T(8,128)S(1)} %get-tuple-element.65.refs_0_.refs_1_, s32[1,4]{1,0:T(1,128)S(1)} %copy-done.9, f32[264,256]{1,0:T(8,128)S(1)} %get-tuple-element.66.refs_2_, f32[264,256]{1,0:T(8,128)S(1)} %shard_map.74.refs_3_), custom_call_target="tpu_custom_call" | custom-call | tf_op jit(solution)/shard_map/pallas_call | solution.py:108
  12.4 1.2 %shard_map.76.refs_0_ = f32[512,256]{1,0:T(8,128)S(1)} custom-call(f32[512,256]{1,0:T(8,128)S(1)} %get-tuple-element.67.refs_0_, f32[8,512]{1,0:T(8,128)S(1)} %get-tuple-element.65.refs_0_.refs_1_, f32[8,256]{1,0:T(8,128)S(1)} %get-tuple-element.68.refs_2_, f32[264,256]{1,0:T(8,128)S(1)} %collective-permute-done.refs_3_, ...), custom_call_target="tpu_custom_call" | custom-call | tf_op jit(solution)/shard_map/pallas_call | solution.py:108
  13.6 1.2 %collective-permute-start.4 = (f32[264,256]{1,0:T(8,128)S(1)}, f32[264,256]{1,0:T(8,128)S(1)}, u32[]{:S(2)}, u32[]{:S(2)}) collective-permute-start(f32[264,256]{1,0:T(8,128)S(1)} %collective-permute-done.2.refs_3_), channel_id=1, source_target_pairs={{0,4},{1,5},{2,30},{3,31},{4,8},{5,9},{6,2},{7,3},{8,12},{9,13},{1... | collective-permute-start | bytes 811016 | tf_op jit(solution)/shard_map/ppermute | solution.py:22
  14.8 0.9 collective-permute-done.5
  15.7 3.6 %collective-permute-start.6 = (f32[264,256]{1,0:T(8,128)}, f32[264,256]{1,0:T(8,128)S(1)}, u32[]{:S(2)}, u32[]{:S(2)}) collective-permute-start(f32[264,256]{1,0:T(8,128)} %collective-permute-done.5), channel_id=1, source_target_pairs={{0,2},{1,3},{2,0},{3,1},{4,6},{5,7},{6,4},{7,5},{8,10},{9,11},{10,... | collective-permute-start | bytes 811016 | tf_op jit(solution)/shard_map/ppermute | solution.py:22
  19.4 2.6 %shard_map.79 = (bf16[512,512]{1,0:T(8,128)(2,1)S(1)}, bf16[512,512]{1,0:T(8,128)(2,1)S(1)}, bf16[512,512]{1,0:T(8,128)(2,1)S(1)}, bf16[512,512]{1,0:T(8,128)(2,1)S(1)}) custom-call(f32[4,512,512]{2,1,0:T(8,128)} %refs_3_.5, f32[512,512]{1,0:T(8,128)S(1)} %copy-done.1), custom_call_target="tpu_custom_call" | custom-call | tf_op jit(solution)/shard_map/pallas_call | solution.py:108
  22.0 0.8 copy-done.2
  22.8 0.8 copy-done.4
  23.6 0.8 copy-done.6
  24.4 3.6 %shard_map.80 = (bf16[512,512]{1,0:T(8,128)(2,1)S(1)}, bf16[512,512]{1,0:T(8,128)(2,1)S(1)}, bf16[2,512,256]{2,1,0:T(8,128)(2,1)S(1)}, bf16[2,512,256]{2,1,0:T(8...) custom-call(f32[512,256]{1,0:T(8,128)S(1)} %shard_map.76.refs_0_, ...), custom_call_target="tpu_custom_call" | custom-call | tf_op jit(solution)/shard_map/pallas_call | solution.py:108
  28.1 1.2 %shard_map.77.refs_0_ = f32[512,256]{1,0:T(8,128)S(1)} custom-call(f32[512,256]{1,0:T(8,128)S(1)} %shard_map.76.refs_0_, f32[8,512]{1,0:T(8,128)S(1)} %get-tuple-element.65.refs_0_.refs_1_, f32[8,256]{1,0:T(8,128)S(1)} %get-tuple-element.68.refs_2_, f32[264,256]{1,0:T(8,128)S(1)} %collective-permute-done.2.refs_3_, f32[264,256]{1,0:T(8,128)S(1)} %collective-permute-done.3.refs_4_), custom_call_target="tpu_custom_call" | custom-call | tf_op jit(solution)/shard_map/pallas_call | solution.py:108
  29.4 0.8 shard_map.78.refs_0_
  30.2 0.6 collective-permute-start.8
  30.9 1.2 %shard_map.81.refs_0_ = f32[512,256]{1,0:T(8,128)S(1)} custom-call(f32[512,256]{1,0:T(8,128)S(1)} %shard_map.78.refs_0_, f32[8,512]{1,0:T(8,128)S(1)} %get-tuple-element.65.refs_0_.refs_1_, f32[8,256]{1,0:T(8,128)S(1)} %get-tuple-element.68.refs_2_, f32[264,256]{1,0:T(8,128)S(1)} %collective-permute-done.6.refs_3_, f32[264,256]{1,0:T(8,128)S(1)} %collective-permute-done.7.refs_4_), custom_call_target="tpu_custom_call" | custom-call | tf_op jit(solution)/shard_map/pallas_call | solution.py:108
  32.1 1.3 %shard_map.82 = (bf16[512,256]{1,0:T(8,128)(2,1)S(1)}, bf16[512,256]{1,0:T(8,128)(2,1)S(1)}, f32[512,256]{1,0:T(8,128)S(1)}) custom-call(f32[512,256]{1,0:T(8,128)S(1)} %shard_map.81.refs_0_, f32[8,512]{1,0:T(8,128)S(1)} %get-tuple-element.65.refs_0_.refs_1_, f32[8,256]{1,0:T(8,128)S(1)} %get-tuple-element.68.refs_2_, ...), custom_call_target="tpu_custom_call" | custom-call | tf_op jit(solution)/shard_map/pallas_call | solution.py:108
  33.4 0.4 collective-permute-start.9
  33.8 3.3 %shard_map.83 = (f32[512,256]{1,0:T(8,128)S(1)}, f32[256,256]{1,0:T(8,128)S(1)}, f32[256,256]{1,0:T(8,128)S(1)}) custom-call(bf16[512,256]{1,0:T(8,128)(2,1)S(1)} %get-tuple-element.78.refs_0_, bf16[512,256]{1,0:T(8,128)(2,1)S(1)} %get-tuple-element.79.refs_1_, f32[512,256]{1,0:T(8,128)S(1)} %get-tuple-element.80.refs_2_.refs_3_, ...), custom_call_target="tpu_custom_call" | custom-call | tf_op jit(solution)/shard_map/pallas_call | solution.py:108
  37.4 1.4 %collective-permute-done.10.refs_1_ = f32[256,256]{1,0:T(8,128)S(1)} collective-permute-done((f32[256,256]{1,0:T(8,128)S(1)}, f32[256,256]{1,0:T(8,128)S(1)}, u32[]{:S(2)}, u32[]{:S(2)}) %collective-permute-start.10) | collective-permute-done | bytes 262176 | tf_op jit(solution)/shard_map/ppermute | solution.py:22
  38.7 0.4 shard_map.84.refs_0_
  39.1 0.4 shard_map.85.refs_0_.refs_4_
  39.8 3.6 %shard_map.86 = (bf16[512,512]{1,0:T(8,128)(2,1)S(1)}, bf16[512,512]{1,0:T(8,128)(2,1)S(1)}, bf16[2,512,256]{2,1,0:T(8,128)(2,1)S(1)}, bf16[2,512,256]{2,1,0:T(8...) custom-call(f32[256,256]{1,0:T(8,128)S(1)} %shard_map.85.refs_0_.ref, ...), custom_call_target="tpu_custom_call" | custom-call | tf_op jit(solution)/shard_map/pallas_call | solution.py:108
  43.4 2.9 %shard_map.87 = (f32[512,256]{1,0:T(8,128)S(1)}, f32[512,256]{1,0:T(8,128)S(1)}) custom-call(f32[512,256]{1,0:T(8,128)S(1)} %get-tuple-element.85.refs_0_, bf16[2,512,256]{2,1,0:T(8,128)(2,1)S(1)} %get-tuple-element.75.refs_1_, bf16[2,512,256]{2,1,0:T(8,128)(2,1)S(1)} %get-tuple-element.76.refs_2_, f32[512,256]{1,0:T(8,128)S(1)} %collective-permute-done.9.refs_2_.refs_3_, ...), custom_call_target="tpu_custom_call" | custom-call | tf_op jit(solution)/shard_map/pallas_call | solution.py:108
  46.4 1.9 %collective-permute-done.13.refs_3_ = f32[256,256]{1,0:T(8,128)S(1)} collective-permute-done((f32[256,256]{1,0:T(8,128)S(1)}, f32[256,256]{1,0:T(8,128)S(1)}, u32[]{:S(2)}, u32[]{:S(2)}) %collective-permute-start.13) | collective-permute-done | bytes 262176 | tf_op jit(solution)/shard_map/ppermute | solution.py:22
  48.3 0.4 shard_map.88.refs_0_
  48.7 1.1 %collective-permute-done.14.refs_3_.refs_4_ = f32[256,256]{1,0:T(8,128)S(1)} collective-permute-done((f32[256,256]{1,0:T(8,128)S(1)}, f32[256,256]{1,0:T(8,128)S(1)}, u32[]{:S(2)}, u32[]{:S(2)}) %collective-permute-start.14) | collective-permute-done | bytes 262176 | tf_op jit(solution)/shard_map/ppermute | solution.py:22
  50.7 1.1 %collective-permute-done.15 = f32[256,256]{1,0:T(8,128)S(1)} collective-permute-done((f32[256,256]{1,0:T(8,128)S(1)}, f32[256,256]{1,0:T(8,128)S(1)}, u32[]{:S(2)}, u32[]{:S(2)}) %collective-permute-start.15) | collective-permute-done | bytes 262176 | tf_op jit(solution)/shard_map/ppermute | solution.py:22
  52.1 3.9 %shard_map.91 = (bf16[512,512]{1,0:T(8,128)(2,1)S(1)}, bf16[512,512]{1,0:T(8,128)(2,1)S(1)}, bf16[2,512,256]{2,1,0:T(8,128)(2,1)S(1)}, bf16[2,512,256]{2,1,0:T(8...) custom-call(f32[256,256]{1,0:T(8,128)S(1)} %add.12.refs_0_, ...), custom_call_target="tpu_custom_call" | custom-call | tf_op jit(solution)/shard_map/pallas_call | solution.py:108
  56.0 4.2 %collective-permute-done.16 = f32[256,256]{1,0:T(8,128)S(1)} collective-permute-done((f32[256,256]{1,0:T(8,128)S(1)}, f32[256,256]{1,0:T(8,128)S(1)}, u32[]{:S(2)}, u32[]{:S(2)}) %collective-permute-start.16) | collective-permute-done | bytes 262176 | tf_op jit(solution)/shard_map/ppermute | solution.py:22
  60.4 0.4 collective-permute-start.20
  60.8 1.0 %collective-permute-done.17.refs_6_ = f32[256,256]{1,0:T(8,128)S(1)} collective-permute-done((f32[256,256]{1,0:T(8,128)S(1)}, f32[256,256]{1,0:T(8,128)S(1)}, u32[]{:S(2)}, u32[]{:S(2)}) %collective-permute-start.17) | collective-permute-done | bytes 262176 | tf_op jit(solution)/shard_map/ppermute | solution.py:22
  61.8 3.1 %shard_map.92 = (f32[512,256]{1,0:T(8,128)S(1)}, f32[256,256]{1,0:T(8,128)S(1)}, f32[256,256]{1,0:T(8,128)S(1)}) custom-call(f32[512,256]{1,0:T(8,128)S(1)} %get-tuple-element.95.refs_0_, bf16[2,512,256]{2,1,0:T(8,128)(2,1)S(1)} %get-tuple-element.96.refs_1_, bf16[2,512,256]{2,1,0:T(8,128)(2,1)S(1)} %get-tuple-element.97.refs_2_, ...), custom_call_target="tpu_custom_call" | custom-call | tf_op jit(solution)/shard_map/pallas_call | solution.py:108
  65.0 4.0 %collective-permute-done.18.refs_3_ = f32[256,256]{1,0:T(8,128)S(1)} collective-permute-done((f32[256,256]{1,0:T(8,128)S(1)}, f32[256,256]{1,0:T(8,128)S(1)}, u32[]{:S(2)}, u32[]{:S(2)}) %collective-permute-start.18) | collective-permute-done | bytes 262176 | tf_op jit(solution)/shard_map/ppermute | solution.py:22
  69.1 0.5 collective-permute-start.19
  69.6 1.0 %collective-permute-done.21.refs_3_ = f32[256,256]{1,0:T(8,128)S(1)} collective-permute-done((f32[256,256]{1,0:T(8,128)S(1)}, f32[256,256]{1,0:T(8,128)S(1)}, u32[]{:S(2)}, u32[]{:S(2)}) %collective-permute-start.21) | collective-permute-done | bytes 262176 | tf_op jit(solution)/shard_map/ppermute | solution.py:22
  71.7 2.6 %shard_map.96 = (bf16[512,512]{1,0:T(8,128)(2,1)S(1)}, bf16[512,512]{1,0:T(8,128)(2,1)S(1)}, bf16[2,512,256]{2,1,0:T(8,128)(2,1)S(1)}, bf16[2,512,256]{2,1,0:T(8,128)(2,1)S(1)}) custom-call(f32[256,256]{1,0:T(8,128)S(1)} %shard_map.95.refs_0_, f32[4,512,512]{2,1,0:T(8,128)} %refs_1_.15, f32[4,512,1024]{2,1,0:T(8,128)} %refs_7_.3), custom_call_target="tpu_custom_call" | custom-call | tf_op jit(solution)/shard_map/pallas_call | solution.py:108
  74.2 3.5 %collective-permute-done.22 = f32[256,256]{1,0:T(8,128)S(1)} collective-permute-done((f32[256,256]{1,0:T(8,128)S(1)}, f32[256,256]{1,0:T(8,128)S(1)}, u32[]{:S(2)}, u32[]{:S(2)}) %collective-permute-start.22) | collective-permute-done | bytes 262176 | tf_op jit(solution)/shard_map/ppermute | solution.py:22
  78.2 6.1 %collective-permute-done.23 = f32[256,256]{1,0:T(8,128)S(1)} collective-permute-done((f32[256,256]{1,0:T(8,128)S(1)}, f32[256,256]{1,0:T(8,128)S(1)}, u32[]{:S(2)}, u32[]{:S(2)}) %collective-permute-start.23) | collective-permute-done | bytes 262176 | tf_op jit(solution)/shard_map/ppermute | solution.py:22
  84.4 1.4 %collective-permute-done.24.refs_6_ = f32[256,256]{1,0:T(8,128)S(1)} collective-permute-done((f32[256,256]{1,0:T(8,128)S(1)}, f32[256,256]{1,0:T(8,128)S(1)}, u32[]{:S(2)}, u32[]{:S(2)}) %collective-permute-start.24) | collective-permute-done | bytes 262176 | tf_op jit(solution)/shard_map/ppermute | solution.py:22
  85.9 2.5 %shard_map.97.refs_0_ = f32[512,256]{1,0:T(8,128)S(1)} custom-call(f32[512,256]{1,0:T(8,128)S(1)} %get-tuple-element.111.refs_0_, bf16[2,512,256]{2,1,0:T(8,128)(2,1)S(1)} %get-tuple-element.104.refs_1_, bf16[2,512,256]{2,1,0:T(8,128)(2,1)S(1)} %get-tuple-element.105.refs_2_, f32[256,256]{1,0:T(8,128)S(1)} %collective-permute-done.18.refs_3_, ...), custom_call_target="tpu_custom_call" | custom-call | tf_op jit(solution)/shard_map/pallas_call | solution.py:108
  88.4 4.7 %collective-permute-done.25.refs_3_ = f32[256,256]{1,0:T(8,128)S(1)} collective-permute-done((f32[256,256]{1,0:T(8,128)S(1)}, f32[256,256]{1,0:T(8,128)S(1)}, u32[]{:S(2)}, u32[]{:S(2)}) %collective-permute-start.25) | collective-permute-done | bytes 262176 | tf_op jit(solution)/shard_map/ppermute | solution.py:22
  93.5 1.1 %collective-permute-done.26.refs_3_ = f32[256,256]{1,0:T(8,128)S(1)} collective-permute-done((f32[256,256]{1,0:T(8,128)S(1)}, f32[256,256]{1,0:T(8,128)S(1)}, u32[]{:S(2)}, u32[]{:S(2)}) %collective-permute-start.26) | collective-permute-done | bytes 262176 | tf_op jit(solution)/shard_map/ppermute | solution.py:22
  94.6 1.2 %shard_map.99 = f32[512,256]{1,0:T(8,128)} custom-call(f32[512,256]{1,0:T(8,128)S(1)} %shard_map.98.refs_0_, bf16[2,512,256]{2,1,0:T(8,128)(2,1)S(1)} %get-tuple-element.121.refs_1_, bf16[2,512,256]{2,1,0:T(8,128)(2,1)S(1)} %get-tuple-element.122.refs_2_, f32[256,256]{1,0:T(8,128)S(1)} %collective-permute-done.26.refs_3_), custom_call_target="tpu_custom_call" | custom-call | tf_op jit(solution)/shard_map/pallas_call | solution.py:108
  (59 shorter events, 4.4 us)
Async XLA Ops:
  0.0 1.0 %copy-start = (f32[512,256]{1,0:T(8,128)S(1)}, f32[512,256]{1,0:T(8,128)}, u32[]{:S(2)}) copy-start(f32[512,256]{1,0:T(8,128)} %refs_1_.9) | copy-start | bytes 1572868
  1.0 0.7 copy-start.8
  1.7 17.6 %copy-start.1 = (f32[512,512]{1,0:T(8,128)S(1)}, f32[512,512]{1,0:T(8,128)}, u32[]{:S(2)}) copy-start(f32[512,512]{1,0:T(8,128)} %refs_1_.11) | copy-start | bytes 3145732
  1.8 10.6 %collective-permute-start = (f32[264,256]{1,0:T(8,128)S(1)}, f32[264,256]{1,0:T(8,128)S(1)}, u32[]{:S(2)}, u32[]{:S(2)}) collective-permute-start(f32[264,256]{1,0:T(8,128)S(1)} %get-tuple-element.66.refs_2_), channel_id=1, source_target_pairs={{0,1},{1,0},{2,3},{3,2},{4,5},{5,4},{6,7},{7,6},{8,9},{9,8},{10,11... | collective-permute-start | bytes 811016 | tf_op jit(solution)/shard_map/ppermute | solution.py:22
  2.4 10.0 %collective-permute-start.1 = (f32[264,256]{1,0:T(8,128)S(1)}, f32[264,256]{1,0:T(8,128)S(1)}, u32[]{:S(2)}, u32[]{:S(2)}) collective-permute-start(f32[264,256]{1,0:T(8,128)S(1)} %shard_map.74.refs_3_), channel_id=1, source_target_pairs={{0,1},{1,0},{2,3},{3,2},{4,5},{5,4},{6,7},{7,6},{8,9},{9,8},{10,11... | collective-permute-start | bytes 811016 | tf_op jit(solution)/shard_map/ppermute | solution.py:22
  2.5 11.1 %collective-permute-start.2 = (f32[264,256]{1,0:T(8,128)S(1)}, f32[264,256]{1,0:T(8,128)S(1)}, u32[]{:S(2)}, u32[]{:S(2)}) collective-permute-start(f32[264,256]{1,0:T(8,128)S(1)} %get-tuple-element.66.refs_2_), channel_id=1, source_target_pairs={{0,2},{1,3},{2,0},{3,1},{4,6},{5,7},{6,4},{7,5},{8,10},{9,11},{10,... | collective-permute-start | bytes 811016 | tf_op jit(solution)/shard_map/ppermute | solution.py:22
  5.5 10.3 %collective-permute-start.5 = (f32[264,256]{1,0:T(8,128)S(1)}, f32[264,256]{1,0:T(8,128)}, u32[]{:S(2)}, u32[]{:S(2)}) collective-permute-start(f32[264,256]{1,0:T(8,128)S(1)} %shard_map.74.refs_3_), channel_id=1, source_target_pairs={{0,28},{1,29},{2,6},{3,7},{4,0},{5,1},{6,10},{7,11},{8,4},{9,5},{1... | collective-permute-start | bytes 811016 | tf_op jit(solution)/shard_map/ppermute | solution.py:22
  10.0 18.0 %collective-permute-start.3 = (f32[264,256]{1,0:T(8,128)S(1)}, f32[264,256]{1,0:T(8,128)S(1)}, u32[]{:S(2)}, u32[]{:S(2)}) collective-permute-start(f32[264,256]{1,0:T(8,128)S(1)} %shard_map.74.refs_3_), channel_id=1, source_target_pairs={{0,2},{1,3},{2,0},{3,1},{4,6},{5,7},{6,4},{7,5},{8,10},{9,11},{10,... | collective-permute-start | bytes 811016 | tf_op jit(solution)/shard_map/ppermute | solution.py:22
  10.0 0.7 copy-start.9
  13.6 15.6 %collective-permute-start.4 = (f32[264,256]{1,0:T(8,128)S(1)}, f32[264,256]{1,0:T(8,128)S(1)}, u32[]{:S(2)}, u32[]{:S(2)}) collective-permute-start(f32[264,256]{1,0:T(8,128)S(1)} %collective-permute-done.2.refs_3_), channel_id=1, source_target_pairs={{0,4},{1,5},{2,30},{3,31},{4,8},{5,9},{6,2},{7,3},{8,12},{9,13},{1... | collective-permute-start | bytes 811016 | tf_op jit(solution)/shard_map/ppermute | solution.py:22
  15.7 14.4 %collective-permute-start.6 = (f32[264,256]{1,0:T(8,128)}, f32[264,256]{1,0:T(8,128)S(1)}, u32[]{:S(2)}, u32[]{:S(2)}) collective-permute-start(f32[264,256]{1,0:T(8,128)} %collective-permute-done.5), channel_id=1, source_target_pairs={{0,2},{1,3},{2,0},{3,1},{4,6},{5,7},{6,4},{7,5},{8,10},{9,11},{10,... | collective-permute-start | bytes 811016 | tf_op jit(solution)/shard_map/ppermute | solution.py:22
  22.0 0.8 copy-start.2
  22.8 0.8 copy-start.4
  23.6 0.8 copy-start.6
  28.0 4.1 %copy-start.5 = (bf16[512,512]{1,0:T(8,128)(2,1)S(1)}, bf16[512,512]{1,0:T(8,128)(2,1)}, u32[]{:S(2)}) copy-start(bf16[512,512]{1,0:T(8,128)(2,1)} %copy-done.4) | copy-start | bytes 1572868
  28.0 4.1 %copy-start.7 = (bf16[512,512]{1,0:T(8,128)(2,1)S(1)}, bf16[512,512]{1,0:T(8,128)(2,1)}, u32[]{:S(2)}) copy-start(bf16[512,512]{1,0:T(8,128)(2,1)} %copy-done.6) | copy-start | bytes 1572868
  28.1 5.8 %copy-start.3 = (bf16[512,512]{1,0:T(8,128)(2,1)S(1)}, bf16[512,512]{1,0:T(8,128)(2,1)}, u32[]{:S(2)}) copy-start(bf16[512,512]{1,0:T(8,128)(2,1)} %copy-done.2) | copy-start | bytes 1572868
  29.3 1.6 %collective-permute-start.7 = (f32[264,256]{1,0:T(8,128)S(1)}, f32[264,256]{1,0:T(8,128)S(1)}, u32[]{:S(2)}, u32[]{:S(2)}) collective-permute-start(f32[264,256]{1,0:T(8,128)S(1)} %broadcast_select_fusion.1), channel_id=1, source_target_pairs={{0,1},{1,0},{2,3},{3,2},{4,5},{5,4},{6,7},{7,6},{8,9},{9,8},{10,11... | collective-permute-start | bytes 811016 | tf_op jit(solution)/shard_map/ppermute | solution.py:22
  30.2 1.9 %collective-permute-start.8 = (f32[264,256]{1,0:T(8,128)S(1)}, f32[264,256]{1,0:T(8,128)S(1)}, u32[]{:S(2)}, u32[]{:S(2)}) collective-permute-start(f32[264,256]{1,0:T(8,128)S(1)} %broadcast_select_fusion), channel_id=1, source_target_pairs={{0,1},{1,0},{2,3},{3,2},{4,5},{5,4},{6,7},{7,6},{8,9},{9,8},{10,11... | collective-permute-start | bytes 811016 | tf_op jit(solution)/shard_map/ppermute | solution.py:22
  30.8 6.6 %collective-permute-start.11 = (f32[256,512]{1,0:T(8,128)S(1)}, f32[256,512]{1,0:T(8,128)S(1)}, u32[]{:S(2)}, u32[]{:S(2)}) collective-permute-start(f32[256,512]{1,0:T(8,128)S(1)} %get-tuple-element.88), channel_id=1, source_target_pairs={{0,1},{1,0},{2,3},{3,2},{4,5},{5,4},{6,7},{7,6},{8,9},{9,8},{10,11... | collective-permute-start | bytes 1572872 | tf_op jit(solution)/shard_map/ppermute | solution.py:22
  33.4 5.7 %collective-permute-start.9 = (f32[512,256]{1,0:T(8,128)S(1)}, f32[512,256]{1,0:T(8,128)S(1)}, u32[]{:S(2)}, u32[]{:S(2)}) collective-permute-start(f32[512,256]{1,0:T(8,128)S(1)} %get-tuple-element.80.refs_2_.refs_3_), channel_id=1, source_target_pairs={{0,1},{1,0},{2,3},{3,2},{4,5},{5,4},{6,7},{7,6},{8,9},{9,8},{10,11... | collective-permute-start | bytes 1572872 | tf_op jit(solution)/shard_map/ppermute | solution.py:22
  37.1 1.6 %collective-permute-start.10 = (f32[256,256]{1,0:T(8,128)S(1)}, f32[256,256]{1,0:T(8,128)S(1)}, u32[]{:S(2)}, u32[]{:S(2)}) collective-permute-start(f32[256,256]{1,0:T(8,128)S(1)} %get-tuple-element.87), channel_id=1, source_target_pairs={{0,1},{1,0},{2,3},{3,2},{4,5},{5,4},{6,7},{7,6},{8,9},{9,8},{10,11... | collective-permute-start | bytes 786440 | tf_op jit(solution)/shard_map/ppermute | solution.py:22
  39.5 3.9 %collective-permute-start.12 = (f32[256,256]{1,0:T(8,128)S(1)}, f32[256,256]{1,0:T(8,128)S(1)}, u32[]{:S(2)}, u32[]{:S(2)}) collective-permute-start(f32[256,256]{1,0:T(8,128)S(1)} %shard_map.85.refs_0_.refs_4_), channel_id=1, source_target_pairs={{0,1},{1,0},{2,3},{3,2},{4,5},{5,4},{6,7},{7,6},{8,9},{9,8},{10,11... | collective-permute-start | bytes 786440 | tf_op jit(solution)/shard_map/ppermute | solution.py:22
  39.8 8.6 %collective-permute-start.13 = (f32[256,256]{1,0:T(8,128)S(1)}, f32[256,256]{1,0:T(8,128)S(1)}, u32[]{:S(2)}, u32[]{:S(2)}) collective-permute-start(f32[256,256]{1,0:T(8,128)S(1)} %shard_map.85.refs_0_.refs_4_), channel_id=1, source_target_pairs={{0,2},{1,3},{2,0},{3,1},{4,6},{5,7},{6,4},{7,5},{8,10},{9,11},{10,... | collective-permute-start | bytes 786440 | tf_op jit(solution)/shard_map/ppermute | solution.py:22
  48.3 1.5 %collective-permute-start.14 = (f32[256,256]{1,0:T(8,128)S(1)}, f32[256,256]{1,0:T(8,128)S(1)}, u32[]{:S(2)}, u32[]{:S(2)}) collective-permute-start(f32[256,256]{1,0:T(8,128)S(1)} %collective-permute-done.13.refs_3_), channel_id=1, source_target_pairs={{0,1},{1,0},{2,3},{3,2},{4,5},{5,4},{6,7},{7,6},{8,9},{9,8},{10,11... | collective-permute-start | bytes 786440 | tf_op jit(solution)/shard_map/ppermute | solution.py:22
  50.2 1.6 %collective-permute-start.15 = (f32[256,256]{1,0:T(8,128)S(1)}, f32[256,256]{1,0:T(8,128)S(1)}, u32[]{:S(2)}, u32[]{:S(2)}) collective-permute-start(f32[256,256]{1,0:T(8,128)S(1)} %shard_map.90), channel_id=1, source_target_pairs={{0,1},{1,0},{2,3},{3,2},{4,5},{5,4},{6,7},{7,6},{8,9},{9,8},{10,11... | collective-permute-start | bytes 786440 | tf_op jit(solution)/shard_map/ppermute | solution.py:22
  51.8 8.4 %collective-permute-start.16 = (f32[256,256]{1,0:T(8,128)S(1)}, f32[256,256]{1,0:T(8,128)S(1)}, u32[]{:S(2)}, u32[]{:S(2)}) collective-permute-start(f32[256,256]{1,0:T(8,128)S(1)} %add.12.refs_0_), channel_id=1, source_target_pairs={{0,2},{1,3},{2,0},{3,1},{4,6},{5,7},{6,4},{7,5},{8,10},{9,11},{10,... | collective-permute-start | bytes 786440 | tf_op jit(solution)/shard_map/ppermute | solution.py:22
  60.2 1.6 %collective-permute-start.17 = (f32[256,256]{1,0:T(8,128)S(1)}, f32[256,256]{1,0:T(8,128)S(1)}, u32[]{:S(2)}, u32[]{:S(2)}) collective-permute-start(f32[256,256]{1,0:T(8,128)S(1)} %add.13.refs_5_), channel_id=1, source_target_pairs={{0,1},{1,0},{2,3},{3,2},{4,5},{5,4},{6,7},{7,6},{8,9},{9,8},{10,11... | collective-permute-start | bytes 786440 | tf_op jit(solution)/shard_map/ppermute | solution.py:22
  60.3 8.7 %collective-permute-start.18 = (f32[256,256]{1,0:T(8,128)S(1)}, f32[256,256]{1,0:T(8,128)S(1)}, u32[]{:S(2)}, u32[]{:S(2)}) collective-permute-start(f32[256,256]{1,0:T(8,128)S(1)} %add.13.refs_5_), channel_id=1, source_target_pairs={{0,4},{1,5},{2,6},{3,7},{4,0},{5,1},{6,2},{7,3},{8,12},{9,13},{10,... | collective-permute-start | bytes 786440 | tf_op jit(solution)/shard_map/ppermute | solution.py:22
  60.4 9.2 %collective-permute-start.20 = (f32[256,512]{1,0:T(8,128)S(1)}, f32[256,512]{1,0:T(8,128)S(1)}, u32[]{:S(2)}, u32[]{:S(2)}) collective-permute-start(f32[256,512]{1,0:T(8,128)S(1)} %get-tuple-element.109), channel_id=1, source_target_pairs={{0,1},{1,0},{2,3},{3,2},{4,5},{5,4},{6,7},{7,6},{8,9},{9,8},{10,11... | collective-permute-start | bytes 1572872 | tf_op jit(solution)/shard_map/ppermute | solution.py:22
  69.0 1.5 %collective-permute-start.21 = (f32[256,256]{1,0:T(8,128)S(1)}, f32[256,256]{1,0:T(8,128)S(1)}, u32[]{:S(2)}, u32[]{:S(2)}) collective-permute-start(f32[256,256]{1,0:T(8,128)S(1)} %get-tuple-element.115), channel_id=1, source_target_pairs={{0,1},{1,0},{2,3},{3,2},{4,5},{5,4},{6,7},{7,6},{8,9},{9,8},{10,11... | collective-permute-start | bytes 786440 | tf_op jit(solution)/shard_map/ppermute | solution.py:22
  69.1 2.0 %collective-permute-start.19 = (f32[256,256]{1,0:T(8,128)S(1)}, f32[256,256]{1,0:T(8,128)S(1)}, u32[]{:S(2)}, u32[]{:S(2)}) collective-permute-start(f32[256,256]{1,0:T(8,128)S(1)} %collective-permute-done.18.refs_3_), channel_id=1, source_target_pairs={{0,1},{1,0},{2,3},{3,2},{4,5},{5,4},{6,7},{7,6},{8,9},{9,8},{10,11... | collective-permute-start | bytes 786440 | tf_op jit(solution)/shard_map/ppermute | solution.py:22
  71.3 6.4 %collective-permute-start.22 = (f32[256,256]{1,0:T(8,128)S(1)}, f32[256,256]{1,0:T(8,128)S(1)}, u32[]{:S(2)}, u32[]{:S(2)}) collective-permute-start(f32[256,256]{1,0:T(8,128)S(1)} %shard_map.95.refs_0_), channel_id=1, source_target_pairs={{0,4},{1,3},{2,6},{3,1},{4,0},{5,7},{6,2},{7,5},{8,12},{9,11},{10,... | collective-permute-start | bytes 786440 | tf_op jit(solution)/shard_map/ppermute | solution.py:22
  77.8 6.4 %collective-permute-start.23 = (f32[256,256]{1,0:T(8,128)S(1)}, f32[256,256]{1,0:T(8,128)S(1)}, u32[]{:S(2)}, u32[]{:S(2)}) collective-permute-start(f32[256,256]{1,0:T(8,128)S(1)} %add.14), channel_id=1, source_target_pairs={{0,2},{1,5},{2,0},{3,7},{4,6},{5,1},{6,4},{7,3},{8,10},{9,13},{10,... | collective-permute-start | bytes 786440 | tf_op jit(solution)/shard_map/ppermute | solution.py:22
  84.3 1.6 %collective-permute-start.24 = (f32[256,256]{1,0:T(8,128)S(1)}, f32[256,256]{1,0:T(8,128)S(1)}, u32[]{:S(2)}, u32[]{:S(2)}) collective-permute-start(f32[256,256]{1,0:T(8,128)S(1)} %add.15.refs_5_), channel_id=1, source_target_pairs={{0,1},{1,0},{2,3},{3,2},{4,5},{5,4},{6,7},{7,6},{8,9},{9,8},{10,11... | collective-permute-start | bytes 786440 | tf_op jit(solution)/shard_map/ppermute | solution.py:22
  84.4 8.7 %collective-permute-start.25 = (f32[256,256]{1,0:T(8,128)S(1)}, f32[256,256]{1,0:T(8,128)S(1)}, u32[]{:S(2)}, u32[]{:S(2)}) collective-permute-start(f32[256,256]{1,0:T(8,128)S(1)} %add.15.refs_5_), channel_id=1, source_target_pairs={{0,8},{1,9},{2,10},{3,11},{4,12},{5,13},{6,14},{7,15},{8,0},{9,1},... | collective-permute-start | bytes 786440 | tf_op jit(solution)/shard_map/ppermute | solution.py:22
  93.1 1.5 %collective-permute-start.26 = (f32[256,256]{1,0:T(8,128)S(1)}, f32[256,256]{1,0:T(8,128)S(1)}, u32[]{:S(2)}, u32[]{:S(2)}) collective-permute-start(f32[256,256]{1,0:T(8,128)S(1)} %collective-permute-done.25.refs_3_), channel_id=1, source_target_pairs={{0,1},{1,0},{2,3},{3,2},{4,5},{5,4},{6,7},{7,6},{8,9},{9,8},{10,11... | collective-permute-start | bytes 786440 | tf_op jit(solution)/shard_map/ppermute | solution.py:22

commit v3 on v2

--- a/solution.py
+++ b/solution.py
@@ -191,11 +191,29 @@
     other[...] = jnp.where(core == 0, high, low)
 
 
-def open_body(up, inverse, start_high, start_low, inverse_high, inverse_low):
+def open_body(up, inverse, coupling, down, up_next, *outs):
     up_parts = split(up().T)
     inverse_parts = split(inverse())
-    put((inverse_high, inverse_low), ..., inverse_parts)
-    put((start_high, start_low), ..., split(product(up_parts, inverse_parts)))
+    put(outs[0:2], ..., split(product(up_parts, inverse_parts)))
+    put(outs[2:4], ..., inverse_parts)
+    put(outs[4:6], ..., split(coupling()))
+    put(outs[6:8], ..., split(down()))
+    put(outs[8:10], ..., split(up_next().T))
+
+
+def first_body(near_high, near_low, skeleton, inverse_high, inverse_low, high, low, iterate, middle):
+    rank = skeleton.shape[0]
+    middle[...] = product((high[:, 0:rank], low[:, 0:rank]), split(skeleton[...]))
+    iterate[...] = product(parts((inverse_high, inverse_low)), parts((near_high, near_low)))
+
+
+def second_body(iterate, middle, partner, high, low, down_high, down_low, up_high, up_low, out, mine, other):
+    rank = partner.shape[0]
+    factor = high[:, rank : 2 * rank], low[:, rank : 2 * rank]
+    correction = (middle[...] + product(factor, split(partner[...]))) * scale_of(0)
+    value = iterate[...] - product(parts((down_high, down_low)), split(correction))
+    halves_by_core(product(parts((up_high, up_low)), split(value)), mine, other)
+    out[...] = value
 
 
 def fold_body(level, ahead, split_rows, *refs):
@@ -242,28 +260,17 @@
     return got[0:2], got[2:4], got[4:6], got[6:8]
 
 
-def settle_first_body(near_high, near_low, skeleton, inverse_high, inverse_low, coupling, down_high, down_low, up_high, up_low, iterate, mine, other):
-    weights = split(coupling())
-    value = product(parts((inverse_high, inverse_low)), parts((near_high, near_low)))
-    middle = product(weights, split(skeleton[...]))
-    value = value - product(parts((down_high, down_low)), split(middle * scale_of(0)))
-    iterate[...] = value
-    halves_by_core(product(parts((up_high, up_low)), split(value)), mine, other)
-
-
 def settle_body(level, count, ahead, split_rows, *refs):
-    base_iterate, old_high, old_low = refs[0:3]
-    theirs, refs = refs[3 : 3 + count], refs[3 + count :]
+    base_iterate, refs = refs[0], refs[1:]
+    if count:
+        old, theirs, refs = refs[0:2], refs[2 : 2 + count], refs[2 + count :]
     mine, other, coupling, down_high, down_low = refs[0:5]
     core = lax.axis_index("leaf") & 1
     half = mine.shape[0]
     value = base_iterate[...]
-    if count == 1:
-        pieces = [(k, theirs[0][k * half : (k + 1) * half, :]) for k in range(2)]
-    else:
-        pieces = [(core, theirs[0][...]), (1 - core, theirs[1][...])]
-    for k, piece in pieces:
-        value = value - product(parts((old_high, old_low), k), split(piece))
+    for k in range(count):
+        at = core if k == 0 else 1 - core
+        value = value - product(parts(old, at), split(theirs[k][...]))
     low = jnp.where(core == 0, mine[...], other[...])
     high = jnp.where(core == 0, other[...], mine[...])
     middle = product(split(coupling()), split(jnp.concatenate([low, high])))
@@ -341,18 +348,6 @@
     return call(functools.partial(sub_body, side), [(base.shape, F32)], base, *factor, value)[0]
 
 
-def sub_whole_body(*refs):
-    jump, value, out = refs[-3:]
-    acc = refs[0][...]
-    for ref in refs[1:-3]:
-        acc = acc + ref[...]
-    out[...] = acc - product(split(jump[...]), split(value[...]))
-
-
-def sub_whole(bases, jump, value):
-    return call(sub_whole_body, [(bases[0].shape, F32)], *bases, jump, value)[0]
-
-
 def per_device(coords, weights, near_mask, leaf_inverse, up_basis, coupling, down_basis):
     points, columns = weights.shape
     rank = up_basis.shape[2]
@@ -386,9 +381,13 @@
     )
     opening = call(
         open_body,
-        two_parts(rank, points) + two_parts(points, points),
+        two_parts(rank, points) + two_parts(points, points) + two_parts(rank, 2 * rank)
+        + two_parts(points, rank) + two_parts(rank, points),
         Window(up_basis, (0,), (points, rank)),
         Window(leaf_inverse, (ALL,), (points, points)),
+        Window(coupling, (0,), (rank, 2 * rank)),
+        Window(down_basis, (0,), (points, rank)),
+        Window(up_basis, (1,), (points, rank)),
     )
 
     def add(total, **kinds):
@@ -405,10 +404,8 @@
     across[0] = after(across[0], total)
     passed = [permute(across[0], lambda i: i - 4 if i & 2 else i + 4)]
     passed = passed + [exchange(far, 2)]
-    downs, factor, ups, jump = fold(0, *bases, total, True)
-    jump_sent = exchange(jump[1], 1)
     total = add(total, across=across)
-    crossed = [exchange(jnp.where(same, across[0], after(passed[0], total, *opening, *factor)), 1)]
+    crossed = [exchange(jnp.where(same, across[0], after(passed[0], total, *opening)), 1)]
     total = add(total, passed=passed[:1])
     far = after(passed[1], total)
     crossed = crossed + [exchange(jnp.where(same, across[1], far), 1)]
@@ -425,20 +422,24 @@
 
     half = rank // 2
     partner = exchange(skeleton, 1)
-    iterate, base_mine, base_other = call(
-        settle_first_body,
-        [((points, columns), F32)] + [((half, columns), F32)] * 2,
+    iterate, middle = call(
+        first_body,
+        [((points, columns), F32), ((rank, columns), F32)],
         *near,
         skeleton,
-        *opening[2:4],
-        Window(coupling, (0, ALL, slice(0, rank)), (rank, rank)),
-        *downs,
-        *ups,
-    )
-    base = sub_whole((base_mine, exchange(base_other, 1)), jump_sent, skeleton)
-    partner = after(partner, base)
-    mine = sub_whole((base,), jump[0], partner)
-    theirs = [partner]
+        *opening[2:6],
+    )
+    partner = after(partner, iterate, middle)
+    iterate, base_mine, base_other = call(
+        second_body,
+        [((points, columns), F32)] + [((half, columns), F32)] * 2,
+        iterate,
+        middle,
+        partner,
+        *opening[4:10],
+    )
+    mine = base_mine + exchange(base_other, 1)
+    factor, theirs = (), ()
 
     for level in range(1, LEVELS):
         ahead, joined = level + 1 < LEVELS, level == 2

time: 96.4 us -> 91.6 us (0.950)
  Pallas kernels: 39.5 us -> 35.8 us
  local copies, waits for them, and re-layouts: 4.82 us -> 2.4 us
    pallas_call x27 -> x25, Pallas kernels: 39.5 us -> 35.8 us  [call(): pl.pallas_call(kernel, in_specs=[spec(arg) for arg in args], out_specs=[p...]
    unnamed x20 -> x8, local copies, waits for them, and re-layouts: 4.82 us -> 2.4 us
    ppermute x27 -> x26, waiting for transfers between devices: 33.8 us -> 34.5 us  [permute(): lax.ppermute(x, 'leaf', [(i, target(i) % count) for i in range(count)])]
    ppermute x27 -> x26, starting transfers between devices: 17 us -> 17.7 us  [permute(): lax.ppermute(x, 'leaf', [(i, target(i) % count) for i in range(count)])]
  transfers between devices with their start and end apart: 27 -> 26, of which waited for: 15 -> 16; matrix products, arithmetic and copies ran while one was open for 0% -> 0% of each run, Pallas kernels for 39% -> 34%
where the time goes in v3:
time: 91.6 us; the launch traced here: 91.2 us
  Pallas kernels  35.8 us (39%)
  waiting for transfers between devices  34.5 us (38%)
  starting transfers between devices  17.7 us (19%)
  local copies, waits for them, and re-layouts  2.4 us (3%)
    pallas_call x25, Pallas kernels, call(): pl.pallas_call(kernel, in_specs=[spec(arg) for arg in args], out_specs=[p...  35.8 us
    ppermute x26, waiting for transfers between devices, permute(): lax.ppermute(x, 'leaf', [(i, target(i) % count) for i in range(count)])  34.5 us
    ppermute x26, starting transfers between devices, permute(): lax.ppermute(x, 'leaf', [(i, target(i) % count) for i in range(count)])  17.7 us
    unnamed x8, local copies, waits for them, and re-layouts  2.4 us
  transfers between devices with their start and end apart: 26, of which 16 were waited for; matrix products, arithmetic and copies ran while one was open for 0% of the time, Pallas kernels for 34%

profile of v3, /device:TPU:0, one launch (start us, length us, event | category | flops | bytes accessed | tf_op | source)
XLA Modules:
  0.0 91.2 jit_solution(8725433012942271666)
XLA Ops:
  0.0 1.0 %copy-done.1 = f32[512,256]{1,0:T(8,128)S(1)} copy-done((f32[512,256]{1,0:T(8,128)S(1)}, f32[512,256]{1,0:T(8,128)}, u32[]{:S(2)}) %copy-start.1) | copy-done | bytes 524312
  1.0 0.7 copy-done.2
  1.8 0.5 collective-permute-start
  2.5 2.9 %collective-permute-start.2 = (f32[264,256]{1,0:T(8,128)S(1)}, f32[264,256]{1,0:T(8,128)S(1)}, u32[]{:S(2)}, u32[]{:S(2)}) collective-permute-start(f32[264,256]{1,0:T(8,128)S(1)} %get-tuple-element.66.refs_2_), channel_id=1, source_target_pairs={{0,2},{1,3},{2,0},{3,1},{4,6},{5,7},{6,4},{7,5},{8,10},{9,11},{10,... | collective-permute-start | bytes 811016 | tf_op jit(solution)/shard_map/ppermute | solution.py:22
  5.5 4.6 %collective-permute-start.5 = (f32[264,256]{1,0:T(8,128)S(1)}, f32[264,256]{1,0:T(8,128)S(1)}, u32[]{:S(2)}, u32[]{:S(2)}) collective-permute-start(f32[264,256]{1,0:T(8,128)S(1)} %shard_map.74.refs_3_), channel_id=1, source_target_pairs={{0,28},{1,29},{2,6},{3,7},{4,0},{5,1},{6,10},{7,11},{8,4},{9,5},{1... | collective-permute-start | bytes 811016 | tf_op jit(solution)/shard_map/ppermute | solution.py:22
  10.0 0.7 copy-done.3
  10.7 1.7 %shard_map.75 = (f32[512,256]{1,0:T(8,128)S(1)}, f32[8,256]{1,0:T(8,128)S(1)}) custom-call(f32[8,512]{1,0:T(8,128)S(1)} %get-tuple-element.65.refs_0_.refs_1_, s32[1,4]{1,0:T(1,128)S(1)} %copy-done.3, f32[264,256]{1,0:T(8,128)S(1)} %get-tuple-element.66.refs_2_, f32[264,256]{1,0:T(8,128)S(1)} %shard_map.74.refs_3_), custom_call_target="tpu_custom_call" | custom-call | tf_op jit(solution)/shard_map/pallas_call | solution.py:108
  12.4 1.2 %shard_map.76.refs_0_ = f32[512,256]{1,0:T(8,128)S(1)} custom-call(f32[512,256]{1,0:T(8,128)S(1)} %get-tuple-element.67.refs_0_, f32[8,512]{1,0:T(8,128)S(1)} %get-tuple-element.65.refs_0_.refs_1_, f32[8,256]{1,0:T(8,128)S(1)} %get-tuple-element.68.refs_2_, f32[264,256]{1,0:T(8,128)S(1)} %collective-permute-done.refs_3_, ...), custom_call_target="tpu_custom_call" | custom-call | tf_op jit(solution)/shard_map/pallas_call | solution.py:108
  13.6 1.2 %collective-permute-start.4 = (f32[264,256]{1,0:T(8,128)S(1)}, f32[264,256]{1,0:T(8,128)S(1)}, u32[]{:S(2)}, u32[]{:S(2)}) collective-permute-start(f32[264,256]{1,0:T(8,128)S(1)} %collective-permute-done.2.refs_3_), channel_id=1, source_target_pairs={{0,4},{1,5},{2,30},{3,31},{4,8},{5,9},{6,2},{7,3},{8,12},{9,13},{1... | collective-permute-start | bytes 811016 | tf_op jit(solution)/shard_map/ppermute | solution.py:22
  14.8 0.9 collective-permute-done.5
  15.7 3.6 %collective-permute-start.6 = (f32[264,256]{1,0:T(8,128)S(1)}, f32[264,256]{1,0:T(8,128)S(1)}, u32[]{:S(2)}, u32[]{:S(2)}) collective-permute-start(f32[264,256]{1,0:T(8,128)S(1)} %collective-permute-done.5), channel_id=1, source_target_pairs={{0,2},{1,3},{2,0},{3,1},{4,6},{5,7},{6,4},{7,5},{8,10},{9,11},{10,... | collective-permute-start | bytes 811016 | tf_op jit(solution)/shard_map/ppermute | solution.py:22
  19.4 4.0 %shard_map.79 = (bf16[512,512]{1,0:T(8,128)(2,1)S(1)}, bf16[512,512]{1,0:T(8,128)(2,1)S(1)}, bf16[512,512]{1,0:T(8,128)(2,1)S(1)}, bf16[512,512]{1,0:T(8,128)(2,...) custom-call(f32[4,512,512]{2,1,0:T(8,128)} %refs_3_.7, ...), custom_call_target="tpu_custom_call" | custom-call | tf_op jit(solution)/shard_map/pallas_call | solution.py:108
  23.4 1.2 %shard_map.77.refs_0_ = f32[512,256]{1,0:T(8,128)S(1)} custom-call(f32[512,256]{1,0:T(8,128)S(1)} %shard_map.76.refs_0_, f32[8,512]{1,0:T(8,128)S(1)} %get-tuple-element.65.refs_0_.refs_1_, f32[8,256]{1,0:T(8,128)S(1)} %get-tuple-element.68.refs_2_, f32[264,256]{1,0:T(8,128)S(1)} %collective-permute-done.2.refs_3_, f32[264,256]{1,0:T(8,128)S(1)} %collective-permute-done.3.refs_4_), custom_call_target="tpu_custom_call" | custom-call | tf_op jit(solution)/shard_map/pallas_call | solution.py:108
  24.6 0.8 shard_map.78.refs_0_
  25.5 0.6 collective-permute-start.8
  26.1 0.9 %collective-permute-done.7.refs_4_ = f32[264,256]{1,0:T(8,128)S(1)} collective-permute-done((f32[264,256]{1,0:T(8,128)S(1)}, f32[264,256]{1,0:T(8,128)S(1)}, u32[]{:S(2)}, u32[]{:S(2)}) %collective-permute-start.7) | collective-permute-done | bytes 270368 | tf_op jit(solution)/shard_map/ppermute | solution.py:22
  27.0 1.2 %shard_map.80.refs_0_ = f32[512,256]{1,0:T(8,128)S(1)} custom-call(f32[512,256]{1,0:T(8,128)S(1)} %shard_map.78.refs_0_, f32[8,512]{1,0:T(8,128)S(1)} %get-tuple-element.65.refs_0_.refs_1_, f32[8,256]{1,0:T(8,128)S(1)} %get-tuple-element.68.refs_2_, f32[264,256]{1,0:T(8,128)S(1)} %collective-permute-done.6.refs_3_, f32[264,256]{1,0:T(8,128)S(1)} %collective-permute-done.7.refs_4_), custom_call_target="tpu_custom_call" | custom-call | tf_op jit(solution)/shard_map/pallas_call | solution.py:108
  28.2 1.3 %shard_map.81 = (bf16[512,256]{1,0:T(8,128)(2,1)S(1)}, bf16[512,256]{1,0:T(8,128)(2,1)S(1)}, f32[512,256]{1,0:T(8,128)S(1)}) custom-call(f32[512,256]{1,0:T(8,128)S(1)} %shard_map.80.refs_0_, f32[8,512]{1,0:T(8,128)S(1)} %get-tuple-element.65.refs_0_.refs_1_, f32[8,256]{1,0:T(8,128)S(1)} %get-tuple-element.68.refs_2_, ...), custom_call_target="tpu_custom_call" | custom-call | tf_op jit(solution)/shard_map/pallas_call | solution.py:108
  29.7 1.0 %shard_map.82 = (f32[512,256]{1,0:T(8,128)S(1)}, f32[512,256]{1,0:T(8,128)S(1)}) custom-call(bf16[512,256]{1,0:T(8,128)(2,1)S(1)} %get-tuple-element.82.refs_0_, bf16[512,256]{1,0:T(8,128)(2,1)S(1)} %get-tuple-element.83.refs_1_, f32[512,256]{1,0:T(8,128)S(1)} %get-tuple-element.84.refs_2_, bf16[512,512]{1,0:T(8,128)(2,1)S(1)} %get-tuple-element.73.refs_3_, ...), custom_call_target="tpu_custom_call" | custom-call | tf_op jit(solution)/shard_map/pallas_call | solution.py:108
  30.7 0.8 collective-permute-done.9.refs_2_
  31.5 1.7 %shard_map.83 = (f32[512,256]{1,0:T(8,128)S(1)}, f32[256,256]{1,0:T(8,128)S(1)}, f32[256,256]{1,0:T(8,128)S(1)}) custom-call(f32[512,256]{1,0:T(8,128)S(1)} %get-tuple-element.85.refs_0_, f32[512,256]{1,0:T(8,128)S(1)} %get-tuple-element.86.refs_1_, f32[512,256]{1,0:T(8,128)S(1)} %collective-permute-done.9.refs_2_, ...), custom_call_target="tpu_custom_call" | custom-call | tf_op jit(solution)/shard_map/pallas_call | solution.py:108
  33.4 1.4 %collective-permute-done.10 = f32[256,256]{1,0:T(8,128)S(1)} collective-permute-done((f32[256,256]{1,0:T(8,128)S(1)}, f32[256,256]{1,0:T(8,128)S(1)}, u32[]{:S(2)}, u32[]{:S(2)}) %collective-permute-start.10) | collective-permute-done | bytes 262176 | tf_op jit(solution)/shard_map/ppermute | solution.py:22
  35.0 0.5 collective-permute-start.12
  35.5 3.6 %shard_map.84 = (bf16[512,512]{1,0:T(8,128)(2,1)S(1)}, bf16[512,512]{1,0:T(8,128)(2,1)S(1)}, bf16[2,512,256]{2,1,0:T(8,128)(2,1)S(1)}, bf16[2,512,256]{2,1,0:T(8...) custom-call(f32[256,256]{1,0:T(8,128)S(1)} %add.15.refs_0_.refs_1_, ...), custom_call_target="tpu_custom_call" | custom-call | tf_op jit(solution)/shard_map/pallas_call | solution.py:108
  39.1 2.9 %shard_map.85 = (f32[512,256]{1,0:T(8,128)S(1)}, f32[512,256]{1,0:T(8,128)S(1)}) custom-call(f32[512,256]{1,0:T(8,128)S(1)} %get-tuple-element.88.refs_0_, f32[256,256]{1,0:T(8,128)S(1)} %add.15.refs_0_.refs_1_, f32[256,256]{1,0:T(8,128)S(1)} %collective-permute-done.11.refs_2_, f32[4,512,1024]{2,1,0:T(8,128)} %refs_7_.3, ...), custom_call_target="tpu_custom_call" | custom-call | tf_op jit(solution)/shard_map/pallas_call | solution.py:108
  42.0 1.5 %collective-permute-done.12.refs_3_ = f32[256,256]{1,0:T(8,128)S(1)} collective-permute-done((f32[256,256]{1,0:T(8,128)S(1)}, f32[256,256]{1,0:T(8,128)S(1)}, u32[]{:S(2)}, u32[]{:S(2)}) %collective-permute-start.12) | collective-permute-done | bytes 262176 | tf_op jit(solution)/shard_map/ppermute | solution.py:22
  43.6 0.4 shard_map.86.refs_0_
  44.0 1.1 %collective-permute-done.13.refs_3_.refs_4_ = f32[256,256]{1,0:T(8,128)S(1)} collective-permute-done((f32[256,256]{1,0:T(8,128)S(1)}, f32[256,256]{1,0:T(8,128)S(1)}, u32[]{:S(2)}, u32[]{:S(2)}) %collective-permute-start.13) | collective-permute-done | bytes 262176 | tf_op jit(solution)/shard_map/ppermute | solution.py:22
  45.9 1.1 %collective-permute-done.14 = f32[256,256]{1,0:T(8,128)S(1)} collective-permute-done((f32[256,256]{1,0:T(8,128)S(1)}, f32[256,256]{1,0:T(8,128)S(1)}, u32[]{:S(2)}, u32[]{:S(2)}) %collective-permute-start.14) | collective-permute-done | bytes 262176 | tf_op jit(solution)/shard_map/ppermute | solution.py:22
  47.0 0.5 collective-permute-start.15
  47.6 3.9 %shard_map.89 = (bf16[512,512]{1,0:T(8,128)(2,1)S(1)}, bf16[512,512]{1,0:T(8,128)(2,1)S(1)}, bf16[2,512,256]{2,1,0:T(8,128)(2,1)S(1)}, bf16[2,512,256]{2,1,0:T(8...) custom-call(f32[256,256]{1,0:T(8,128)S(1)} %add.16.refs_0_, ...), custom_call_target="tpu_custom_call" | custom-call | tf_op jit(solution)/shard_map/pallas_call | solution.py:108
  51.4 4.0 %collective-permute-done.15 = f32[256,256]{1,0:T(8,128)S(1)} collective-permute-done((f32[256,256]{1,0:T(8,128)S(1)}, f32[256,256]{1,0:T(8,128)S(1)}, u32[]{:S(2)}, u32[]{:S(2)}) %collective-permute-start.15) | collective-permute-done | bytes 262176 | tf_op jit(solution)/shard_map/ppermute | solution.py:22
  56.1 1.0 %collective-permute-done.16.refs_6_ = f32[256,256]{1,0:T(8,128)S(1)} collective-permute-done((f32[256,256]{1,0:T(8,128)S(1)}, f32[256,256]{1,0:T(8,128)S(1)}, u32[]{:S(2)}, u32[]{:S(2)}) %collective-permute-start.16) | collective-permute-done | bytes 262176 | tf_op jit(solution)/shard_map/ppermute | solution.py:22
  57.1 3.1 %shard_map.90 = (f32[512,256]{1,0:T(8,128)S(1)}, f32[256,256]{1,0:T(8,128)S(1)}, f32[256,256]{1,0:T(8,128)S(1)}) custom-call(f32[512,256]{1,0:T(8,128)S(1)} %get-tuple-element.95.refs_0_, bf16[2,512,256]{2,1,0:T(8,128)(2,1)S(1)} %get-tuple-element.96.refs_1_, bf16[2,512,256]{2,1,0:T(8,128)(2,1)S(1)} %get-tuple-element.97.refs_2_, ...), custom_call_target="tpu_custom_call" | custom-call | tf_op jit(solution)/shard_map/pallas_call | solution.py:108
  60.3 4.0 %collective-permute-done.17.refs_3_ = f32[256,256]{1,0:T(8,128)S(1)} collective-permute-done((f32[256,256]{1,0:T(8,128)S(1)}, f32[256,256]{1,0:T(8,128)S(1)}, u32[]{:S(2)}, u32[]{:S(2)}) %collective-permute-start.17) | collective-permute-done | bytes 262176 | tf_op jit(solution)/shard_map/ppermute | solution.py:22
  64.3 0.5 collective-permute-start.18
  64.8 1.0 %collective-permute-done.20.refs_3_ = f32[256,256]{1,0:T(8,128)S(1)} collective-permute-done((f32[256,256]{1,0:T(8,128)S(1)}, f32[256,256]{1,0:T(8,128)S(1)}, u32[]{:S(2)}, u32[]{:S(2)}) %collective-permute-start.20) | collective-permute-done | bytes 262176 | tf_op jit(solution)/shard_map/ppermute | solution.py:22
  66.6 0.3 collective-permute-start.21
  66.9 2.6 %shard_map.94 = (bf16[512,512]{1,0:T(8,128)(2,1)S(1)}, bf16[512,512]{1,0:T(8,128)(2,1)S(1)}, bf16[2,512,256]{2,1,0:T(8,128)(2,1)S(1)}, bf16[2,512,256]{2,1,0:T(8,128)(2,1)S(1)}) custom-call(f32[256,256]{1,0:T(8,128)S(1)} %shard_map.93.refs_0_, f32[4,512,512]{2,1,0:T(8,128)} %refs_1_.13, f32[4,512,1024]{2,1,0:T(8,128)} %refs_7_.3), custom_call_target="tpu_custom_call" | custom-call | tf_op jit(solution)/shard_map/pallas_call | solution.py:108
  69.5 3.5 %collective-permute-done.21 = f32[256,256]{1,0:T(8,128)S(1)} collective-permute-done((f32[256,256]{1,0:T(8,128)S(1)}, f32[256,256]{1,0:T(8,128)S(1)}, u32[]{:S(2)}, u32[]{:S(2)}) %collective-permute-start.21) | collective-permute-done | bytes 262176 | tf_op jit(solution)/shard_map/ppermute | solution.py:22
  73.0 0.5 collective-permute-start.22
  73.6 5.9 %collective-permute-done.22 = f32[256,256]{1,0:T(8,128)S(1)} collective-permute-done((f32[256,256]{1,0:T(8,128)S(1)}, f32[256,256]{1,0:T(8,128)S(1)}, u32[]{:S(2)}, u32[]{:S(2)}) %collective-permute-start.22) | collective-permute-done | bytes 262176 | tf_op jit(solution)/shard_map/ppermute | solution.py:22
  79.9 1.2 %collective-permute-done.23.refs_6_ = f32[256,256]{1,0:T(8,128)S(1)} collective-permute-done((f32[256,256]{1,0:T(8,128)S(1)}, f32[256,256]{1,0:T(8,128)S(1)}, u32[]{:S(2)}, u32[]{:S(2)}) %collective-permute-start.23) | collective-permute-done | bytes 262176 | tf_op jit(solution)/shard_map/ppermute | solution.py:22
  81.1 2.5 %shard_map.95.refs_0_ = f32[512,256]{1,0:T(8,128)S(1)} custom-call(f32[512,256]{1,0:T(8,128)S(1)} %get-tuple-element.111.refs_0_, bf16[2,512,256]{2,1,0:T(8,128)(2,1)S(1)} %get-tuple-element.104.refs_1_, bf16[2,512,256]{2,1,0:T(8,128)(2,1)S(1)} %get-tuple-element.105.refs_2_, f32[256,256]{1,0:T(8,128)S(1)} %collective-permute-done.17.refs_3_, ...), custom_call_target="tpu_custom_call" | custom-call | tf_op jit(solution)/shard_map/pallas_call | solution.py:108
  83.6 4.7 %collective-permute-done.24.refs_3_ = f32[256,256]{1,0:T(8,128)S(1)} collective-permute-done((f32[256,256]{1,0:T(8,128)S(1)}, f32[256,256]{1,0:T(8,128)S(1)}, u32[]{:S(2)}, u32[]{:S(2)}) %collective-permute-start.24) | collective-permute-done | bytes 262176 | tf_op jit(solution)/shard_map/ppermute | solution.py:22
  88.3 0.4 shard_map.96.refs_0_
  88.7 1.1 %collective-permute-done.25.refs_3_ = f32[256,256]{1,0:T(8,128)S(1)} collective-permute-done((f32[256,256]{1,0:T(8,128)S(1)}, f32[256,256]{1,0:T(8,128)S(1)}, u32[]{:S(2)}, u32[]{:S(2)}) %collective-permute-start.25) | collective-permute-done | bytes 262176 | tf_op jit(solution)/shard_map/ppermute | solution.py:22
  89.9 1.2 %shard_map.97 = f32[512,256]{1,0:T(8,128)} custom-call(f32[512,256]{1,0:T(8,128)S(1)} %shard_map.96.refs_0_, bf16[2,512,256]{2,1,0:T(8,128)(2,1)S(1)} %get-tuple-element.121.refs_1_, bf16[2,512,256]{2,1,0:T(8,128)(2,1)S(1)} %get-tuple-element.122.refs_2_, f32[256,256]{1,0:T(8,128)S(1)} %collective-permute-done.25.refs_3_), custom_call_target="tpu_custom_call" | custom-call | tf_op jit(solution)/shard_map/pallas_call | solution.py:108
  (44 shorter events, 3.6 us)
Async XLA Ops:
  0.0 1.0 %copy-start.1 = (f32[512,256]{1,0:T(8,128)S(1)}, f32[512,256]{1,0:T(8,128)}, u32[]{:S(2)}) copy-start(f32[512,256]{1,0:T(8,128)} %refs_1_.8) | copy-start | bytes 1572868
  1.0 0.7 copy-start.2
  1.8 10.6 %collective-permute-start = (f32[264,256]{1,0:T(8,128)S(1)}, f32[264,256]{1,0:T(8,128)S(1)}, u32[]{:S(2)}, u32[]{:S(2)}) collective-permute-start(f32[264,256]{1,0:T(8,128)S(1)} %get-tuple-element.66.refs_2_), channel_id=1, source_target_pairs={{0,1},{1,0},{2,3},{3,2},{4,5},{5,4},{6,7},{7,6},{8,9},{9,8},{10,11... | collective-permute-start | bytes 811016 | tf_op jit(solution)/shard_map/ppermute | solution.py:22
  2.4 10.0 %collective-permute-start.1 = (f32[264,256]{1,0:T(8,128)S(1)}, f32[264,256]{1,0:T(8,128)S(1)}, u32[]{:S(2)}, u32[]{:S(2)}) collective-permute-start(f32[264,256]{1,0:T(8,128)S(1)} %shard_map.74.refs_3_), channel_id=1, source_target_pairs={{0,1},{1,0},{2,3},{3,2},{4,5},{5,4},{6,7},{7,6},{8,9},{9,8},{10,11... | collective-permute-start | bytes 811016 | tf_op jit(solution)/shard_map/ppermute | solution.py:22
  2.5 11.1 %collective-permute-start.2 = (f32[264,256]{1,0:T(8,128)S(1)}, f32[264,256]{1,0:T(8,128)S(1)}, u32[]{:S(2)}, u32[]{:S(2)}) collective-permute-start(f32[264,256]{1,0:T(8,128)S(1)} %get-tuple-element.66.refs_2_), channel_id=1, source_target_pairs={{0,2},{1,3},{2,0},{3,1},{4,6},{5,7},{6,4},{7,5},{8,10},{9,11},{10,... | collective-permute-start | bytes 811016 | tf_op jit(solution)/shard_map/ppermute | solution.py:22
  5.5 10.3 %collective-permute-start.5 = (f32[264,256]{1,0:T(8,128)S(1)}, f32[264,256]{1,0:T(8,128)S(1)}, u32[]{:S(2)}, u32[]{:S(2)}) collective-permute-start(f32[264,256]{1,0:T(8,128)S(1)} %shard_map.74.refs_3_), channel_id=1, source_target_pairs={{0,28},{1,29},{2,6},{3,7},{4,0},{5,1},{6,10},{7,11},{8,4},{9,5},{1... | collective-permute-start | bytes 811016 | tf_op jit(solution)/shard_map/ppermute | solution.py:22
  10.0 13.4 %collective-permute-start.3 = (f32[264,256]{1,0:T(8,128)S(1)}, f32[264,256]{1,0:T(8,128)S(1)}, u32[]{:S(2)}, u32[]{:S(2)}) collective-permute-start(f32[264,256]{1,0:T(8,128)S(1)} %shard_map.74.refs_3_), channel_id=1, source_target_pairs={{0,2},{1,3},{2,0},{3,1},{4,6},{5,7},{6,4},{7,5},{8,10},{9,11},{10,... | collective-permute-start | bytes 811016 | tf_op jit(solution)/shard_map/ppermute | solution.py:22
  10.0 0.7 copy-start.3
  13.6 11.0 %collective-permute-start.4 = (f32[264,256]{1,0:T(8,128)S(1)}, f32[264,256]{1,0:T(8,128)S(1)}, u32[]{:S(2)}, u32[]{:S(2)}) collective-permute-start(f32[264,256]{1,0:T(8,128)S(1)} %collective-permute-done.2.refs_3_), channel_id=1, source_target_pairs={{0,4},{1,5},{2,30},{3,31},{4,8},{5,9},{6,2},{7,3},{8,12},{9,13},{1... | collective-permute-start | bytes 811016 | tf_op jit(solution)/shard_map/ppermute | solution.py:22
  15.7 9.6 %collective-permute-start.6 = (f32[264,256]{1,0:T(8,128)S(1)}, f32[264,256]{1,0:T(8,128)S(1)}, u32[]{:S(2)}, u32[]{:S(2)}) collective-permute-start(f32[264,256]{1,0:T(8,128)S(1)} %collective-permute-done.5), channel_id=1, source_target_pairs={{0,2},{1,3},{2,0},{3,1},{4,6},{5,7},{6,4},{7,5},{8,10},{9,11},{10,... | collective-permute-start | bytes 811016 | tf_op jit(solution)/shard_map/ppermute | solution.py:22
  23.4 6.3 %copy-start = (bf16[512,1024]{1,0:T(8,128)(2,1)S(1)}, bf16[512,1024]{1,0:T(8,128)(2,1)}, u32[]{:S(2)}) copy-start(bf16[512,1024]{1,0:T(8,128)(2,1)} %get-tuple-element.76.refs_6_.refs_4_) | copy-start | bytes 3145732
  25.4 1.6 %collective-permute-start.7 = (f32[264,256]{1,0:T(8,128)S(1)}, f32[264,256]{1,0:T(8,128)S(1)}, u32[]{:S(2)}, u32[]{:S(2)}) collective-permute-start(f32[264,256]{1,0:T(8,128)S(1)} %broadcast_select_fusion.1), channel_id=1, source_target_pairs={{0,1},{1,0},{2,3},{3,2},{4,5},{5,4},{6,7},{7,6},{8,9},{9,8},{10,11... | collective-permute-start | bytes 811016 | tf_op jit(solution)/shard_map/ppermute | solution.py:22
  25.5 2.7 %collective-permute-start.8 = (f32[264,256]{1,0:T(8,128)S(1)}, f32[264,256]{1,0:T(8,128)S(1)}, u32[]{:S(2)}, u32[]{:S(2)}) collective-permute-start(f32[264,256]{1,0:T(8,128)S(1)} %broadcast_select_fusion), channel_id=1, source_target_pairs={{0,1},{1,0},{2,3},{3,2},{4,5},{5,4},{6,7},{7,6},{8,9},{9,8},{10,11... | collective-permute-start | bytes 811016 | tf_op jit(solution)/shard_map/ppermute | solution.py:22
  29.5 2.0 %collective-permute-start.9 = (f32[512,256]{1,0:T(8,128)S(1)}, f32[512,256]{1,0:T(8,128)S(1)}, u32[]{:S(2)}, u32[]{:S(2)}) collective-permute-start(f32[512,256]{1,0:T(8,128)S(1)} %get-tuple-element.84.refs_2_), channel_id=1, source_target_pairs={{0,1},{1,0},{2,3},{3,2},{4,5},{5,4},{6,7},{7,6},{8,9},{9,8},{10,11... | collective-permute-start | bytes 1572872 | tf_op jit(solution)/shard_map/ppermute | solution.py:22
  33.2 1.6 %collective-permute-start.10 = (f32[256,256]{1,0:T(8,128)S(1)}, f32[256,256]{1,0:T(8,128)S(1)}, u32[]{:S(2)}, u32[]{:S(2)}) collective-permute-start(f32[256,256]{1,0:T(8,128)S(1)} %get-tuple-element.90), channel_id=1, source_target_pairs={{0,1},{1,0},{2,3},{3,2},{4,5},{5,4},{6,7},{7,6},{8,9},{9,8},{10,11... | collective-permute-start | bytes 786440 | tf_op jit(solution)/shard_map/ppermute | solution.py:22
  34.8 4.3 %collective-permute-start.11 = (f32[256,256]{1,0:T(8,128)S(1)}, f32[256,256]{1,0:T(8,128)S(1)}, u32[]{:S(2)}, u32[]{:S(2)}) collective-permute-start(f32[256,256]{1,0:T(8,128)S(1)} %add.15.refs_0_.refs_1_), channel_id=1, source_target_pairs={{0,1},{1,0},{2,3},{3,2},{4,5},{5,4},{6,7},{7,6},{8,9},{9,8},{10,11... | collective-permute-start | bytes 786440 | tf_op jit(solution)/shard_map/ppermute | solution.py:22
  35.0 8.6 %collective-permute-start.12 = (f32[256,256]{1,0:T(8,128)S(1)}, f32[256,256]{1,0:T(8,128)S(1)}, u32[]{:S(2)}, u32[]{:S(2)}) collective-permute-start(f32[256,256]{1,0:T(8,128)S(1)} %add.15.refs_0_.refs_1_), channel_id=1, source_target_pairs={{0,2},{1,3},{2,0},{3,1},{4,6},{5,7},{6,4},{7,5},{8,10},{9,11},{10,... | collective-permute-start | bytes 786440 | tf_op jit(solution)/shard_map/ppermute | solution.py:22
  43.6 1.5 %collective-permute-start.13 = (f32[256,256]{1,0:T(8,128)S(1)}, f32[256,256]{1,0:T(8,128)S(1)}, u32[]{:S(2)}, u32[]{:S(2)}) collective-permute-start(f32[256,256]{1,0:T(8,128)S(1)} %collective-permute-done.12.refs_3_), channel_id=1, source_target_pairs={{0,1},{1,0},{2,3},{3,2},{4,5},{5,4},{6,7},{7,6},{8,9},{9,8},{10,11... | collective-permute-start | bytes 786440 | tf_op jit(solution)/shard_map/ppermute | solution.py:22
  45.4 1.6 %collective-permute-start.14 = (f32[256,256]{1,0:T(8,128)S(1)}, f32[256,256]{1,0:T(8,128)S(1)}, u32[]{:S(2)}, u32[]{:S(2)}) collective-permute-start(f32[256,256]{1,0:T(8,128)S(1)} %shard_map.88), channel_id=1, source_target_pairs={{0,1},{1,0},{2,3},{3,2},{4,5},{5,4},{6,7},{7,6},{8,9},{9,8},{10,11... | collective-permute-start | bytes 786440 | tf_op jit(solution)/shard_map/ppermute | solution.py:22
  47.0 8.4 %collective-permute-start.15 = (f32[256,256]{1,0:T(8,128)S(1)}, f32[256,256]{1,0:T(8,128)S(1)}, u32[]{:S(2)}, u32[]{:S(2)}) collective-permute-start(f32[256,256]{1,0:T(8,128)S(1)} %add.16.refs_0_), channel_id=1, source_target_pairs={{0,2},{1,3},{2,0},{3,1},{4,6},{5,7},{6,4},{7,5},{8,10},{9,11},{10,... | collective-permute-start | bytes 786440 | tf_op jit(solution)/shard_map/ppermute | solution.py:22
  55.5 1.6 %collective-permute-start.16 = (f32[256,256]{1,0:T(8,128)S(1)}, f32[256,256]{1,0:T(8,128)S(1)}, u32[]{:S(2)}, u32[]{:S(2)}) collective-permute-start(f32[256,256]{1,0:T(8,128)S(1)} %add.17.refs_5_), channel_id=1, source_target_pairs={{0,1},{1,0},{2,3},{3,2},{4,5},{5,4},{6,7},{7,6},{8,9},{9,8},{10,11... | collective-permute-start | bytes 786440 | tf_op jit(solution)/shard_map/ppermute | solution.py:22
  55.6 8.7 %collective-permute-start.17 = (f32[256,256]{1,0:T(8,128)S(1)}, f32[256,256]{1,0:T(8,128)S(1)}, u32[]{:S(2)}, u32[]{:S(2)}) collective-permute-start(f32[256,256]{1,0:T(8,128)S(1)} %add.17.refs_5_), channel_id=1, source_target_pairs={{0,4},{1,5},{2,6},{3,7},{4,0},{5,1},{6,2},{7,3},{8,12},{9,13},{10,... | collective-permute-start | bytes 786440 | tf_op jit(solution)/shard_map/ppermute | solution.py:22
  55.8 9.0 %collective-permute-start.19 = (f32[256,512]{1,0:T(8,128)S(1)}, f32[256,512]{1,0:T(8,128)S(1)}, u32[]{:S(2)}, u32[]{:S(2)}) collective-permute-start(f32[256,512]{1,0:T(8,128)S(1)} %get-tuple-element.109), channel_id=1, source_target_pairs={{0,1},{1,0},{2,3},{3,2},{4,5},{5,4},{6,7},{7,6},{8,9},{9,8},{10,11... | collective-permute-start | bytes 1572872 | tf_op jit(solution)/shard_map/ppermute | solution.py:22
  64.3 1.5 %collective-permute-start.20 = (f32[256,256]{1,0:T(8,128)S(1)}, f32[256,256]{1,0:T(8,128)S(1)}, u32[]{:S(2)}, u32[]{:S(2)}) collective-permute-start(f32[256,256]{1,0:T(8,128)S(1)} %get-tuple-element.115), channel_id=1, source_target_pairs={{0,1},{1,0},{2,3},{3,2},{4,5},{5,4},{6,7},{7,6},{8,9},{9,8},{10,11... | collective-permute-start | bytes 786440 | tf_op jit(solution)/shard_map/ppermute | solution.py:22
  64.3 2.0 %collective-permute-start.18 = (f32[256,256]{1,0:T(8,128)S(1)}, f32[256,256]{1,0:T(8,128)S(1)}, u32[]{:S(2)}, u32[]{:S(2)}) collective-permute-start(f32[256,256]{1,0:T(8,128)S(1)} %collective-permute-done.17.refs_3_), channel_id=1, source_target_pairs={{0,1},{1,0},{2,3},{3,2},{4,5},{5,4},{6,7},{7,6},{8,9},{9,8},{10,11... | collective-permute-start | bytes 786440 | tf_op jit(solution)/shard_map/ppermute | solution.py:22
  66.6 6.4 %collective-permute-start.21 = (f32[256,256]{1,0:T(8,128)S(1)}, f32[256,256]{1,0:T(8,128)S(1)}, u32[]{:S(2)}, u32[]{:S(2)}) collective-permute-start(f32[256,256]{1,0:T(8,128)S(1)} %shard_map.93.refs_0_), channel_id=1, source_target_pairs={{0,4},{1,3},{2,6},{3,1},{4,0},{5,7},{6,2},{7,5},{8,12},{9,11},{10,... | collective-permute-start | bytes 786440 | tf_op jit(solution)/shard_map/ppermute | solution.py:22
  73.0 6.4 %collective-permute-start.22 = (f32[256,256]{1,0:T(8,128)S(1)}, f32[256,256]{1,0:T(8,128)S(1)}, u32[]{:S(2)}, u32[]{:S(2)}) collective-permute-start(f32[256,256]{1,0:T(8,128)S(1)} %add.18), channel_id=1, source_target_pairs={{0,2},{1,5},{2,0},{3,7},{4,6},{5,1},{6,4},{7,3},{8,10},{9,13},{10,... | collective-permute-start | bytes 786440 | tf_op jit(solution)/shard_map/ppermute | solution.py:22
  79.5 1.6 %collective-permute-start.23 = (f32[256,256]{1,0:T(8,128)S(1)}, f32[256,256]{1,0:T(8,128)S(1)}, u32[]{:S(2)}, u32[]{:S(2)}) collective-permute-start(f32[256,256]{1,0:T(8,128)S(1)} %add.19.refs_5_), channel_id=1, source_target_pairs={{0,1},{1,0},{2,3},{3,2},{4,5},{5,4},{6,7},{7,6},{8,9},{9,8},{10,11... | collective-permute-start | bytes 786440 | tf_op jit(solution)/shard_map/ppermute | solution.py:22
  79.6 8.7 %collective-permute-start.24 = (f32[256,256]{1,0:T(8,128)S(1)}, f32[256,256]{1,0:T(8,128)S(1)}, u32[]{:S(2)}, u32[]{:S(2)}) collective-permute-start(f32[256,256]{1,0:T(8,128)S(1)} %add.19.refs_5_), channel_id=1, source_target_pairs={{0,8},{1,9},{2,10},{3,11},{4,12},{5,13},{6,14},{7,15},{8,0},{9,1},... | collective-permute-start | bytes 786440 | tf_op jit(solution)/shard_map/ppermute | solution.py:22
  88.3 1.5 %collective-permute-start.25 = (f32[256,256]{1,0:T(8,128)S(1)}, f32[256,256]{1,0:T(8,128)S(1)}, u32[]{:S(2)}, u32[]{:S(2)}) collective-permute-start(f32[256,256]{1,0:T(8,128)S(1)} %collective-permute-done.24.refs_3_), channel_id=1, source_target_pairs={{0,1},{1,0},{2,3},{3,2},{4,5},{5,4},{6,7},{7,6},{8,9},{9,8},{10,11... | collective-permute-start | bytes 786440 | tf_op jit(solution)/shard_map/ppermute | solution.py:22

commit v4 on v3

--- a/solution.py
+++ b/solution.py
@@ -19,7 +19,8 @@
 
 def permute(x, target):
     count = lax.axis_size("leaf")
-    return lax.ppermute(x, "leaf", [(i, target(i) % count) for i in range(count)])
+    pairs = [(i, target(i)) for i in range(count)]
+    return lax.ppermute(x, "leaf", [(i, j) for i, j in pairs if 0 <= j < count])
 
 
 def exchange(x, bit):
@@ -370,7 +371,6 @@
     across = [exchange(messages[0], 2)]
     far = permute(messages[1], lambda i: i + 4 if i & 2 else i - 4)
     across = across + [exchange(messages[1], 2)]
-    beside = [exchange(m, 1) for m in messages]
 
     total, flags = call(
         own_body,
@@ -400,11 +400,11 @@
             *[m for v in kinds.values() for m in v],
         )[0]
 
-    total = add(total, beside=beside)
+    beside = [exchange(m, 1) for m in after(messages, total)]
     across[0] = after(across[0], total)
     passed = [permute(across[0], lambda i: i - 4 if i & 2 else i + 4)]
     passed = passed + [exchange(far, 2)]
-    total = add(total, across=across)
+    total = add(total, beside=beside, across=across)
     crossed = [exchange(jnp.where(same, across[0], after(passed[0], total, *opening)), 1)]
     total = add(total, passed=passed[:1])
     far = after(passed[1], total)
@@ -450,7 +450,7 @@
             mine = mine + after(got, *pending)
             pending = ()
         arriving = exchange(mine, 1 << level)
-        other = exchange(mine, 1)
+        other = jnp.concatenate([exchange(m, 1) for m in jnp.split(mine, 2)])
         if joined:
             jump = jump[0], exchange(jump[1], 1)
         iterate, *base = settle(

time: 91.6 us -> 86.5 us (0.944)
  waiting for transfers between devices: 34.5 us -> 23.5 us
  starting transfers between devices: 17.7 us -> 24.1 us
    ppermute x26 -> x29, waiting for transfers between devices: 34.5 us -> 23.5 us  [permute(): return lax.ppermute(x, 'leaf', [(i, j) for i, j in pairs if 0 <= j < count])]
    ppermute x26 -> x29, starting transfers between devices: 17.7 us -> 24.1 us  [permute(): return lax.ppermute(x, 'leaf', [(i, j) for i, j in pairs if 0 <= j < count])]
    pallas_call x25 -> x24, Pallas kernels: 35.8 us -> 35.2 us  [call(): pl.pallas_call(kernel, in_specs=[spec(arg) for arg in args], out_specs=[p...]
  transfers between devices with their start and end apart: 26 -> 29, of which waited for: 16 -> 18; matrix products, arithmetic and copies ran while one was open for 0% -> 0% of each run, Pallas kernels for 34% -> 35%
where the time goes in v4:
time: 86.5 us; the launch traced here: 86.1 us
  Pallas kernels  35.2 us (41%)
  starting transfers between devices  24.1 us (28%)
  waiting for transfers between devices  23.5 us (27%)
  local copies, waits for them, and re-layouts  2.45 us (3%)
    pallas_call x24, Pallas kernels, call(): pl.pallas_call(kernel, in_specs=[spec(arg) for arg in args], out_specs=[p...  35.2 us
    ppermute x29, starting transfers between devices, permute(): return lax.ppermute(x, 'leaf', [(i, j) for i, j in pairs if 0 <= j < count])  24.1 us
    ppermute x29, waiting for transfers between devices, permute(): return lax.ppermute(x, 'leaf', [(i, j) for i, j in pairs if 0 <= j < count])  23.5 us
    unnamed x8, local copies, waits for them, and re-layouts  2.4 us
  transfers between devices with their start and end apart: 29, of which 18 were waited for; matrix products, arithmetic and copies ran while one was open for 0% of the time, Pallas kernels for 35%

profile of v4, /device:TPU:0, one launch (start us, length us, event | category | flops | bytes accessed | tf_op | source)
XLA Modules:
  0.0 86.1 jit_solution(2519339442673283084)
XLA Ops:
  0.0 1.0 %copy-done.1 = f32[512,256]{1,0:T(8,128)S(1)} copy-done((f32[512,256]{1,0:T(8,128)S(1)}, f32[512,256]{1,0:T(8,128)}, u32[]{:S(2)}) %copy-start.1) | copy-done | bytes 524312
  1.0 0.7 copy-done.2
  1.8 3.0 %collective-permute-start.2 = (f32[264,256]{1,0:T(8,128)S(1)}, f32[264,256]{1,0:T(8,128)S(1)}, u32[]{:S(2)}, u32[]{:S(2)}) collective-permute-start(f32[264,256]{1,0:T(8,128)S(1)} %get-tuple-element.71.refs_2_), channel_id=1, source_target_pairs={{0,2},{1,3},{2,0},{3,1},{4,6},{5,7},{6,4},{7,5},{8,10},{9,11},{10,... | collective-permute-start | bytes 811016 | tf_op jit(solution)/shard_map/ppermute | solution.py:23
  4.9 1.3 %collective-permute-start.5 = (f32[264,256]{1,0:T(8,128)S(1)}, f32[264,256]{1,0:T(8,128)S(1)}, u32[]{:S(2)}, u32[]{:S(2)}) collective-permute-start(f32[264,256]{1,0:T(8,128)S(1)} %shard_map.74.refs_3_), channel_id=1, source_target_pairs={{2,6},{3,7},{4,0},{5,1},{6,10},{7,11},{8,4},{9,5},{10,14},{11,15},... | collective-permute-start | bytes 811016 | tf_op jit(solution)/shard_map/ppermute | solution.py:23
  6.2 2.7 %collective-permute-start.3 = (f32[264,256]{1,0:T(8,128)S(1)}, f32[264,256]{1,0:T(8,128)S(1)}, u32[]{:S(2)}, u32[]{:S(2)}) collective-permute-start(f32[264,256]{1,0:T(8,128)S(1)} %shard_map.74.refs_3_), channel_id=1, source_target_pairs={{0,2},{1,3},{2,0},{3,1},{4,6},{5,7},{6,4},{7,5},{8,10},{9,11},{10,... | collective-permute-start | bytes 811016 | tf_op jit(solution)/shard_map/ppermute | solution.py:23
  8.9 0.7 copy-done.3
  9.6 1.7 %shard_map.75 = (f32[512,256]{1,0:T(8,128)S(1)}, f32[8,256]{1,0:T(8,128)S(1)}) custom-call(f32[8,512]{1,0:T(8,128)S(1)} %get-tuple-element.67.refs_0_.refs_1_, s32[1,4]{1,0:T(1,128)S(1)} %copy-done.3, f32[264,256]{1,0:T(8,128)S(1)} %get-tuple-element.71.refs_2_, f32[264,256]{1,0:T(8,128)S(1)} %shard_map.74.refs_3_), custom_call_target="tpu_custom_call" | custom-call | tf_op jit(solution)/shard_map/pallas_call | solution.py:109
  11.4 0.5 collective-permute-start.1
  12.1 4.0 %collective-permute-start.4 = (f32[264,256]{1,0:T(8,128)S(1)}, f32[264,256]{1,0:T(8,128)S(1)}, u32[]{:S(2)}, u32[]{:S(2)}) collective-permute-start(f32[264,256]{1,0:T(8,128)S(1)} %collective-permute-done.2.refs_5_), channel_id=1, source_target_pairs={{0,4},{1,5},{4,8},{5,9},{6,2},{7,3},{8,12},{9,13},{10,6},{11,7},{1... | collective-permute-start | bytes 811016 | tf_op jit(solution)/shard_map/ppermute | solution.py:23
  16.2 4.1 %shard_map.78 = (bf16[512,512]{1,0:T(8,128)(2,1)S(1)}, bf16[512,512]{1,0:T(8,128)(2,1)S(1)}, bf16[512,512]{1,0:T(8,128)(2,1)S(1)}, bf16[512,512]{1,0:T(8,128)(2,...) custom-call(f32[4,512,512]{2,1,0:T(8,128)} %refs_3_.7, ...), custom_call_target="tpu_custom_call" | custom-call | tf_op jit(solution)/shard_map/pallas_call | solution.py:109
  20.3 1.7 %shard_map.76.refs_0_ = f32[512,256]{1,0:T(8,128)S(1)} custom-call(f32[512,256]{1,0:T(8,128)S(1)} %get-tuple-element.69.refs_0_, f32[8,512]{1,0:T(8,128)S(1)} %get-tuple-element.67.refs_0_.refs_1_, f32[8,256]{1,0:T(8,128)S(1)} %get-tuple-element.70.refs_2_, f32[264,256]{1,0:T(8,128)S(1)} %collective-permute-done.refs_3_, ...), custom_call_target="tpu_custom_call" | custom-call | tf_op jit(solution)/shard_map/pallas_call | solution.py:109
  22.0 0.8 shard_map.77.refs_0_
  22.8 0.8 collective-permute-done.6.refs_3_
  23.7 0.6 collective-permute-start.8
  24.3 0.9 %collective-permute-done.7.refs_4_ = f32[264,256]{1,0:T(8,128)S(1)} collective-permute-done((f32[264,256]{1,0:T(8,128)S(1)}, f32[264,256]{1,0:T(8,128)S(1)}, u32[]{:S(2)}, u32[]{:S(2)}) %collective-permute-start.7) | collective-permute-done | bytes 270368 | tf_op jit(solution)/shard_map/ppermute | solution.py:23
  25.2 1.2 %shard_map.79.refs_0_ = f32[512,256]{1,0:T(8,128)S(1)} custom-call(f32[512,256]{1,0:T(8,128)S(1)} %shard_map.77.refs_0_, f32[8,512]{1,0:T(8,128)S(1)} %get-tuple-element.67.refs_0_.refs_1_, f32[8,256]{1,0:T(8,128)S(1)} %get-tuple-element.70.refs_2_, f32[264,256]{1,0:T(8,128)S(1)} %collective-permute-done.6.refs_3_, f32[264,256]{1,0:T(8,128)S(1)} %collective-permute-done.7.refs_4_), custom_call_target="tpu_custom_call" | custom-call | tf_op jit(solution)/shard_map/pallas_call | solution.py:109
  26.4 1.3 %shard_map.80 = (bf16[512,256]{1,0:T(8,128)(2,1)S(1)}, bf16[512,256]{1,0:T(8,128)(2,1)S(1)}, f32[512,256]{1,0:T(8,128)S(1)}) custom-call(f32[512,256]{1,0:T(8,128)S(1)} %shard_map.79.refs_0_, f32[8,512]{1,0:T(8,128)S(1)} %get-tuple-element.67.refs_0_.refs_1_, f32[8,256]{1,0:T(8,128)S(1)} %get-tuple-element.70.refs_2_, ...), custom_call_target="tpu_custom_call" | custom-call | tf_op jit(solution)/shard_map/pallas_call | solution.py:109
  27.9 1.0 %shard_map.81 = (f32[512,256]{1,0:T(8,128)S(1)}, f32[512,256]{1,0:T(8,128)S(1)}) custom-call(bf16[512,256]{1,0:T(8,128)(2,1)S(1)} %get-tuple-element.86.refs_0_, bf16[512,256]{1,0:T(8,128)(2,1)S(1)} %get-tuple-element.87.refs_1_, f32[512,256]{1,0:T(8,128)S(1)} %get-tuple-element.88.refs_2_, bf16[512,512]{1,0:T(8,128)(2,1)S(1)} %get-tuple-element.77.refs_3_, ...), custom_call_target="tpu_custom_call" | custom-call | tf_op jit(solution)/shard_map/pallas_call | solution.py:109
  28.9 0.8 collective-permute-done.9.refs_2_
  29.7 1.7 %shard_map.82 = (f32[512,256]{1,0:T(8,128)S(1)}, f32[256,256]{1,0:T(8,128)S(1)}, f32[256,256]{1,0:T(8,128)S(1)}) custom-call(f32[512,256]{1,0:T(8,128)S(1)} %get-tuple-element.89.refs_0_, f32[512,256]{1,0:T(8,128)S(1)} %get-tuple-element.90.refs_1_, f32[512,256]{1,0:T(8,128)S(1)} %collective-permute-done.9.refs_2_, ...), custom_call_target="tpu_custom_call" | custom-call | tf_op jit(solution)/shard_map/pallas_call | solution.py:109
  31.6 1.4 %collective-permute-done.10 = f32[256,256]{1,0:T(8,128)S(1)} collective-permute-done((f32[256,256]{1,0:T(8,128)S(1)}, f32[256,256]{1,0:T(8,128)S(1)}, u32[]{:S(2)}, u32[]{:S(2)}) %collective-permute-start.10) | collective-permute-done | bytes 262176 | tf_op jit(solution)/shard_map/ppermute | solution.py:23
  33.0 1.3 %collective-permute-start.13 = (f32[256,256]{1,0:T(8,128)S(1)}, f32[256,256]{1,0:T(8,128)S(1)}, u32[]{:S(2)}, u32[]{:S(2)}) collective-permute-start(f32[256,256]{1,0:T(8,128)S(1)} %add.15.refs_0_.refs_1_), channel_id=1, source_target_pairs={{0,2},{1,3},{2,0},{3,1},{4,6},{5,7},{6,4},{7,5},{8,10},{9,11},{10,... | collective-permute-start | bytes 786440 | tf_op jit(solution)/shard_map/ppermute | solution.py:23
  34.4 0.5 collective-permute-start.11
  34.9 3.6 %shard_map.83 = (bf16[512,512]{1,0:T(8,128)(2,1)S(1)}, bf16[512,512]{1,0:T(8,128)(2,1)S(1)}, bf16[2,512,256]{2,1,0:T(8,128)(2,1)S(1)}, bf16[2,512,256]{2,1,0:T(8...) custom-call(f32[256,256]{1,0:T(8,128)S(1)} %add.15.refs_0_.refs_1_, ...), custom_call_target="tpu_custom_call" | custom-call | tf_op jit(solution)/shard_map/pallas_call | solution.py:109
  38.6 2.9 %shard_map.84 = (f32[512,256]{1,0:T(8,128)S(1)}, f32[512,256]{1,0:T(8,128)S(1)}) custom-call(f32[512,256]{1,0:T(8,128)S(1)} %get-tuple-element.92.refs_0_, f32[256,256]{1,0:T(8,128)S(1)} %add.15.refs_0_.refs_1_, f32[256,256]{1,0:T(8,128)S(1)} %pad_maximum_fusion.refs_2_, f32[4,512,1024]{2,1,0:T(8,128)} %refs_7_.3, ...), custom_call_target="tpu_custom_call" | custom-call | tf_op jit(solution)/shard_map/pallas_call | solution.py:109
  42.1 1.1 %collective-permute-done.14.refs_3_.refs_4_ = f32[256,256]{1,0:T(8,128)S(1)} collective-permute-done((f32[256,256]{1,0:T(8,128)S(1)}, f32[256,256]{1,0:T(8,128)S(1)}, u32[]{:S(2)}, u32[]{:S(2)}) %collective-permute-start.14) | collective-permute-done | bytes 262176 | tf_op jit(solution)/shard_map/ppermute | solution.py:23
  43.9 1.1 %collective-permute-done.15 = f32[256,256]{1,0:T(8,128)S(1)} collective-permute-done((f32[256,256]{1,0:T(8,128)S(1)}, f32[256,256]{1,0:T(8,128)S(1)}, u32[]{:S(2)}, u32[]{:S(2)}) %collective-permute-start.15) | collective-permute-done | bytes 262176 | tf_op jit(solution)/shard_map/ppermute | solution.py:23
  45.1 1.1 %collective-permute-start.16 = (f32[256,256]{1,0:T(8,128)S(1)}, f32[256,256]{1,0:T(8,128)S(1)}, u32[]{:S(2)}, u32[]{:S(2)}) collective-permute-start(f32[256,256]{1,0:T(8,128)S(1)} %add.16.refs_0_), channel_id=1, source_target_pairs={{0,2},{1,3},{2,0},{3,1},{4,6},{5,7},{6,4},{7,5},{8,10},{9,11},{10,... | collective-permute-start | bytes 786440 | tf_op jit(solution)/shard_map/ppermute | solution.py:23
  46.2 3.8 %shard_map.88 = (bf16[512,512]{1,0:T(8,128)(2,1)S(1)}, bf16[512,512]{1,0:T(8,128)(2,1)S(1)}, bf16[2,512,256]{2,1,0:T(8,128)(2,1)S(1)}, bf16[2,512,256]{2,1,0:T(8...) custom-call(f32[256,256]{1,0:T(8,128)S(1)} %add.16.refs_0_, ...), custom_call_target="tpu_custom_call" | custom-call | tf_op jit(solution)/shard_map/pallas_call | solution.py:109
  50.1 3.4 %collective-permute-done.16 = f32[256,256]{1,0:T(8,128)S(1)} collective-permute-done((f32[256,256]{1,0:T(8,128)S(1)}, f32[256,256]{1,0:T(8,128)S(1)}, u32[]{:S(2)}, u32[]{:S(2)}) %collective-permute-start.16) | collective-permute-done | bytes 262176 | tf_op jit(solution)/shard_map/ppermute | solution.py:23
  53.5 1.6 %collective-permute-start.19 = (f32[256,256]{1,0:T(8,128)S(1)}, f32[256,256]{1,0:T(8,128)S(1)}, u32[]{:S(2)}, u32[]{:S(2)}) collective-permute-start(f32[256,256]{1,0:T(8,128)S(1)} %add.17.refs_5_), channel_id=1, source_target_pairs={{0,4},{1,5},{2,6},{3,7},{4,0},{5,1},{6,2},{7,3},{8,12},{9,13},{10,... | collective-permute-start | bytes 786440 | tf_op jit(solution)/shard_map/ppermute | solution.py:23
  55.2 0.5 collective-permute-start.17
  55.7 0.8 collective-permute-done.18
  56.7 3.2 %shard_map.89 = (f32[512,256]{1,0:T(8,128)S(1)}, f32[256,256]{1,0:T(8,128)S(1)}, f32[256,256]{1,0:T(8,128)S(1)}) custom-call(f32[512,256]{1,0:T(8,128)S(1)} %get-tuple-element.99.refs_0_, bf16[2,512,256]{2,1,0:T(8,128)(2,1)S(1)} %get-tuple-element.100.refs_1_, bf16[2,512,256]{2,1,0:T(8,128)(2,1)S(1)} %get-tuple-element.101.refs_2_, ...), custom_call_target="tpu_custom_call" | custom-call | tf_op jit(solution)/shard_map/pallas_call | solution.py:109
  59.9 1.2 %collective-permute-done.19.refs_3_ = f32[256,256]{1,0:T(8,128)S(1)} collective-permute-done((f32[256,256]{1,0:T(8,128)S(1)}, f32[256,256]{1,0:T(8,128)S(1)}, u32[]{:S(2)}, u32[]{:S(2)}) %collective-permute-start.19) | collective-permute-done | bytes 262176 | tf_op jit(solution)/shard_map/ppermute | solution.py:23
  61.1 0.5 collective-permute-start.20
  61.6 1.0 %collective-permute-done.22.refs_3_ = f32[256,256]{1,0:T(8,128)S(1)} collective-permute-done((f32[256,256]{1,0:T(8,128)S(1)}, f32[256,256]{1,0:T(8,128)S(1)}, u32[]{:S(2)}, u32[]{:S(2)}) %collective-permute-start.22) | collective-permute-done | bytes 262176 | tf_op jit(solution)/shard_map/ppermute | solution.py:23
  63.4 1.6 %collective-permute-start.23 = (f32[256,256]{1,0:T(8,128)S(1)}, f32[256,256]{1,0:T(8,128)S(1)}, u32[]{:S(2)}, u32[]{:S(2)}) collective-permute-start(f32[256,256]{1,0:T(8,128)S(1)} %shard_map.92.refs_0_), channel_id=1, source_target_pairs={{0,4},{1,3},{2,6},{3,1},{4,0},{5,7},{6,2},{7,5},{8,12},{9,11},{10,... | collective-permute-start | bytes 786440 | tf_op jit(solution)/shard_map/ppermute | solution.py:23
  64.9 2.6 %shard_map.93 = (bf16[512,512]{1,0:T(8,128)(2,1)S(1)}, bf16[512,512]{1,0:T(8,128)(2,1)S(1)}, bf16[2,512,256]{2,1,0:T(8,128)(2,1)S(1)}, bf16[2,512,256]{2,1,0:T(8,128)(2,1)S(1)}) custom-call(f32[256,256]{1,0:T(8,128)S(1)} %shard_map.92.refs_0_, f32[4,512,512]{2,1,0:T(8,128)} %refs_1_.13, f32[4,512,1024]{2,1,0:T(8,128)} %refs_7_.3), custom_call_target="tpu_custom_call" | custom-call | tf_op jit(solution)/shard_map/pallas_call | solution.py:109
  67.5 2.3 %collective-permute-done.23 = f32[256,256]{1,0:T(8,128)S(1)} collective-permute-done((f32[256,256]{1,0:T(8,128)S(1)}, f32[256,256]{1,0:T(8,128)S(1)}, u32[]{:S(2)}, u32[]{:S(2)}) %collective-permute-start.23) | collective-permute-done | bytes 262176 | tf_op jit(solution)/shard_map/ppermute | solution.py:23
  69.8 1.1 %collective-permute-start.24 = (f32[256,256]{1,0:T(8,128)S(1)}, f32[256,256]{1,0:T(8,128)S(1)}, u32[]{:S(2)}, u32[]{:S(2)}) collective-permute-start(f32[256,256]{1,0:T(8,128)S(1)} %add.18), channel_id=1, source_target_pairs={{0,2},{1,5},{2,0},{3,7},{4,6},{5,1},{6,4},{7,3},{8,10},{9,13},{10,... | collective-permute-start | bytes 786440 | tf_op jit(solution)/shard_map/ppermute | solution.py:23
  71.0 5.3 %collective-permute-done.24 = f32[256,256]{1,0:T(8,128)S(1)} collective-permute-done((f32[256,256]{1,0:T(8,128)S(1)}, f32[256,256]{1,0:T(8,128)S(1)}, u32[]{:S(2)}, u32[]{:S(2)}) %collective-permute-start.24) | collective-permute-done | bytes 262176 | tf_op jit(solution)/shard_map/ppermute | solution.py:23
  76.3 2.0 %collective-permute-start.27 = (f32[256,256]{1,0:T(8,128)S(1)}, f32[256,256]{1,0:T(8,128)S(1)}, u32[]{:S(2)}, u32[]{:S(2)}) collective-permute-start(f32[256,256]{1,0:T(8,128)S(1)} %add.19.refs_5_), channel_id=1, source_target_pairs={{0,8},{1,9},{2,10},{3,11},{4,12},{5,13},{6,14},{7,15},{8,0},{9,1},... | collective-permute-start | bytes 786440 | tf_op jit(solution)/shard_map/ppermute | solution.py:23
  79.0 0.8 collective-permute-done.26
  80.0 2.5 %shard_map.94.refs_0_ = f32[512,256]{1,0:T(8,128)S(1)} custom-call(f32[512,256]{1,0:T(8,128)S(1)} %get-tuple-element.115.refs_0_, bf16[2,512,256]{2,1,0:T(8,128)(2,1)S(1)} %get-tuple-element.108.refs_1_, bf16[2,512,256]{2,1,0:T(8,128)(2,1)S(1)} %get-tuple-element.109.refs_2_, f32[256,256]{1,0:T(8,128)S(1)} %collective-permute-done.19.refs_3_, ...), custom_call_target="tpu_custom_call" | custom-call | tf_op jit(solution)/shard_map/pallas_call | solution.py:109
  82.5 0.8 collective-permute-done.27.refs_3_
  83.6 1.1 %collective-permute-done.28.refs_3_ = f32[256,256]{1,0:T(8,128)S(1)} collective-permute-done((f32[256,256]{1,0:T(8,128)S(1)}, f32[256,256]{1,0:T(8,128)S(1)}, u32[]{:S(2)}, u32[]{:S(2)}) %collective-permute-start.28) | collective-permute-done | bytes 262176 | tf_op jit(solution)/shard_map/ppermute | solution.py:23
  84.8 1.2 %shard_map.96 = f32[512,256]{1,0:T(8,128)} custom-call(f32[512,256]{1,0:T(8,128)S(1)} %shard_map.95.refs_0_, bf16[2,512,256]{2,1,0:T(8,128)(2,1)S(1)} %get-tuple-element.125.refs_1_, bf16[2,512,256]{2,1,0:T(8,128)(2,1)S(1)} %get-tuple-element.126.refs_2_, f32[256,256]{1,0:T(8,128)S(1)} %collective-permute-done.28.refs_3_), custom_call_target="tpu_custom_call" | custom-call | tf_op jit(solution)/shard_map/pallas_call | solution.py:109
  (55 shorter events, 4.9 us)
Async XLA Ops:
  0.0 1.0 %copy-start.1 = (f32[512,256]{1,0:T(8,128)S(1)}, f32[512,256]{1,0:T(8,128)}, u32[]{:S(2)}) copy-start(f32[512,256]{1,0:T(8,128)} %refs_1_.8) | copy-start | bytes 1572868
  1.0 0.7 copy-start.2
  1.8 10.3 %collective-permute-start.2 = (f32[264,256]{1,0:T(8,128)S(1)}, f32[264,256]{1,0:T(8,128)S(1)}, u32[]{:S(2)}, u32[]{:S(2)}) collective-permute-start(f32[264,256]{1,0:T(8,128)S(1)} %get-tuple-element.71.refs_2_), channel_id=1, source_target_pairs={{0,2},{1,3},{2,0},{3,1},{4,6},{5,7},{6,4},{7,5},{8,10},{9,11},{10,... | collective-permute-start | bytes 811016 | tf_op jit(solution)/shard_map/ppermute | solution.py:23
  4.9 11.2 %collective-permute-start.5 = (f32[264,256]{1,0:T(8,128)S(1)}, f32[264,256]{1,0:T(8,128)S(1)}, u32[]{:S(2)}, u32[]{:S(2)}) collective-permute-start(f32[264,256]{1,0:T(8,128)S(1)} %shard_map.74.refs_3_), channel_id=1, source_target_pairs={{2,6},{3,7},{4,0},{5,1},{6,10},{7,11},{8,4},{9,5},{10,14},{11,15},... | collective-permute-start | bytes 811016 | tf_op jit(solution)/shard_map/ppermute | solution.py:23
  6.2 14.1 %collective-permute-start.3 = (f32[264,256]{1,0:T(8,128)S(1)}, f32[264,256]{1,0:T(8,128)S(1)}, u32[]{:S(2)}, u32[]{:S(2)}) collective-permute-start(f32[264,256]{1,0:T(8,128)S(1)} %shard_map.74.refs_3_), channel_id=1, source_target_pairs={{0,2},{1,3},{2,0},{3,1},{4,6},{5,7},{6,4},{7,5},{8,10},{9,11},{10,... | collective-permute-start | bytes 811016 | tf_op jit(solution)/shard_map/ppermute | solution.py:23
  8.9 0.7 copy-start.3
  11.3 9.0 %collective-permute-start = (f32[264,256]{1,0:T(8,128)S(1)}, f32[264,256]{1,0:T(8,128)S(1)}, u32[]{:S(2)}, u32[]{:S(2)}) collective-permute-start(f32[264,256]{1,0:T(8,128)S(1)} %get-tuple-element.71.refs_2_), channel_id=1, source_target_pairs={{0,1},{1,0},{2,3},{3,2},{4,5},{5,4},{6,7},{7,6},{8,9},{9,8},{10,11... | collective-permute-start | bytes 811016 | tf_op jit(solution)/shard_map/ppermute | solution.py:23
  11.4 8.9 %collective-permute-start.1 = (f32[264,256]{1,0:T(8,128)S(1)}, f32[264,256]{1,0:T(8,128)S(1)}, u32[]{:S(2)}, u32[]{:S(2)}) collective-permute-start(f32[264,256]{1,0:T(8,128)S(1)} %shard_map.74.refs_3_), channel_id=1, source_target_pairs={{0,1},{1,0},{2,3},{3,2},{4,5},{5,4},{6,7},{7,6},{8,9},{9,8},{10,11... | collective-permute-start | bytes 811016 | tf_op jit(solution)/shard_map/ppermute | solution.py:23
  12.1 9.9 %collective-permute-start.4 = (f32[264,256]{1,0:T(8,128)S(1)}, f32[264,256]{1,0:T(8,128)S(1)}, u32[]{:S(2)}, u32[]{:S(2)}) collective-permute-start(f32[264,256]{1,0:T(8,128)S(1)} %collective-permute-done.2.refs_5_), channel_id=1, source_target_pairs={{0,4},{1,5},{4,8},{5,9},{6,2},{7,3},{8,12},{9,13},{10,6},{11,7},{1... | collective-permute-start | bytes 811016 | tf_op jit(solution)/shard_map/ppermute | solution.py:23
  16.1 7.4 %collective-permute-start.6 = (f32[264,256]{1,0:T(8,128)S(1)}, f32[264,256]{1,0:T(8,128)S(1)}, u32[]{:S(2)}, u32[]{:S(2)}) collective-permute-start(f32[264,256]{1,0:T(8,128)S(1)} %collective-permute-done.5), channel_id=1, source_target_pairs={{0,2},{1,3},{2,0},{3,1},{4,6},{5,7},{6,4},{7,5},{8,10},{9,11},{10,... | collective-permute-start | bytes 811016 | tf_op jit(solution)/shard_map/ppermute | solution.py:23
  20.3 7.6 %copy-start = (bf16[512,1024]{1,0:T(8,128)(2,1)S(1)}, bf16[512,1024]{1,0:T(8,128)(2,1)}, u32[]{:S(2)}) copy-start(bf16[512,1024]{1,0:T(8,128)(2,1)} %get-tuple-element.80.refs_6_.refs_4_) | copy-start | bytes 3145732
  23.6 1.6 %collective-permute-start.7 = (f32[264,256]{1,0:T(8,128)S(1)}, f32[264,256]{1,0:T(8,128)S(1)}, u32[]{:S(2)}, u32[]{:S(2)}) collective-permute-start(f32[264,256]{1,0:T(8,128)S(1)} %broadcast_select_fusion.1), channel_id=1, source_target_pairs={{0,1},{1,0},{2,3},{3,2},{4,5},{5,4},{6,7},{7,6},{8,9},{9,8},{10,11... | collective-permute-start | bytes 811016 | tf_op jit(solution)/shard_map/ppermute | solution.py:23
  23.7 2.7 %collective-permute-start.8 = (f32[264,256]{1,0:T(8,128)S(1)}, f32[264,256]{1,0:T(8,128)S(1)}, u32[]{:S(2)}, u32[]{:S(2)}) collective-permute-start(f32[264,256]{1,0:T(8,128)S(1)} %broadcast_select_fusion), channel_id=1, source_target_pairs={{0,1},{1,0},{2,3},{3,2},{4,5},{5,4},{6,7},{7,6},{8,9},{9,8},{10,11... | collective-permute-start | bytes 811016 | tf_op jit(solution)/shard_map/ppermute | solution.py:23
  27.7 2.0 %collective-permute-start.9 = (f32[512,256]{1,0:T(8,128)S(1)}, f32[512,256]{1,0:T(8,128)S(1)}, u32[]{:S(2)}, u32[]{:S(2)}) collective-permute-start(f32[512,256]{1,0:T(8,128)S(1)} %get-tuple-element.88.refs_2_), channel_id=1, source_target_pairs={{0,1},{1,0},{2,3},{3,2},{4,5},{5,4},{6,7},{7,6},{8,9},{9,8},{10,11... | collective-permute-start | bytes 1572872 | tf_op jit(solution)/shard_map/ppermute | solution.py:23
  31.4 1.6 %collective-permute-start.10 = (f32[256,256]{1,0:T(8,128)S(1)}, f32[256,256]{1,0:T(8,128)S(1)}, u32[]{:S(2)}, u32[]{:S(2)}) collective-permute-start(f32[256,256]{1,0:T(8,128)S(1)} %get-tuple-element.94), channel_id=1, source_target_pairs={{0,1},{1,0},{2,3},{3,2},{4,5},{5,4},{6,7},{7,6},{8,9},{9,8},{10,11... | collective-permute-start | bytes 786440 | tf_op jit(solution)/shard_map/ppermute | solution.py:23
  33.0 8.5 %collective-permute-start.13 = (f32[256,256]{1,0:T(8,128)S(1)}, f32[256,256]{1,0:T(8,128)S(1)}, u32[]{:S(2)}, u32[]{:S(2)}) collective-permute-start(f32[256,256]{1,0:T(8,128)S(1)} %add.15.refs_0_.refs_1_), channel_id=1, source_target_pairs={{0,2},{1,3},{2,0},{3,1},{4,6},{5,7},{6,4},{7,5},{8,10},{9,11},{10,... | collective-permute-start | bytes 786440 | tf_op jit(solution)/shard_map/ppermute | solution.py:23
  34.3 4.2 %collective-permute-start.12 = (f32[128,256]{1,0:T(8,128)S(1)}, f32[128,256]{1,0:T(8,128)S(1)}, u32[]{:S(2)}, u32[]{:S(2)}) collective-permute-start(f32[128,256]{1,0:T(8,128)S(1)} %get-tuple-element.134), channel_id=1, source_target_pairs={{0,1},{1,0},{2,3},{3,2},{4,5},{5,4},{6,7},{7,6},{8,9},{9,8},{10,11... | collective-permute-start | bytes 393224 | tf_op jit(solution)/shard_map/ppermute | solution.py:23
  34.4 4.2 %collective-permute-start.11 = (f32[128,256]{1,0:T(8,128)S(1)}, f32[128,256]{1,0:T(8,128)S(1)}, u32[]{:S(2)}, u32[]{:S(2)}) collective-permute-start(f32[128,256]{1,0:T(8,128)S(1)} %get-tuple-element.133), channel_id=1, source_target_pairs={{0,1},{1,0},{2,3},{3,2},{4,5},{5,4},{6,7},{7,6},{8,9},{9,8},{10,11... | collective-permute-start | bytes 393224 | tf_op jit(solution)/shard_map/ppermute | solution.py:23
  41.5 1.6 %collective-permute-start.14 = (f32[256,256]{1,0:T(8,128)S(1)}, f32[256,256]{1,0:T(8,128)S(1)}, u32[]{:S(2)}, u32[]{:S(2)}) collective-permute-start(f32[256,256]{1,0:T(8,128)S(1)} %collective-permute-done.13.refs_3_), channel_id=1, source_target_pairs={{0,1},{1,0},{2,3},{3,2},{4,5},{5,4},{6,7},{7,6},{8,9},{9,8},{10,11... | collective-permute-start | bytes 786440 | tf_op jit(solution)/shard_map/ppermute | solution.py:23
  43.4 1.6 %collective-permute-start.15 = (f32[256,256]{1,0:T(8,128)S(1)}, f32[256,256]{1,0:T(8,128)S(1)}, u32[]{:S(2)}, u32[]{:S(2)}) collective-permute-start(f32[256,256]{1,0:T(8,128)S(1)} %shard_map.87), channel_id=1, source_target_pairs={{0,1},{1,0},{2,3},{3,2},{4,5},{5,4},{6,7},{7,6},{8,9},{9,8},{10,11... | collective-permute-start | bytes 786440 | tf_op jit(solution)/shard_map/ppermute | solution.py:23
  45.1 8.4 %collective-permute-start.16 = (f32[256,256]{1,0:T(8,128)S(1)}, f32[256,256]{1,0:T(8,128)S(1)}, u32[]{:S(2)}, u32[]{:S(2)}) collective-permute-start(f32[256,256]{1,0:T(8,128)S(1)} %add.16.refs_0_), channel_id=1, source_target_pairs={{0,2},{1,3},{2,0},{3,1},{4,6},{5,7},{6,4},{7,5},{8,10},{9,11},{10,... | collective-permute-start | bytes 786440 | tf_op jit(solution)/shard_map/ppermute | solution.py:23
  50.0 11.6 %collective-permute-start.21 = (f32[256,512]{1,0:T(8,128)S(1)}, f32[256,512]{1,0:T(8,128)S(1)}, u32[]{:S(2)}, u32[]{:S(2)}) collective-permute-start(f32[256,512]{1,0:T(8,128)S(1)} %get-tuple-element.113), channel_id=1, source_target_pairs={{0,1},{1,0},{2,3},{3,2},{4,5},{5,4},{6,7},{7,6},{8,9},{9,8},{10,11... | collective-permute-start | bytes 1572872 | tf_op jit(solution)/shard_map/ppermute | solution.py:23
  53.5 7.6 %collective-permute-start.19 = (f32[256,256]{1,0:T(8,128)S(1)}, f32[256,256]{1,0:T(8,128)S(1)}, u32[]{:S(2)}, u32[]{:S(2)}) collective-permute-start(f32[256,256]{1,0:T(8,128)S(1)} %add.17.refs_5_), channel_id=1, source_target_pairs={{0,4},{1,5},{2,6},{3,7},{4,0},{5,1},{6,2},{7,3},{8,12},{9,13},{10,... | collective-permute-start | bytes 786440 | tf_op jit(solution)/shard_map/ppermute | solution.py:23
  55.1 1.4 %collective-permute-start.18 = (f32[128,256]{1,0:T(8,128)S(1)}, f32[128,256]{1,0:T(8,128)S(1)}, u32[]{:S(2)}, u32[]{:S(2)}) collective-permute-start(f32[128,256]{1,0:T(8,128)S(1)} %get-tuple-element.132), channel_id=1, source_target_pairs={{0,1},{1,0},{2,3},{3,2},{4,5},{5,4},{6,7},{7,6},{8,9},{9,8},{10,11... | collective-permute-start | bytes 393224 | tf_op jit(solution)/shard_map/ppermute | solution.py:23
  55.2 1.5 %collective-permute-start.17 = (f32[128,256]{1,0:T(8,128)S(1)}, f32[128,256]{1,0:T(8,128)S(1)}, u32[]{:S(2)}, u32[]{:S(2)}) collective-permute-start(f32[128,256]{1,0:T(8,128)S(1)} %get-tuple-element.131), channel_id=1, source_target_pairs={{0,1},{1,0},{2,3},{3,2},{4,5},{5,4},{6,7},{7,6},{8,9},{9,8},{10,11... | collective-permute-start | bytes 393224 | tf_op jit(solution)/shard_map/ppermute | solution.py:23
  61.1 1.5 %collective-permute-start.22 = (f32[256,256]{1,0:T(8,128)S(1)}, f32[256,256]{1,0:T(8,128)S(1)}, u32[]{:S(2)}, u32[]{:S(2)}) collective-permute-start(f32[256,256]{1,0:T(8,128)S(1)} %get-tuple-element.119), channel_id=1, source_target_pairs={{0,1},{1,0},{2,3},{3,2},{4,5},{5,4},{6,7},{7,6},{8,9},{9,8},{10,11... | collective-permute-start | bytes 786440 | tf_op jit(solution)/shard_map/ppermute | solution.py:23
  61.1 2.0 %collective-permute-start.20 = (f32[256,256]{1,0:T(8,128)S(1)}, f32[256,256]{1,0:T(8,128)S(1)}, u32[]{:S(2)}, u32[]{:S(2)}) collective-permute-start(f32[256,256]{1,0:T(8,128)S(1)} %collective-permute-done.19.refs_3_), channel_id=1, source_target_pairs={{0,1},{1,0},{2,3},{3,2},{4,5},{5,4},{6,7},{7,6},{8,9},{9,8},{10,11... | collective-permute-start | bytes 786440 | tf_op jit(solution)/shard_map/ppermute | solution.py:23
  63.4 6.4 %collective-permute-start.23 = (f32[256,256]{1,0:T(8,128)S(1)}, f32[256,256]{1,0:T(8,128)S(1)}, u32[]{:S(2)}, u32[]{:S(2)}) collective-permute-start(f32[256,256]{1,0:T(8,128)S(1)} %shard_map.92.refs_0_), channel_id=1, source_target_pairs={{0,4},{1,3},{2,6},{3,1},{4,0},{5,7},{6,2},{7,5},{8,12},{9,11},{10,... | collective-permute-start | bytes 786440 | tf_op jit(solution)/shard_map/ppermute | solution.py:23
  69.8 6.4 %collective-permute-start.24 = (f32[256,256]{1,0:T(8,128)S(1)}, f32[256,256]{1,0:T(8,128)S(1)}, u32[]{:S(2)}, u32[]{:S(2)}) collective-permute-start(f32[256,256]{1,0:T(8,128)S(1)} %add.18), channel_id=1, source_target_pairs={{0,2},{1,5},{2,0},{3,7},{4,6},{5,1},{6,4},{7,3},{8,10},{9,13},{10,... | collective-permute-start | bytes 786440 | tf_op jit(solution)/shard_map/ppermute | solution.py:23
  76.3 6.9 %collective-permute-start.27 = (f32[256,256]{1,0:T(8,128)S(1)}, f32[256,256]{1,0:T(8,128)S(1)}, u32[]{:S(2)}, u32[]{:S(2)}) collective-permute-start(f32[256,256]{1,0:T(8,128)S(1)} %add.19.refs_5_), channel_id=1, source_target_pairs={{0,8},{1,9},{2,10},{3,11},{4,12},{5,13},{6,14},{7,15},{8,0},{9,1},... | collective-permute-start | bytes 786440 | tf_op jit(solution)/shard_map/ppermute | solution.py:23
  78.4 1.4 %collective-permute-start.26 = (f32[128,256]{1,0:T(8,128)S(1)}, f32[128,256]{1,0:T(8,128)S(1)}, u32[]{:S(2)}, u32[]{:S(2)}) collective-permute-start(f32[128,256]{1,0:T(8,128)S(1)} %get-tuple-element.130), channel_id=1, source_target_pairs={{0,1},{1,0},{2,3},{3,2},{4,5},{5,4},{6,7},{7,6},{8,9},{9,8},{10,11... | collective-permute-start | bytes 393224 | tf_op jit(solution)/shard_map/ppermute | solution.py:23
  78.5 1.5 %collective-permute-start.25 = (f32[128,256]{1,0:T(8,128)S(1)}, f32[128,256]{1,0:T(8,128)S(1)}, u32[]{:S(2)}, u32[]{:S(2)}) collective-permute-start(f32[128,256]{1,0:T(8,128)S(1)} %get-tuple-element.129), channel_id=1, source_target_pairs={{0,1},{1,0},{2,3},{3,2},{4,5},{5,4},{6,7},{7,6},{8,9},{9,8},{10,11... | collective-permute-start | bytes 393224 | tf_op jit(solution)/shard_map/ppermute | solution.py:23
  83.3 1.5 %collective-permute-start.28 = (f32[256,256]{1,0:T(8,128)S(1)}, f32[256,256]{1,0:T(8,128)S(1)}, u32[]{:S(2)}, u32[]{:S(2)}) collective-permute-start(f32[256,256]{1,0:T(8,128)S(1)} %collective-permute-done.27.refs_3_), channel_id=1, source_target_pairs={{0,1},{1,0},{2,3},{3,2},{4,5},{5,4},{6,7},{7,6},{8,9},{9,8},{10,11... | collective-permute-start | bytes 786440 | tf_op jit(solution)/shard_map/ppermute | solution.py:23

commit v5 on v4

--- a/solution.py
+++ b/solution.py
@@ -15,6 +15,7 @@
 F32, BF16 = jnp.float32, jnp.bfloat16
 VMEM, WINDOW_VMEM = 24 * 2**20, 48 * 2**20
 ALL = slice(None)
+PIECES = {1: 1, 2: 1, 3: 2}
 
 
 def permute(x, target):
@@ -58,6 +59,14 @@
 def put(refs, index, values):
     for ref, value in zip(refs, values):
         ref[index] = value
+
+
+def joined_rows(refs):
+    return jnp.concatenate([ref[...] for ref in refs]) if len(refs) > 1 else refs[0][...]
+
+
+def cut(x, count):
+    return jnp.split(x, count)
 
 
 def two_parts(*shape):
@@ -118,14 +127,9 @@
     )(*arrays)
 
 
-def pack_body(k, coords, weights, message, points=None):
+def pack_body(k, points, weights, message):
     rows = message.shape[0] - PAD
-    where = coords()
-    message[rows : rows + PAD, :] = jnp.zeros((PAD, message.shape[1]), F32)
-    message[rows : rows + 3, :] = where[:, k * rows : (k + 1) * rows]
-    if points is not None:
-        points[...] = jnp.zeros(points.shape, F32)
-        points[0:3, :] = where
+    message[rows : rows + PAD, :] = points[:, k * rows : (k + 1) * rows]
     message[0:rows, :] = weights()
 
 
@@ -174,8 +178,9 @@
     out[...] = acc
 
 
-def start_body(total, points, flags, message, start_high, start_low, near_high, near_low, skeleton):
-    k = KINDS.index("crossed")
+def start_body(total, points, flags, *refs):
+    start_high, start_low, near_high, near_low, skeleton = refs[-5:]
+    k, message = KINDS.index("crossed"), joined_rows(refs[:-5])
     near = split(0.5 * (total[...] + tile(points, message, flags[k : k + 1, :])))
     skeleton[...] = product(parts((start_high, start_low)), near)
     put((near_high, near_low), ..., near)
@@ -222,6 +227,9 @@
     refs = refs[3:]
     if ahead:
         up, refs = refs[0], refs[1:]
+    if level > 1:
+        own, refs = refs[0], refs[1:]
+        put(refs[-2:], ..., split(own()))
     down_parts = split(down())
     put(refs[0:2], ..., down_parts)
     step = split(product(down_parts, split(coupling())) * scale_of(level))
@@ -250,6 +258,8 @@
     if ahead:
         outs = outs + two_parts(rank, points)
         outs = outs + ([((half, rank), F32)] * 2 if split_rows else two_parts(2, rank, half))
+    owns = [Window(coupling, (level, ALL, slice(0, rank)), (rank, rank))] * (level > 1)
+    outs = outs + two_parts(rank, rank) * len(owns)
     got = call(
         functools.partial(fold_body, level, ahead, split_rows),
         outs,
@@ -257,96 +267,159 @@
         Window(down_basis, (level,), (points, rank)),
         Window(coupling, (level, ALL, slice(rank, 2 * rank)), (rank, rank)),
         *ups,
-    )
-    return got[0:2], got[2:4], got[4:6], got[6:8]
-
-
-def settle_body(level, count, ahead, split_rows, *refs):
+        *owns,
+    )
+    owned = got[-2:] if owns else ()
+    got = got[:-2] if owns else got
+    return got[0:2], got[2:4], got[4:6], got[6:8], owned
+
+
+def complete_body(count, iterate, factor_high, factor_low, *refs):
+    core = lax.axis_index("leaf") & 1
+    value = iterate[...]
+    for k, at in enumerate((core, 1 - core)):
+        theirs = joined_rows(refs[k * count : (k + 1) * count])
+        value = value - product(parts((factor_high, factor_low), at), split(theirs))
+    refs[-1][...] = value
+
+
+def complete(iterate, factor, theirs):
+    pieces = [piece for half_of in theirs for piece in half_of]
+    return call(
+        functools.partial(complete_body, len(theirs[0])), [(iterate.shape, F32)], iterate, *factor, *pieces
+    )[0]
+
+
+def settle_body(level, counts, ahead, split_rows, *refs):
     base_iterate, refs = refs[0], refs[1:]
-    if count:
-        old, theirs, refs = refs[0:2], refs[2 : 2 + count], refs[2 + count :]
-    mine, other, coupling, down_high, down_low = refs[0:5]
     core = lax.axis_index("leaf") & 1
-    half = mine.shape[0]
     value = base_iterate[...]
-    for k in range(count):
-        at = core if k == 0 else 1 - core
-        value = value - product(parts(old, at), split(theirs[k][...]))
-    low = jnp.where(core == 0, mine[...], other[...])
-    high = jnp.where(core == 0, other[...], mine[...])
-    middle = product(split(coupling()), split(jnp.concatenate([low, high])))
+    if counts[0]:
+        old, refs = refs[0:2], refs[2:]
+        for at in (core, 1 - core):
+            theirs, refs = refs[: counts[0]], refs[counts[0] :]
+            value = value - product(parts(old, at), split(joined_rows(theirs)))
+    mine, refs = joined_rows(refs[: counts[1]]), refs[counts[1] :]
+    other, refs = joined_rows(refs[: counts[2]]), refs[counts[2] :]
+    if level > 1:
+        own, refs = parts(refs[0:2]), refs[1:]
+    else:
+        own = split(refs[0]())
+    down_high, down_low = refs[1:3]
+    low = jnp.where(core == 0, mine, other)
+    high = jnp.where(core == 0, other, mine)
+    middle = product(own, split(jnp.concatenate([low, high])))
     value = value - product(parts((down_high, down_low)), split(middle * scale_of(level)))
     if ahead:
-        up_high, up_low, iterate = refs[5:8]
+        up_high, up_low, iterate = refs[3:6]
         base = product(parts((up_high, up_low)), split(value))
         if split_rows:
-            halves_by_core(base, refs[8], refs[9])
+            halves_by_core(base, refs[6], refs[7])
         else:
-            refs[8][...] = base
+            refs[6][...] = base
     else:
-        iterate = refs[5]
+        iterate = refs[3]
     iterate[...] = value
 
 
-def settle(level, iterate, old, theirs, mine, other, coupling, downs, ups, split_rows):
+def settle(level, iterate, old, theirs, mine, other, coupling, owned, downs, ups, split_rows):
     points, columns = iterate.shape
-    half, rank = mine.shape[0], coupling.shape[2] // 2
+    rank = coupling.shape[2] // 2
+    half = rank // 2
     ahead = len(ups) > 0
     outs = [((points, columns), F32)]
     if ahead:
         outs = outs + ([((half, columns), F32)] * 2 if split_rows else [((rank, columns), F32)])
+    counts = len(theirs[0]) if theirs else 0, len(mine), len(other)
     return call(
-        functools.partial(settle_body, level, len(theirs), ahead, split_rows),
+        functools.partial(settle_body, level, counts, ahead, split_rows),
         outs,
         iterate,
         *old,
-        *theirs,
-        mine,
-        other,
-        Window(coupling, (level, ALL, slice(0, rank)), (rank, rank)),
+        *[piece for half_of in theirs for piece in half_of],
+        *mine,
+        *other,
+        *(owned or [Window(coupling, (level, ALL, slice(0, rank)), (rank, rank))]),
         *downs,
         *ups,
     )
 
 
-def join_body(jump_mine, jump_sent, base_mine, base_sent, jump_high, jump_low, base):
-    half = base.shape[0]
+def join_body(mine, sent, high, low):
+    half = mine.shape[0]
     for k in range(2):
         at = ALL, slice(k * half, (k + 1) * half)
-        put((jump_high, jump_low), k, split(jump_mine[at] + jump_sent[at]))
-    base[...] = base_mine[...] + base_sent[...]
-
-
-def join(jump, base):
-    half, rank = jump[0].shape
-    columns = base[0].shape[1]
-    return call(
-        join_body, two_parts(2, half, half) + [((half, columns), F32)], *jump, *base
-    )
-
-
-def sub_body(side, base, factor_high, factor_low, value, out):
+        put((high, low), k, split(mine[at] + sent[at]))
+
+
+def join(mine, sent):
+    half, rank = mine.shape
+    return call(join_body, two_parts(2, half, half), mine, sent)
+
+
+def add_sub_body(base, sent, factor_high, factor_low, *refs):
+    at = 1 - (lax.axis_index("leaf") & 1)
+    change = product(parts((factor_high, factor_low), at), split(joined_rows(refs[:-1])))
+    refs[-1][...] = (base[...] + sent[...]) - change
+
+
+def add_sub(base, sent, factor, value):
+    return call(add_sub_body, [(base.shape, F32)], base, sent, *factor, *value)[0]
+
+
+def sub_body(side, base, factor_high, factor_low, *refs):
     core = lax.axis_index("leaf") & 1
     at = core if side == 0 else 1 - core
-    out[...] = base[...] - product(parts((factor_high, factor_low), at), split(value[...]))
-
-
-def rows_body(turn, base, factor_high, factor_low, value, out):
+    value = joined_rows(refs[:-1])
+    refs[-1][...] = base[...] - product(parts((factor_high, factor_low), at), split(value))
+
+
+def rows_body(turn, base, factor_high, factor_low, *refs):
     core = lax.axis_index("leaf") & 1
+    out = refs[-1]
     half = out.shape[0]
     rows = pl.ds(pl.multiple_of((1 - core if turn else core) * half, half), half)
     out[...] = base[rows, :] - product(
-        parts((factor_high, factor_low), (1 - core, rows)), split(value[...])
+        parts((factor_high, factor_low), (1 - core, rows)), split(joined_rows(refs[:-1]))
     )
 
 
 def rows_of(turn, base, factor, value):
     rows, columns = base.shape
-    return call(functools.partial(rows_body, turn), [((rows // 2, columns), F32)], base, *factor, value)[0]
+    return call(functools.partial(rows_body, turn), [((rows // 2, columns), F32)], base, *factor, *value)[0]
 
 
 def sub(side, base, factor, value):
-    return call(functools.partial(sub_body, side), [(base.shape, F32)], base, *factor, value)[0]
+    return call(functools.partial(sub_body, side), [(base.shape, F32)], base, *factor, *value)[0]
+
+
+def finish_body(base, factor_high, factor_low, *refs):
+    out, buffer, semaphores = refs[-3:]
+    at = 1 - (lax.axis_index("leaf") & 1)
+    value = split(joined_rows(refs[:-3]))
+    half = buffer.shape[0] // 2
+    copies = []
+    for k in range(2):
+        rows = pl.ds(k * half, half)
+        change = product(parts((factor_high, factor_low), (at, rows)), value)
+        buffer[rows, :] = base[rows, :] - change
+        copies.append(pltpu.make_async_copy(buffer.at[rows], out.at[rows], semaphores.at[k]))
+        copies[k].start()
+    for copy in copies:
+        copy.wait()
+
+
+def finish(base, factor, value):
+    args = (base, *factor, *value)
+    return pl.pallas_call(
+        finish_body,
+        in_specs=[pl.BlockSpec(memory_space=pltpu.VMEM) for _ in args],
+        out_specs=pl.BlockSpec(memory_space=pltpu.HBM),
+        out_shape=jax.ShapeDtypeStruct(base.shape, F32),
+        scratch_shapes=[pltpu.VMEM(base.shape, F32), pltpu.SemaphoreType.DMA((2,))],
+        compiler_params=pltpu.CompilerParams(vmem_limit_bytes=VMEM),
+        cost_estimate=pl.CostEstimate(flops=0, bytes_accessed=0, transcendentals=0),
+    )(*args)
 
 
 def per_device(coords, weights, near_mask, leaf_inverse, up_basis, coupling, down_basis):
@@ -357,17 +430,17 @@
     same = (me & 1) == ((me >> 1) & 1)
     bases = up_basis, coupling, down_basis
 
+    where = jnp.pad(coords, ((0, PAD - 3), (0, 0)))
+
     def pack(k):
-        outs = [((rows + PAD, columns), F32)] + [((8, points), F32)] * (k == 0)
         return call(
             functools.partial(pack_body, k),
-            outs,
-            Window(coords, (ALL, ALL), (3, points)),
+            [((rows + PAD, columns), F32)],
+            where,
             Window(weights, (slice(k * rows, (k + 1) * rows),), (rows, columns)),
         )
 
-    message, where = pack(0)
-    messages = [message, pack(1)[0]]
+    messages = [pack(k)[0] for k in range(CHUNKS)]
     across = [exchange(messages[0], 2)]
     far = permute(messages[1], lambda i: i + 4 if i & 2 else i - 4)
     across = across + [exchange(messages[1], 2)]
@@ -408,15 +481,19 @@
     crossed = [exchange(jnp.where(same, across[0], after(passed[0], total, *opening)), 1)]
     total = add(total, passed=passed[:1])
     far = after(passed[1], total)
-    crossed = crossed + [exchange(jnp.where(same, across[1], far), 1)]
-    total = add(total, passed=[far], crossed=crossed[:1])
+    near_cut = (rows + PAD) // 16 * 8
+    last = [
+        exchange(jnp.where(same, across[1][at], far[at]), 1)
+        for at in (slice(0, near_cut), slice(near_cut, rows + PAD))
+    ]
+    total = add(add(total, passed=[far]), crossed=crossed[:1])
     *near, skeleton = call(
         start_body,
         two_parts(points, columns) + [((rank, columns), F32)],
         total,
         where,
         flags,
-        crossed[1],
+        *last,
         *opening[0:2],
     )
 
@@ -443,32 +520,37 @@
 
     for level in range(1, LEVELS):
         ahead, joined = level + 1 < LEVELS, level == 2
-        downs, next_factor, ups, jump = fold(level, *bases, mine, joined)
-        pending = (*downs, *next_factor, *ups, *jump)
+        downs, next_factor, ups, jump, owned = fold(level, *bases, mine, joined)
+        pending = (*downs, *next_factor, *ups, *jump, *owned)
+        if theirs:
+            iterate = complete(after(iterate, *next_factor), factor, theirs)
+            pending, factor, theirs = (*pending, iterate), (), ()
+        mine = cut(mine, PIECES[level])
         for even, odd in {1: (), 2: ((2, 2),), 3: ((4, 2), (2, 4))}[level]:
-            got = permute(mine, lambda i: i ^ (odd if i & 1 else even))
-            mine = mine + after(got, *pending)
+            got = [permute(m, lambda i: i ^ (odd if i & 1 else even)) for m in mine]
+            mine = [m + after(g, *pending) for m, g in zip(mine, got)]
             pending = ()
-        arriving = exchange(mine, 1 << level)
-        other = jnp.concatenate([exchange(m, 1) for m in jnp.split(mine, 2)])
+        arriving = [exchange(m, 1 << level) for m in mine]
+        other = [exchange(c, 1) for m in mine for c in cut(m, 2)]
         if joined:
-            jump = jump[0], exchange(jump[1], 1)
+            jump = join(jump[0], exchange(jump[1], 1))
+            pending = tuple(jump)
         iterate, *base = settle(
-            level, iterate, factor, theirs, mine, other, coupling, downs, ups, joined
+            level, iterate, factor, theirs, mine, other, coupling, owned, downs, ups, joined
         )
         factor = next_factor
-        arriving = after(arriving, iterate, *base)
-        theirs = [arriving, exchange(arriving, 1)]
+        arriving = [after(a, iterate, *base, *pending) for a in arriving]
+        theirs = arriving, [exchange(a, 1) for a in arriving]
         if joined:
-            base_other = after(base[1], arriving)
-            *jump, base = join(jump, (base[0], exchange(base_other, 1)))
-            mine = sub(1, sub(0, base, jump, theirs[0]), jump, theirs[1])
+            base_other = after(base[1], arriving[-1])
+            sent = exchange(base_other, 1)
+            mine = add_sub(sub(0, base[0], jump, theirs[0]), sent, jump, theirs[1])
         elif ahead:
             base = sub(0, base[0], jump, theirs[0])
             mine = rows_of(0, base, jump, theirs[1]) + exchange(
                 rows_of(1, base, jump, theirs[1]), 1
             )
-    return sub(1, sub(0, iterate, factor, theirs[0]), factor, theirs[1])
+    return finish(sub(0, iterate, factor, theirs[0]), factor, theirs[1])
 
 
 def solution(mesh):

time: 86.5 us -> 85.9 us (level)
  waiting for transfers between devices: 23.5 us -> 18.8 us
  starting transfers between devices: 24.1 us -> 28 us
    ppermute x29 -> x36, waiting for transfers between devices: 23.5 us -> 18.8 us  [permute(): return lax.ppermute(x, 'leaf', [(i, j) for i, j in pairs if 0 <= j < count])]
    ppermute x29 -> x36, starting transfers between devices: 24.1 us -> 28 us  [permute(): return lax.ppermute(x, 'leaf', [(i, j) for i, j in pairs if 0 <= j < count])]
    pallas_call x0 -> x1, Pallas kernels: none -> 1.09 us  [finish(): pl.pallas_call(finish_body, in_specs=[pl.BlockSpec(memory_space=pltpu.VME...]
    pallas_call x24 -> x26, Pallas kernels: 35.2 us -> 34.4 us  [call(): pl.pallas_call(kernel, in_specs=[spec(arg) for arg in args], out_specs=[p...]
    unnamed x8 -> x6, local copies, waits for them, and re-layouts: 2.4 us -> 1.7 us
  transfers between devices with their start and end apart: 29 -> 36, of which waited for: 18 -> 21; matrix products, arithmetic and copies ran while one was open for 0% -> 0% of each run, Pallas kernels for 35% -> 36%
where the time goes in v5:
time: 85.9 us; the launch traced here: 85.6 us
  Pallas kernels  35.5 us (41%)
  starting transfers between devices  28 us (33%)
  waiting for transfers between devices  18.8 us (22%)
  local copies, waits for them, and re-layouts  2.48 us (3%)
    pallas_call x26, Pallas kernels, call(): pl.pallas_call(kernel, in_specs=[spec(arg) for arg in args], out_specs=[p...  34.4 us
    ppermute x36, starting transfers between devices, permute(): return lax.ppermute(x, 'leaf', [(i, j) for i, j in pairs if 0 <= j < count])  28 us
    ppermute x36, waiting for transfers between devices, permute(): return lax.ppermute(x, 'leaf', [(i, j) for i, j in pairs if 0 <= j < count])  18.8 us
  transfers between devices with their start and end apart: 36, of which 21 were waited for; matrix products, arithmetic and copies ran while one was open for 0% of the time, Pallas kernels for 36%

profile of v5, /device:TPU:0, one launch (start us, length us, event | category | flops | bytes accessed | tf_op | source)
XLA Modules:
  0.0 85.6 jit_solution(9295247523358643656)
XLA Ops:
  0.0 0.7 pad.4.refs_0_.refs_1_
  0.7 1.0 %copy-done.1 = f32[512,256]{1,0:T(8,128)S(1)} copy-done((f32[512,256]{1,0:T(8,128)S(1)}, f32[512,256]{1,0:T(8,128)}, u32[]{:S(2)}) %copy-start.1) | copy-done | bytes 524312
  1.8 3.0 %collective-permute-start.2 = (f32[264,256]{1,0:T(8,128)S(1)}, f32[264,256]{1,0:T(8,128)S(1)}, u32[]{:S(2)}, u32[]{:S(2)}) collective-permute-start(f32[264,256]{1,0:T(8,128)S(1)} %shard_map.73.refs_2_), channel_id=1, source_target_pairs={{0,2},{1,3},{2,0},{3,1},{4,6},{5,7},{6,4},{7,5},{8,10},{9,11},{10,... | collective-permute-start | bytes 811016 | tf_op jit(solution)/shard_map/ppermute | solution.py:24
  4.9 1.3 %collective-permute-start.5 = (f32[264,256]{1,0:T(8,128)S(1)}, f32[264,256]{1,0:T(8,128)S(1)}, u32[]{:S(2)}, u32[]{:S(2)}) collective-permute-start(f32[264,256]{1,0:T(8,128)S(1)} %shard_map.74.refs_3_), channel_id=1, source_target_pairs={{2,6},{3,7},{4,0},{5,1},{6,10},{7,11},{8,4},{9,5},{10,14},{11,15},... | collective-permute-start | bytes 811016 | tf_op jit(solution)/shard_map/ppermute | solution.py:24
  6.2 2.7 %collective-permute-start.3 = (f32[264,256]{1,0:T(8,128)S(1)}, f32[264,256]{1,0:T(8,128)S(1)}, u32[]{:S(2)}, u32[]{:S(2)}) collective-permute-start(f32[264,256]{1,0:T(8,128)S(1)} %shard_map.74.refs_3_), channel_id=1, source_target_pairs={{0,2},{1,3},{2,0},{3,1},{4,6},{5,7},{6,4},{7,5},{8,10},{9,11},{10,... | collective-permute-start | bytes 811016 | tf_op jit(solution)/shard_map/ppermute | solution.py:24
  8.9 0.7 copy-done.2
  9.6 1.7 %shard_map.75 = (f32[512,256]{1,0:T(8,128)S(1)}, f32[8,256]{1,0:T(8,128)S(1)}) custom-call(f32[8,512]{1,0:T(8,128)S(1)} %pad.4.refs_0_.refs_1_, s32[1,4]{1,0:T(1,128)S(1)} %copy-done.2, f32[264,256]{1,0:T(8,128)S(1)} %shard_map.73.refs_2_, f32[264,256]{1,0:T(8,128)S(1)} %shard_map.74.refs_3_), custom_call_target="tpu_custom_call" | custom-call | tf_op jit(solution)/shard_map/pallas_call | solution.py:118
  12.1 4.0 %collective-permute-start.4 = (f32[264,256]{1,0:T(8,128)S(1)}, f32[264,256]{1,0:T(8,128)S(1)}, u32[]{:S(2)}, u32[]{:S(2)}) collective-permute-start(f32[264,256]{1,0:T(8,128)S(1)} %collective-permute-done.2.refs_5_), channel_id=1, source_target_pairs={{0,4},{1,5},{4,8},{5,9},{6,2},{7,3},{8,12},{9,13},{10,6},{11,7},{1... | collective-permute-start | bytes 811016 | tf_op jit(solution)/shard_map/ppermute | solution.py:24
  16.2 4.1 %shard_map.79 = (bf16[512,512]{1,0:T(8,128)(2,1)S(1)}, bf16[512,512]{1,0:T(8,128)(2,1)S(1)}, bf16[512,512]{1,0:T(8,128)(2,1)S(1)}, bf16[512,512]{1,0:T(8,128)(2,...) custom-call(f32[4,512,512]{2,1,0:T(8,128)} %refs_3_.6, ...), custom_call_target="tpu_custom_call" | custom-call | tf_op jit(solution)/shard_map/pallas_call | solution.py:118
  20.3 1.7 %shard_map.76.refs_0_ = f32[512,256]{1,0:T(8,128)S(1)} custom-call(f32[512,256]{1,0:T(8,128)S(1)} %get-tuple-element.72.refs_0_, f32[8,512]{1,0:T(8,128)S(1)} %pad.4.refs_0_.refs_1_, f32[8,256]{1,0:T(8,128)S(1)} %get-tuple-element.73.refs_2_, f32[264,256]{1,0:T(8,128)S(1)} %collective-permute-done.refs_3_, f32[264,256]{1,0:T(8,128)S(1)} %collective-permute-done.1.refs_4_, ...), custom_call_target="tpu_custom_call" | custom-call | tf_op jit(solution)/shard_map/pallas_call | solution.py:118
  22.0 0.8 shard_map.77.refs_0_
  22.8 0.7 collective-permute-done.6.refs_3_
  23.7 0.6 collective-permute-start.7
  24.4 0.7 shard_map.78.refs_0_
  25.4 0.7 shard_map.80.refs_0_
  26.2 1.3 %shard_map.81 = (bf16[512,256]{1,0:T(8,128)(2,1)S(1)}, bf16[512,256]{1,0:T(8,128)(2,1)S(1)}, f32[512,256]{1,0:T(8,128)S(1)}) custom-call(f32[512,256]{1,0:T(8,128)S(1)} %shard_map.80.refs_0_, f32[8,512]{1,0:T(8,128)S(1)} %pad.4.refs_0_.refs_1_, f32[8,256]{1,0:T(8,128)S(1)} %get-tuple-element.73.refs_2_, f32[128,256]{1,0:T(8,128)S(1)} %collective-permute-done.8.refs_3_, ...), custom_call_target="tpu_custom_call" | custom-call | tf_op jit(solution)/shard_map/pallas_call | solution.py:118
  27.9 1.0 %shard_map.82 = (f32[512,256]{1,0:T(8,128)S(1)}, f32[512,256]{1,0:T(8,128)S(1)}) custom-call(bf16[512,256]{1,0:T(8,128)(2,1)S(1)} %get-tuple-element.89.refs_0_, bf16[512,256]{1,0:T(8,128)(2,1)S(1)} %get-tuple-element.90.refs_1_, f32[512,256]{1,0:T(8,128)S(1)} %get-tuple-element.91.refs_2_, bf16[512,512]{1,0:T(8,128)(2,1)S(1)} %get-tuple-element.80.refs_3_, ...), custom_call_target="tpu_custom_call" | custom-call | tf_op jit(solution)/shard_map/pallas_call | solution.py:118
  28.9 0.5 collective-permute-done.10.refs_2_
  29.5 1.7 %shard_map.83 = (f32[512,256]{1,0:T(8,128)S(1)}, f32[256,256]{1,0:T(8,128)S(1)}, f32[256,256]{1,0:T(8,128)S(1)}) custom-call(f32[512,256]{1,0:T(8,128)S(1)} %get-tuple-element.92.refs_0_, f32[512,256]{1,0:T(8,128)S(1)} %get-tuple-element.93.refs_1_, f32[512,256]{1,0:T(8,128)S(1)} %collective-permute-done.10.refs_2_, ...), custom_call_target="tpu_custom_call" | custom-call | tf_op jit(solution)/shard_map/pallas_call | solution.py:118
  31.6 1.2 %collective-permute-done.11 = f32[256,256]{1,0:T(8,128)S(1)} collective-permute-done((f32[256,256]{1,0:T(8,128)S(1)}, f32[256,256]{1,0:T(8,128)S(1)}, u32[]{:S(2)}, u32[]{:S(2)}) %collective-permute-start.11) | collective-permute-done | bytes 262176 | tf_op jit(solution)/shard_map/ppermute | solution.py:24
  32.8 1.3 %collective-permute-start.14 = (f32[256,256]{1,0:T(8,128)S(1)}, f32[256,256]{1,0:T(8,128)S(1)}, u32[]{:S(2)}, u32[]{:S(2)}) collective-permute-start(f32[256,256]{1,0:T(8,128)S(1)} %add.23.refs_0_.refs_1_), channel_id=1, source_target_pairs={{0,2},{1,3},{2,0},{3,1},{4,6},{5,7},{6,4},{7,5},{8,10},{9,11},{10,... | collective-permute-start | bytes 786440 | tf_op jit(solution)/shard_map/ppermute | solution.py:24
  34.7 3.6 %shard_map.84 = (bf16[512,512]{1,0:T(8,128)(2,1)S(1)}, bf16[512,512]{1,0:T(8,128)(2,1)S(1)}, bf16[2,512,256]{2,1,0:T(8,128)(2,1)S(1)}, bf16[2,512,256]{2,1,0:T(8...) custom-call(f32[256,256]{1,0:T(8,128)S(1)} %add.23.refs_0_.refs_1_, ...), custom_call_target="tpu_custom_call" | custom-call | tf_op jit(solution)/shard_map/pallas_call | solution.py:118
  38.4 2.9 %shard_map.85 = (f32[512,256]{1,0:T(8,128)S(1)}, f32[512,256]{1,0:T(8,128)S(1)}) custom-call(f32[512,256]{1,0:T(8,128)S(1)} %get-tuple-element.95.refs_0_, f32[256,256]{1,0:T(8,128)S(1)} %add.23.refs_0_.refs_1_, f32[128,256]{1,0:T(8,128)S(1)} %collective-permute-done.12.refs_2_, f32[128,256]{1,0:T(8,128)S(1)} %collective-permute-done.13.refs_3_, ...), custom_call_target="tpu_custom_call" | custom-call | tf_op jit(solution)/shard_map/pallas_call | solution.py:118
  41.9 1.1 %collective-permute-done.15.refs_3_.refs_4_ = f32[256,256]{1,0:T(8,128)S(1)} collective-permute-done((f32[256,256]{1,0:T(8,128)S(1)}, f32[256,256]{1,0:T(8,128)S(1)}, u32[]{:S(2)}, u32[]{:S(2)}) %collective-permute-start.15) | collective-permute-done | bytes 262176 | tf_op jit(solution)/shard_map/ppermute | solution.py:24
  43.8 1.1 %collective-permute-done.16 = f32[256,256]{1,0:T(8,128)S(1)} collective-permute-done((f32[256,256]{1,0:T(8,128)S(1)}, f32[256,256]{1,0:T(8,128)S(1)}, u32[]{:S(2)}, u32[]{:S(2)}) %collective-permute-start.16) | collective-permute-done | bytes 262176 | tf_op jit(solution)/shard_map/ppermute | solution.py:24
  44.9 1.3 %collective-permute-start.17 = (f32[256,256]{1,0:T(8,128)S(1)}, f32[256,256]{1,0:T(8,128)S(1)}, u32[]{:S(2)}, u32[]{:S(2)}) collective-permute-start(f32[256,256]{1,0:T(8,128)S(1)} %add.24.refs_0_), channel_id=1, source_target_pairs={{0,2},{1,3},{2,0},{3,1},{4,6},{5,7},{6,4},{7,5},{8,10},{9,11},{10,... | collective-permute-start | bytes 786440 | tf_op jit(solution)/shard_map/ppermute | solution.py:24
  46.2 4.8 %shard_map.89 = (bf16[512,512]{1,0:T(8,128)(2,1)S(1)}, bf16[512,512]{1,0:T(8,128)(2,1)S(1)}, bf16[2,512,256]{2,1,0:T(8,128)(2,1)S(1)}, bf16[2,512,256]{2,1,0:T(8...) custom-call(f32[256,256]{1,0:T(8,128)S(1)} %add.24.refs_0_, ...), custom_call_target="tpu_custom_call" | custom-call | tf_op jit(solution)/shard_map/pallas_call | solution.py:118
  51.1 0.6 shard_map.90.refs_0_
  51.7 1.6 %collective-permute-done.17 = f32[256,256]{1,0:T(8,128)S(1)} collective-permute-done((f32[256,256]{1,0:T(8,128)S(1)}, f32[256,256]{1,0:T(8,128)S(1)}, u32[]{:S(2)}, u32[]{:S(2)}) %collective-permute-start.17) | collective-permute-done | bytes 262176 | tf_op jit(solution)/shard_map/ppermute | solution.py:24
  53.4 1.6 %collective-permute-start.21 = (f32[256,256]{1,0:T(8,128)S(1)}, f32[256,256]{1,0:T(8,128)S(1)}, u32[]{:S(2)}, u32[]{:S(2)}) collective-permute-start(f32[256,256]{1,0:T(8,128)S(1)} %add.25.refs_1_), channel_id=1, source_target_pairs={{0,4},{1,5},{2,6},{3,7},{4,0},{5,1},{6,2},{7,3},{8,12},{9,13},{10,... | collective-permute-start | bytes 786440 | tf_op jit(solution)/shard_map/ppermute | solution.py:24
  55.5 0.8 collective-permute-done.19.refs_3_
  56.6 1.7 %shard_map.91 = (f32[512,256]{1,0:T(8,128)S(1)}, f32[256,256]{1,0:T(8,128)S(1)}, f32[256,256]{1,0:T(8,128)S(1)}) custom-call(f32[512,256]{1,0:T(8,128)S(1)} %shard_map.90.refs_0_, f32[256,256]{1,0:T(8,128)S(1)} %add.25.refs_1_, f32[128,256]{1,0:T(8,128)S(1)} %collective-permute-done.18.refs_2_, f32[128,256]{1,0:T(8,128)S(1)} %collective-permute-done.19.refs_3_, ...), custom_call_target="tpu_custom_call" | custom-call | tf_op jit(solution)/shard_map/pallas_call | solution.py:118
  58.4 2.5 %collective-permute-done.21.refs_3_ = f32[256,256]{1,0:T(8,128)S(1)} collective-permute-done((f32[256,256]{1,0:T(8,128)S(1)}, f32[256,256]{1,0:T(8,128)S(1)}, u32[]{:S(2)}, u32[]{:S(2)}) %collective-permute-start.21) | collective-permute-done | bytes 262176 | tf_op jit(solution)/shard_map/ppermute | solution.py:24
  61.7 0.7 collective-permute-done.22.refs_1_
  63.2 1.6 %collective-permute-start.26 = (f32[128,256]{1,0:T(8,128)S(1)}, f32[128,256]{1,0:T(8,128)S(1)}, u32[]{:S(2)}, u32[]{:S(2)}) collective-permute-start(f32[128,256]{1,0:T(8,128)S(1)} %get-tuple-element.141), channel_id=1, source_target_pairs={{0,4},{1,3},{2,6},{3,1},{4,0},{5,7},{6,2},{7,5},{8,12},{9,11},{10,... | collective-permute-start | bytes 393224 | tf_op jit(solution)/shard_map/ppermute | solution.py:24
  65.3 3.2 %shard_map.95 = (bf16[512,512]{1,0:T(8,128)(2,1)S(1)}, bf16[512,512]{1,0:T(8,128)(2,1)S(1)}, bf16[2,512,256]{2,1,0:T(8,128)(2,1)S(1)}, bf16[2,512,256]{2,1,0:T(8...) custom-call(f32[256,256]{1,0:T(8,128)S(1)} %shard_map.94.refs_0_, f32[4,512,512]{2,1,0:T(8,128)} %refs_1_.13, ...), custom_call_target="tpu_custom_call" | custom-call | tf_op jit(solution)/shard_map/pallas_call | solution.py:118
  68.5 0.6 shard_map.96.refs_0_
  69.1 0.7 collective-permute-done.24
  69.8 1.3 %collective-permute-start.27 = (f32[128,256]{1,0:T(8,128)S(1)}, f32[128,256]{1,0:T(8,128)S(1)}, u32[]{:S(2)}, u32[]{:S(2)}) collective-permute-start(f32[128,256]{1,0:T(8,128)S(1)} %get-tuple-element.139), channel_id=1, source_target_pairs={{0,2},{1,5},{2,0},{3,7},{4,6},{5,1},{6,4},{7,3},{8,10},{9,13},{10,... | collective-permute-start | bytes 393224 | tf_op jit(solution)/shard_map/ppermute | solution.py:24
  71.1 0.8 collective-permute-start.25
  71.8 2.9 %collective-permute-done.27 = f32[128,256]{1,0:T(8,128)S(1)} collective-permute-done((f32[128,256]{1,0:T(8,128)S(1)}, f32[128,256]{1,0:T(8,128)S(1)}, u32[]{:S(2)}, u32[]{:S(2)}) %collective-permute-start.27) | collective-permute-done | bytes 131104 | tf_op jit(solution)/shard_map/ppermute | solution.py:24
  74.8 2.1 %collective-permute-start.33 = (f32[128,256]{1,0:T(8,128)S(1)}, f32[128,256]{1,0:T(8,128)S(1)}, u32[]{:S(2)}, u32[]{:S(2)}) collective-permute-start(f32[128,256]{1,0:T(8,128)S(1)} %add.29.refs_2_), channel_id=1, source_target_pairs={{0,8},{1,9},{2,10},{3,11},{4,12},{5,13},{6,14},{7,15},{8,0},{9,1},... | collective-permute-start | bytes 393224 | tf_op jit(solution)/shard_map/ppermute | solution.py:24
  77.1 1.3 %collective-permute-start.32 = (f32[128,256]{1,0:T(8,128)S(1)}, f32[128,256]{1,0:T(8,128)S(1)}, u32[]{:S(2)}, u32[]{:S(2)}) collective-permute-start(f32[128,256]{1,0:T(8,128)S(1)} %add.27.refs_1_), channel_id=1, source_target_pairs={{0,8},{1,9},{2,10},{3,11},{4,12},{5,13},{6,14},{7,15},{8,0},{9,1},... | collective-permute-start | bytes 393224 | tf_op jit(solution)/shard_map/ppermute | solution.py:24
  79.0 0.7 collective-permute-done.30.refs_5_
  80.2 1.2 %shard_map.97.refs_0_ = f32[512,256]{1,0:T(8,128)S(1)} custom-call(f32[512,256]{1,0:T(8,128)S(1)} %shard_map.96.refs_0_, f32[128,256]{1,0:T(8,128)S(1)} %add.27.refs_1_, f32[128,256]{1,0:T(8,128)S(1)} %add.29.refs_2_, f32[64,256]{1,0:T(8,128)S(1)} %collective-permute-done.28.refs_3_, f32[64,256]{1,0:T(8,128)S(1)} %collective-permute-done.29.refs_4_, ...), custom_call_target="tpu_custom_call" | custom-call | tf_op jit(solution)/shard_map/pallas_call | solution.py:118
  81.6 1.4 %collective-permute-done.32.refs_3_ = f32[128,256]{1,0:T(8,128)S(1)} collective-permute-done((f32[128,256]{1,0:T(8,128)S(1)}, f32[128,256]{1,0:T(8,128)S(1)}, u32[]{:S(2)}, u32[]{:S(2)}) %collective-permute-start.32) | collective-permute-done | bytes 131104 | tf_op jit(solution)/shard_map/ppermute | solution.py:24
  83.4 0.9 %collective-permute-done.34.refs_0_ = f32[128,256]{1,0:T(8,128)S(1)} collective-permute-done((f32[128,256]{1,0:T(8,128)S(1)}, f32[128,256]{1,0:T(8,128)S(1)}, u32[]{:S(2)}, u32[]{:S(2)}) %collective-permute-start.34) | collective-permute-done | bytes 131104 | tf_op jit(solution)/shard_map/ppermute | solution.py:24
  84.4 1.1 %shard_map.99 = f32[512,256]{1,0:T(8,128)} custom-call(f32[512,256]{1,0:T(8,128)S(1)} %shard_map.98.base, bf16[2,512,256]{2,1,0:T(8,128)(2,1)S(1)} %get-tuple-element.128.refs_1_.factor_high, bf16[2,512,256]{2,1,0:T(8,128)(2,1)S(1)} %get-tuple-element.129.refs_2_.factor_low, f32[128,256]{1,0:T(8,128)S(1)} %collective-permute-done.34.refs_0_, ...), custom_call_target="tpu_custom_call" | custom-call | tf_op jit(solution)/shard_map/pallas_call | solution.py:414
  (72 shorter events, 9.3 us)
Async XLA Ops:
  0.7 1.0 %copy-start.1 = (f32[512,256]{1,0:T(8,128)S(1)}, f32[512,256]{1,0:T(8,128)}, u32[]{:S(2)}) copy-start(f32[512,256]{1,0:T(8,128)} %refs_1_.8) | copy-start | bytes 1572868
  1.8 10.3 %collective-permute-start.2 = (f32[264,256]{1,0:T(8,128)S(1)}, f32[264,256]{1,0:T(8,128)S(1)}, u32[]{:S(2)}, u32[]{:S(2)}) collective-permute-start(f32[264,256]{1,0:T(8,128)S(1)} %shard_map.73.refs_2_), channel_id=1, source_target_pairs={{0,2},{1,3},{2,0},{3,1},{4,6},{5,7},{6,4},{7,5},{8,10},{9,11},{10,... | collective-permute-start | bytes 811016 | tf_op jit(solution)/shard_map/ppermute | solution.py:24
  4.9 11.3 %collective-permute-start.5 = (f32[264,256]{1,0:T(8,128)S(1)}, f32[264,256]{1,0:T(8,128)S(1)}, u32[]{:S(2)}, u32[]{:S(2)}) collective-permute-start(f32[264,256]{1,0:T(8,128)S(1)} %shard_map.74.refs_3_), channel_id=1, source_target_pairs={{2,6},{3,7},{4,0},{5,1},{6,10},{7,11},{8,4},{9,5},{10,14},{11,15},... | collective-permute-start | bytes 811016 | tf_op jit(solution)/shard_map/ppermute | solution.py:24
  6.2 14.1 %collective-permute-start.3 = (f32[264,256]{1,0:T(8,128)S(1)}, f32[264,256]{1,0:T(8,128)S(1)}, u32[]{:S(2)}, u32[]{:S(2)}) collective-permute-start(f32[264,256]{1,0:T(8,128)S(1)} %shard_map.74.refs_3_), channel_id=1, source_target_pairs={{0,2},{1,3},{2,0},{3,1},{4,6},{5,7},{6,4},{7,5},{8,10},{9,11},{10,... | collective-permute-start | bytes 811016 | tf_op jit(solution)/shard_map/ppermute | solution.py:24
  8.9 0.7 copy-start.2
  11.3 9.0 %collective-permute-start = (f32[264,256]{1,0:T(8,128)S(1)}, f32[264,256]{1,0:T(8,128)S(1)}, u32[]{:S(2)}, u32[]{:S(2)}) collective-permute-start(f32[264,256]{1,0:T(8,128)S(1)} %shard_map.73.refs_2_), channel_id=1, source_target_pairs={{0,1},{1,0},{2,3},{3,2},{4,5},{5,4},{6,7},{7,6},{8,9},{9,8},{10,11... | collective-permute-start | bytes 811016 | tf_op jit(solution)/shard_map/ppermute | solution.py:24
  11.4 9.0 %collective-permute-start.1 = (f32[264,256]{1,0:T(8,128)S(1)}, f32[264,256]{1,0:T(8,128)S(1)}, u32[]{:S(2)}, u32[]{:S(2)}) collective-permute-start(f32[264,256]{1,0:T(8,128)S(1)} %shard_map.74.refs_3_), channel_id=1, source_target_pairs={{0,1},{1,0},{2,3},{3,2},{4,5},{5,4},{6,7},{7,6},{8,9},{9,8},{10,11... | collective-permute-start | bytes 811016 | tf_op jit(solution)/shard_map/ppermute | solution.py:24
  12.1 9.9 %collective-permute-start.4 = (f32[264,256]{1,0:T(8,128)S(1)}, f32[264,256]{1,0:T(8,128)S(1)}, u32[]{:S(2)}, u32[]{:S(2)}) collective-permute-start(f32[264,256]{1,0:T(8,128)S(1)} %collective-permute-done.2.refs_5_), channel_id=1, source_target_pairs={{0,4},{1,5},{4,8},{5,9},{6,2},{7,3},{8,12},{9,13},{10,6},{11,7},{1... | collective-permute-start | bytes 811016 | tf_op jit(solution)/shard_map/ppermute | solution.py:24
  16.1 7.4 %collective-permute-start.6 = (f32[264,256]{1,0:T(8,128)S(1)}, f32[264,256]{1,0:T(8,128)S(1)}, u32[]{:S(2)}, u32[]{:S(2)}) collective-permute-start(f32[264,256]{1,0:T(8,128)S(1)} %collective-permute-done.5), channel_id=1, source_target_pairs={{0,2},{1,3},{2,0},{3,1},{4,6},{5,7},{6,4},{7,5},{8,10},{9,11},{10,... | collective-permute-start | bytes 811016 | tf_op jit(solution)/shard_map/ppermute | solution.py:24
  22.0 5.9 %copy-start = (bf16[512,1024]{1,0:T(8,128)(2,1)S(1)}, bf16[512,1024]{1,0:T(8,128)(2,1)}, u32[]{:S(2)}) copy-start(bf16[512,1024]{1,0:T(8,128)(2,1)} %get-tuple-element.83.refs_6_.refs_4_) | copy-start | bytes 3145732
  23.6 2.6 %collective-permute-start.9 = (f32[136,256]{1,0:T(8,128)S(1)}, f32[136,256]{1,0:T(8,128)S(1)}, u32[]{:S(2)}, u32[]{:S(2)}) collective-permute-start(f32[136,256]{1,0:T(8,128)S(1)} %slice_select_fusion), channel_id=1, source_target_pairs={{0,1},{1,0},{2,3},{3,2},{4,5},{5,4},{6,7},{7,6},{8,9},{9,8},{10,11... | collective-permute-start | bytes 417800 | tf_op jit(solution)/shard_map/ppermute | solution.py:24
  23.7 1.7 %collective-permute-start.7 = (f32[264,256]{1,0:T(8,128)S(1)}, f32[264,256]{1,0:T(8,128)S(1)}, u32[]{:S(2)}, u32[]{:S(2)}) collective-permute-start(f32[264,256]{1,0:T(8,128)S(1)} %broadcast_select_fusion), channel_id=1, source_target_pairs={{0,1},{1,0},{2,3},{3,2},{4,5},{5,4},{6,7},{7,6},{8,9},{9,8},{10,11... | collective-permute-start | bytes 811016 | tf_op jit(solution)/shard_map/ppermute | solution.py:24
  24.3 1.9 %collective-permute-start.8 = (f32[128,256]{1,0:T(8,128)S(1)}, f32[128,256]{1,0:T(8,128)S(1)}, u32[]{:S(2)}, u32[]{:S(2)}) collective-permute-start(f32[128,256]{1,0:T(8,128)S(1)} %slice_select_fusion.1), channel_id=1, source_target_pairs={{0,1},{1,0},{2,3},{3,2},{4,5},{5,4},{6,7},{7,6},{8,9},{9,8},{10,11... | collective-permute-start | bytes 393224 | tf_op jit(solution)/shard_map/ppermute | solution.py:24
  27.5 2.0 %collective-permute-start.10 = (f32[512,256]{1,0:T(8,128)S(1)}, f32[512,256]{1,0:T(8,128)S(1)}, u32[]{:S(2)}, u32[]{:S(2)}) collective-permute-start(f32[512,256]{1,0:T(8,128)S(1)} %get-tuple-element.91.refs_2_), channel_id=1, source_target_pairs={{0,1},{1,0},{2,3},{3,2},{4,5},{5,4},{6,7},{7,6},{8,9},{9,8},{10,11... | collective-permute-start | bytes 1572872 | tf_op jit(solution)/shard_map/ppermute | solution.py:24
  31.1 1.6 %collective-permute-start.11 = (f32[256,256]{1,0:T(8,128)S(1)}, f32[256,256]{1,0:T(8,128)S(1)}, u32[]{:S(2)}, u32[]{:S(2)}) collective-permute-start(f32[256,256]{1,0:T(8,128)S(1)} %get-tuple-element.97), channel_id=1, source_target_pairs={{0,1},{1,0},{2,3},{3,2},{4,5},{5,4},{6,7},{7,6},{8,9},{9,8},{10,11... | collective-permute-start | bytes 786440 | tf_op jit(solution)/shard_map/ppermute | solution.py:24
  32.8 8.6 %collective-permute-start.14 = (f32[256,256]{1,0:T(8,128)S(1)}, f32[256,256]{1,0:T(8,128)S(1)}, u32[]{:S(2)}, u32[]{:S(2)}) collective-permute-start(f32[256,256]{1,0:T(8,128)S(1)} %add.23.refs_0_.refs_1_), channel_id=1, source_target_pairs={{0,2},{1,3},{2,0},{3,1},{4,6},{5,7},{6,4},{7,5},{8,10},{9,11},{10,... | collective-permute-start | bytes 786440 | tf_op jit(solution)/shard_map/ppermute | solution.py:24
  34.1 4.2 %collective-permute-start.13 = (f32[128,256]{1,0:T(8,128)S(1)}, f32[128,256]{1,0:T(8,128)S(1)}, u32[]{:S(2)}, u32[]{:S(2)}) collective-permute-start(f32[128,256]{1,0:T(8,128)S(1)} %get-tuple-element.145), channel_id=1, source_target_pairs={{0,1},{1,0},{2,3},{3,2},{4,5},{5,4},{6,7},{7,6},{8,9},{9,8},{10,11... | collective-permute-start | bytes 393224 | tf_op jit(solution)/shard_map/ppermute | solution.py:24
  34.3 4.1 %collective-permute-start.12 = (f32[128,256]{1,0:T(8,128)S(1)}, f32[128,256]{1,0:T(8,128)S(1)}, u32[]{:S(2)}, u32[]{:S(2)}) collective-permute-start(f32[128,256]{1,0:T(8,128)S(1)} %get-tuple-element.146), channel_id=1, source_target_pairs={{0,1},{1,0},{2,3},{3,2},{4,5},{5,4},{6,7},{7,6},{8,9},{9,8},{10,11... | collective-permute-start | bytes 393224 | tf_op jit(solution)/shard_map/ppermute | solution.py:24
  41.4 1.5 %collective-permute-start.15 = (f32[256,256]{1,0:T(8,128)S(1)}, f32[256,256]{1,0:T(8,128)S(1)}, u32[]{:S(2)}, u32[]{:S(2)}) collective-permute-start(f32[256,256]{1,0:T(8,128)S(1)} %collective-permute-done.14.refs_3_), channel_id=1, source_target_pairs={{0,1},{1,0},{2,3},{3,2},{4,5},{5,4},{6,7},{7,6},{8,9},{9,8},{10,11... | collective-permute-start | bytes 786440 | tf_op jit(solution)/shard_map/ppermute | solution.py:24
  43.3 1.6 %collective-permute-start.16 = (f32[256,256]{1,0:T(8,128)S(1)}, f32[256,256]{1,0:T(8,128)S(1)}, u32[]{:S(2)}, u32[]{:S(2)}) collective-permute-start(f32[256,256]{1,0:T(8,128)S(1)} %shard_map.88), channel_id=1, source_target_pairs={{0,1},{1,0},{2,3},{3,2},{4,5},{5,4},{6,7},{7,6},{8,9},{9,8},{10,11... | collective-permute-start | bytes 786440 | tf_op jit(solution)/shard_map/ppermute | solution.py:24
  44.9 8.4 %collective-permute-start.17 = (f32[256,256]{1,0:T(8,128)S(1)}, f32[256,256]{1,0:T(8,128)S(1)}, u32[]{:S(2)}, u32[]{:S(2)}) collective-permute-start(f32[256,256]{1,0:T(8,128)S(1)} %add.24.refs_0_), channel_id=1, source_target_pairs={{0,2},{1,3},{2,0},{3,1},{4,6},{5,7},{6,4},{7,5},{8,10},{9,11},{10,... | collective-permute-start | bytes 786440 | tf_op jit(solution)/shard_map/ppermute | solution.py:24
  51.0 7.3 %collective-permute-start.20 = (f32[256,512]{1,0:T(8,128)S(1)}, f32[256,512]{1,0:T(8,128)S(1)}, u32[]{:S(2)}, u32[]{:S(2)}) collective-permute-start(f32[256,512]{1,0:T(8,128)S(1)} %get-tuple-element.117), channel_id=1, source_target_pairs={{0,1},{1,0},{2,3},{3,2},{4,5},{5,4},{6,7},{7,6},{8,9},{9,8},{10,11... | collective-permute-start | bytes 1572872 | tf_op jit(solution)/shard_map/ppermute | solution.py:24
  53.4 7.6 %collective-permute-start.21 = (f32[256,256]{1,0:T(8,128)S(1)}, f32[256,256]{1,0:T(8,128)S(1)}, u32[]{:S(2)}, u32[]{:S(2)}) collective-permute-start(f32[256,256]{1,0:T(8,128)S(1)} %add.25.refs_1_), channel_id=1, source_target_pairs={{0,4},{1,5},{2,6},{3,7},{4,0},{5,1},{6,2},{7,3},{8,12},{9,13},{10,... | collective-permute-start | bytes 786440 | tf_op jit(solution)/shard_map/ppermute | solution.py:24
  55.0 1.4 %collective-permute-start.19 = (f32[128,256]{1,0:T(8,128)S(1)}, f32[128,256]{1,0:T(8,128)S(1)}, u32[]{:S(2)}, u32[]{:S(2)}) collective-permute-start(f32[128,256]{1,0:T(8,128)S(1)} %get-tuple-element.143), channel_id=1, source_target_pairs={{0,1},{1,0},{2,3},{3,2},{4,5},{5,4},{6,7},{7,6},{8,9},{9,8},{10,11... | collective-permute-start | bytes 393224 | tf_op jit(solution)/shard_map/ppermute | solution.py:24
  55.0 1.5 %collective-permute-start.18 = (f32[128,256]{1,0:T(8,128)S(1)}, f32[128,256]{1,0:T(8,128)S(1)}, u32[]{:S(2)}, u32[]{:S(2)}) collective-permute-start(f32[128,256]{1,0:T(8,128)S(1)} %get-tuple-element.144), channel_id=1, source_target_pairs={{0,1},{1,0},{2,3},{3,2},{4,5},{5,4},{6,7},{7,6},{8,9},{9,8},{10,11... | collective-permute-start | bytes 393224 | tf_op jit(solution)/shard_map/ppermute | solution.py:24
  60.9 1.5 %collective-permute-start.22 = (f32[256,256]{1,0:T(8,128)S(1)}, f32[256,256]{1,0:T(8,128)S(1)}, u32[]{:S(2)}, u32[]{:S(2)}) collective-permute-start(f32[256,256]{1,0:T(8,128)S(1)} %get-tuple-element.127), channel_id=1, source_target_pairs={{0,1},{1,0},{2,3},{3,2},{4,5},{5,4},{6,7},{7,6},{8,9},{9,8},{10,11... | collective-permute-start | bytes 786440 | tf_op jit(solution)/shard_map/ppermute | solution.py:24
  60.9 1.9 %collective-permute-start.23 = (f32[256,256]{1,0:T(8,128)S(1)}, f32[256,256]{1,0:T(8,128)S(1)}, u32[]{:S(2)}, u32[]{:S(2)}) collective-permute-start(f32[256,256]{1,0:T(8,128)S(1)} %collective-permute-done.21.refs_3_), channel_id=1, source_target_pairs={{0,1},{1,0},{2,3},{3,2},{4,5},{5,4},{6,7},{7,6},{8,9},{9,8},{10,11... | collective-permute-start | bytes 786440 | tf_op jit(solution)/shard_map/ppermute | solution.py:24
  63.2 5.9 %collective-permute-start.26 = (f32[128,256]{1,0:T(8,128)S(1)}, f32[128,256]{1,0:T(8,128)S(1)}, u32[]{:S(2)}, u32[]{:S(2)}) collective-permute-start(f32[128,256]{1,0:T(8,128)S(1)} %get-tuple-element.141), channel_id=1, source_target_pairs={{0,4},{1,3},{2,6},{3,1},{4,0},{5,7},{6,2},{7,5},{8,12},{9,11},{10,... | collective-permute-start | bytes 393224 | tf_op jit(solution)/shard_map/ppermute | solution.py:24
  64.7 5.0 %collective-permute-start.24 = (f32[128,256]{1,0:T(8,128)S(1)}, f32[128,256]{1,0:T(8,128)S(1)}, u32[]{:S(2)}, u32[]{:S(2)}) collective-permute-start(f32[128,256]{1,0:T(8,128)S(1)} %get-tuple-element.142), channel_id=1, source_target_pairs={{0,4},{1,3},{2,6},{3,1},{4,0},{5,7},{6,2},{7,5},{8,12},{9,11},{10,... | collective-permute-start | bytes 393224 | tf_op jit(solution)/shard_map/ppermute | solution.py:24
  69.8 5.0 %collective-permute-start.27 = (f32[128,256]{1,0:T(8,128)S(1)}, f32[128,256]{1,0:T(8,128)S(1)}, u32[]{:S(2)}, u32[]{:S(2)}) collective-permute-start(f32[128,256]{1,0:T(8,128)S(1)} %get-tuple-element.139), channel_id=1, source_target_pairs={{0,2},{1,5},{2,0},{3,7},{4,6},{5,1},{6,4},{7,3},{8,10},{9,13},{10,... | collective-permute-start | bytes 393224 | tf_op jit(solution)/shard_map/ppermute | solution.py:24
  71.1 5.9 %collective-permute-start.25 = (f32[128,256]{1,0:T(8,128)S(1)}, f32[128,256]{1,0:T(8,128)S(1)}, u32[]{:S(2)}, u32[]{:S(2)}) collective-permute-start(f32[128,256]{1,0:T(8,128)S(1)} %get-tuple-element.140), channel_id=1, source_target_pairs={{0,2},{1,5},{2,0},{3,7},{4,6},{5,1},{6,4},{7,3},{8,10},{9,13},{10,... | collective-permute-start | bytes 393224 | tf_op jit(solution)/shard_map/ppermute | solution.py:24
  74.8 6.6 %collective-permute-start.33 = (f32[128,256]{1,0:T(8,128)S(1)}, f32[128,256]{1,0:T(8,128)S(1)}, u32[]{:S(2)}, u32[]{:S(2)}) collective-permute-start(f32[128,256]{1,0:T(8,128)S(1)} %add.29.refs_2_), channel_id=1, source_target_pairs={{0,8},{1,9},{2,10},{3,11},{4,12},{5,13},{6,14},{7,15},{8,0},{9,1},... | collective-permute-start | bytes 393224 | tf_op jit(solution)/shard_map/ppermute | solution.py:24
  76.9 2.0 %collective-permute-start.31 = (f32[64,256]{1,0:T(8,128)S(1)}, f32[64,256]{1,0:T(8,128)S(1)}, u32[]{:S(2)}, u32[]{:S(2)}) collective-permute-start(f32[64,256]{1,0:T(8,128)S(1)} %get-tuple-element.147), channel_id=1, source_target_pairs={{0,1},{1,0},{2,3},{3,2},{4,5},{5,4},{6,7},{7,6},{8,9},{9,8},{10,11... | collective-permute-start | bytes 196616 | tf_op jit(solution)/shard_map/ppermute | solution.py:24
  77.1 6.0 %collective-permute-start.32 = (f32[128,256]{1,0:T(8,128)S(1)}, f32[128,256]{1,0:T(8,128)S(1)}, u32[]{:S(2)}, u32[]{:S(2)}) collective-permute-start(f32[128,256]{1,0:T(8,128)S(1)} %add.27.refs_1_), channel_id=1, source_target_pairs={{0,8},{1,9},{2,10},{3,11},{4,12},{5,13},{6,14},{7,15},{8,0},{9,1},... | collective-permute-start | bytes 393224 | tf_op jit(solution)/shard_map/ppermute | solution.py:24
  78.4 1.3 %collective-permute-start.30 = (f32[64,256]{1,0:T(8,128)S(1)}, f32[64,256]{1,0:T(8,128)S(1)}, u32[]{:S(2)}, u32[]{:S(2)}) collective-permute-start(f32[64,256]{1,0:T(8,128)S(1)} %get-tuple-element.148), channel_id=1, source_target_pairs={{0,1},{1,0},{2,3},{3,2},{4,5},{5,4},{6,7},{7,6},{8,9},{9,8},{10,11... | collective-permute-start | bytes 196616 | tf_op jit(solution)/shard_map/ppermute | solution.py:24
  78.4 1.4 %collective-permute-start.29 = (f32[64,256]{1,0:T(8,128)S(1)}, f32[64,256]{1,0:T(8,128)S(1)}, u32[]{:S(2)}, u32[]{:S(2)}) collective-permute-start(f32[64,256]{1,0:T(8,128)S(1)} %get-tuple-element.149), channel_id=1, source_target_pairs={{0,1},{1,0},{2,3},{3,2},{4,5},{5,4},{6,7},{7,6},{8,9},{9,8},{10,11... | collective-permute-start | bytes 196616 | tf_op jit(solution)/shard_map/ppermute | solution.py:24
  78.9 1.3 %collective-permute-start.28 = (f32[64,256]{1,0:T(8,128)S(1)}, f32[64,256]{1,0:T(8,128)S(1)}, u32[]{:S(2)}, u32[]{:S(2)}) collective-permute-start(f32[64,256]{1,0:T(8,128)S(1)} %get-tuple-element.150), channel_id=1, source_target_pairs={{0,1},{1,0},{2,3},{3,2},{4,5},{5,4},{6,7},{7,6},{8,9},{9,8},{10,11... | collective-permute-start | bytes 196616 | tf_op jit(solution)/shard_map/ppermute | solution.py:24
  81.4 2.0 %collective-permute-start.35 = (f32[128,256]{1,0:T(8,128)S(1)}, f32[128,256]{1,0:T(8,128)S(1)}, u32[]{:S(2)}, u32[]{:S(2)}) collective-permute-start(f32[128,256]{1,0:T(8,128)S(1)} %collective-permute-done.33.refs_4_), channel_id=1, source_target_pairs={{0,1},{1,0},{2,3},{3,2},{4,5},{5,4},{6,7},{7,6},{8,9},{9,8},{10,11... | collective-permute-start | bytes 393224 | tf_op jit(solution)/shard_map/ppermute | solution.py:24
  83.0 1.3 %collective-permute-start.34 = (f32[128,256]{1,0:T(8,128)S(1)}, f32[128,256]{1,0:T(8,128)S(1)}, u32[]{:S(2)}, u32[]{:S(2)}) collective-permute-start(f32[128,256]{1,0:T(8,128)S(1)} %collective-permute-done.32.refs_3_), channel_id=1, source_target_pairs={{0,1},{1,0},{2,3},{3,2},{4,5},{5,4},{6,7},{7,6},{8,9},{9,8},{10,11... | collective-permute-start | bytes 393224 | tf_op jit(solution)/shard_map/ppermute | solution.py:24

commit v6 on v5

--- a/solution.py
+++ b/solution.py
@@ -486,7 +486,7 @@
         exchange(jnp.where(same, across[1][at], far[at]), 1)
         for at in (slice(0, near_cut), slice(near_cut, rows + PAD))
     ]
-    total = add(add(total, passed=[far]), crossed=crossed[:1])
+    total = add(total, passed=[far], crossed=crossed[:1])
     *near, skeleton = call(
         start_body,
         two_parts(points, columns) + [((rank, columns), F32)],

time: 85.9 us -> 86 us (level)
    pallas_call x26 -> x25, Pallas kernels: 34.4 us -> 34 us  [call(): pl.pallas_call(kernel, in_specs=[spec(arg) for arg in args], out_specs=[p...]
where the time goes in v6:
time: 86 us; the launch traced here: 85.7 us
  Pallas kernels  35.1 us (41%)
  starting transfers between devices  27.7 us (32%)
  waiting for transfers between devices  19.6 us (23%)
  local copies, waits for them, and re-layouts  2.48 us (3%)
    pallas_call x25, Pallas kernels, call(): pl.pallas_call(kernel, in_specs=[spec(arg) for arg in args], out_specs=[p...  34 us
    ppermute x36, starting transfers between devices, permute(): return lax.ppermute(x, 'leaf', [(i, j) for i, j in pairs if 0 <= j < count])  27.7 us
    ppermute x36, waiting for transfers between devices, permute(): return lax.ppermute(x, 'leaf', [(i, j) for i, j in pairs if 0 <= j < count])  19.6 us
  transfers between devices with their start and end apart: 36, of which 21 were waited for; matrix products, arithmetic and copies ran while one was open for 0% of the time, Pallas kernels for 36%

profile of v6, /device:TPU:0, one launch (start us, length us, event | category | flops | bytes accessed | tf_op | source)
XLA Modules:
  0.0 85.7 jit_solution(11574143100308962806)
XLA Ops:
  0.0 0.7 pad.4.refs_0_.refs_1_
  0.7 1.0 %copy-done.1 = f32[512,256]{1,0:T(8,128)S(1)} copy-done((f32[512,256]{1,0:T(8,128)S(1)}, f32[512,256]{1,0:T(8,128)}, u32[]{:S(2)}) %copy-start.1) | copy-done | bytes 524312
  1.8 3.0 %collective-permute-start.2 = (f32[264,256]{1,0:T(8,128)S(1)}, f32[264,256]{1,0:T(8,128)S(1)}, u32[]{:S(2)}, u32[]{:S(2)}) collective-permute-start(f32[264,256]{1,0:T(8,128)S(1)} %shard_map.73.refs_2_), channel_id=1, source_target_pairs={{0,2},{1,3},{2,0},{3,1},{4,6},{5,7},{6,4},{7,5},{8,10},{9,11},{10,... | collective-permute-start | bytes 811016 | tf_op jit(solution)/shard_map/ppermute | solution.py:24
  4.9 1.3 %collective-permute-start.5 = (f32[264,256]{1,0:T(8,128)S(1)}, f32[264,256]{1,0:T(8,128)S(1)}, u32[]{:S(2)}, u32[]{:S(2)}) collective-permute-start(f32[264,256]{1,0:T(8,128)S(1)} %shard_map.74.refs_3_), channel_id=1, source_target_pairs={{2,6},{3,7},{4,0},{5,1},{6,10},{7,11},{8,4},{9,5},{10,14},{11,15},... | collective-permute-start | bytes 811016 | tf_op jit(solution)/shard_map/ppermute | solution.py:24
  6.2 2.7 %collective-permute-start.3 = (f32[264,256]{1,0:T(8,128)S(1)}, f32[264,256]{1,0:T(8,128)S(1)}, u32[]{:S(2)}, u32[]{:S(2)}) collective-permute-start(f32[264,256]{1,0:T(8,128)S(1)} %shard_map.74.refs_3_), channel_id=1, source_target_pairs={{0,2},{1,3},{2,0},{3,1},{4,6},{5,7},{6,4},{7,5},{8,10},{9,11},{10,... | collective-permute-start | bytes 811016 | tf_op jit(solution)/shard_map/ppermute | solution.py:24
  8.9 0.7 copy-done.2
  9.6 1.7 %shard_map.75 = (f32[512,256]{1,0:T(8,128)S(1)}, f32[8,256]{1,0:T(8,128)S(1)}) custom-call(f32[8,512]{1,0:T(8,128)S(1)} %pad.4.refs_0_.refs_1_, s32[1,4]{1,0:T(1,128)S(1)} %copy-done.2, f32[264,256]{1,0:T(8,128)S(1)} %shard_map.73.refs_2_, f32[264,256]{1,0:T(8,128)S(1)} %shard_map.74.refs_3_), custom_call_target="tpu_custom_call" | custom-call | tf_op jit(solution)/shard_map/pallas_call | solution.py:118
  12.1 4.0 %collective-permute-start.4 = (f32[264,256]{1,0:T(8,128)S(1)}, f32[264,256]{1,0:T(8,128)S(1)}, u32[]{:S(2)}, u32[]{:S(2)}) collective-permute-start(f32[264,256]{1,0:T(8,128)S(1)} %collective-permute-done.2.refs_5_), channel_id=1, source_target_pairs={{0,4},{1,5},{4,8},{5,9},{6,2},{7,3},{8,12},{9,13},{10,6},{11,7},{1... | collective-permute-start | bytes 811016 | tf_op jit(solution)/shard_map/ppermute | solution.py:24
  16.2 4.1 %shard_map.78 = (bf16[512,512]{1,0:T(8,128)(2,1)S(1)}, bf16[512,512]{1,0:T(8,128)(2,1)S(1)}, bf16[512,512]{1,0:T(8,128)(2,1)S(1)}, bf16[512,512]{1,0:T(8,128)(2,...) custom-call(f32[4,512,512]{2,1,0:T(8,128)} %refs_3_.6, ...), custom_call_target="tpu_custom_call" | custom-call | tf_op jit(solution)/shard_map/pallas_call | solution.py:118
  20.3 1.7 %shard_map.76.refs_0_ = f32[512,256]{1,0:T(8,128)S(1)} custom-call(f32[512,256]{1,0:T(8,128)S(1)} %get-tuple-element.72.refs_0_, f32[8,512]{1,0:T(8,128)S(1)} %pad.4.refs_0_.refs_1_, f32[8,256]{1,0:T(8,128)S(1)} %get-tuple-element.73.refs_2_, f32[264,256]{1,0:T(8,128)S(1)} %collective-permute-done.refs_3_, f32[264,256]{1,0:T(8,128)S(1)} %collective-permute-done.1.refs_4_, ...), custom_call_target="tpu_custom_call" | custom-call | tf_op jit(solution)/shard_map/pallas_call | solution.py:118
  22.0 0.8 shard_map.77.refs_0_
  22.8 0.7 collective-permute-done.6.refs_3_
  23.7 0.6 collective-permute-start.9
  24.4 0.8 collective-permute-done.7.refs_4_
  25.2 1.2 %shard_map.79.refs_0_ = f32[512,256]{1,0:T(8,128)S(1)} custom-call(f32[512,256]{1,0:T(8,128)S(1)} %shard_map.77.refs_0_, f32[8,512]{1,0:T(8,128)S(1)} %pad.4.refs_0_.refs_1_, f32[8,256]{1,0:T(8,128)S(1)} %get-tuple-element.73.refs_2_, f32[264,256]{1,0:T(8,128)S(1)} %collective-permute-done.6.refs_3_, f32[264,256]{1,0:T(8,128)S(1)} %collective-permute-done.7.refs_4_), custom_call_target="tpu_custom_call" | custom-call | tf_op jit(solution)/shard_map/pallas_call | solution.py:118
  26.4 1.3 %shard_map.80 = (bf16[512,256]{1,0:T(8,128)(2,1)S(1)}, bf16[512,256]{1,0:T(8,128)(2,1)S(1)}, f32[512,256]{1,0:T(8,128)S(1)}) custom-call(f32[512,256]{1,0:T(8,128)S(1)} %shard_map.79.refs_0_, f32[8,512]{1,0:T(8,128)S(1)} %pad.4.refs_0_.refs_1_, f32[8,256]{1,0:T(8,128)S(1)} %get-tuple-element.73.refs_2_, f32[128,256]{1,0:T(8,128)S(1)} %collective-permute-done.8.refs_3_, ...), custom_call_target="tpu_custom_call" | custom-call | tf_op jit(solution)/shard_map/pallas_call | solution.py:118
  27.9 1.0 %shard_map.81 = (f32[512,256]{1,0:T(8,128)S(1)}, f32[512,256]{1,0:T(8,128)S(1)}) custom-call(bf16[512,256]{1,0:T(8,128)(2,1)S(1)} %get-tuple-element.89.refs_0_, bf16[512,256]{1,0:T(8,128)(2,1)S(1)} %get-tuple-element.90.refs_1_, f32[512,256]{1,0:T(8,128)S(1)} %get-tuple-element.91.refs_2_, bf16[512,512]{1,0:T(8,128)(2,1)S(1)} %get-tuple-element.80.refs_3_, ...), custom_call_target="tpu_custom_call" | custom-call | tf_op jit(solution)/shard_map/pallas_call | solution.py:118
  28.9 0.8 collective-permute-done.10.refs_2_
  29.6 1.7 %shard_map.82 = (f32[512,256]{1,0:T(8,128)S(1)}, f32[256,256]{1,0:T(8,128)S(1)}, f32[256,256]{1,0:T(8,128)S(1)}) custom-call(f32[512,256]{1,0:T(8,128)S(1)} %get-tuple-element.92.refs_0_, f32[512,256]{1,0:T(8,128)S(1)} %get-tuple-element.93.refs_1_, f32[512,256]{1,0:T(8,128)S(1)} %collective-permute-done.10.refs_2_, ...), custom_call_target="tpu_custom_call" | custom-call | tf_op jit(solution)/shard_map/pallas_call | solution.py:118
  31.5 1.4 %collective-permute-done.11 = f32[256,256]{1,0:T(8,128)S(1)} collective-permute-done((f32[256,256]{1,0:T(8,128)S(1)}, f32[256,256]{1,0:T(8,128)S(1)}, u32[]{:S(2)}, u32[]{:S(2)}) %collective-permute-start.11) | collective-permute-done | bytes 262176 | tf_op jit(solution)/shard_map/ppermute | solution.py:24
  33.0 1.3 %collective-permute-start.14 = (f32[256,256]{1,0:T(8,128)S(1)}, f32[256,256]{1,0:T(8,128)S(1)}, u32[]{:S(2)}, u32[]{:S(2)}) collective-permute-start(f32[256,256]{1,0:T(8,128)S(1)} %add.23.refs_0_.refs_1_), channel_id=1, source_target_pairs={{0,2},{1,3},{2,0},{3,1},{4,6},{5,7},{6,4},{7,5},{8,10},{9,11},{10,... | collective-permute-start | bytes 786440 | tf_op jit(solution)/shard_map/ppermute | solution.py:24
  34.9 3.6 %shard_map.83 = (bf16[512,512]{1,0:T(8,128)(2,1)S(1)}, bf16[512,512]{1,0:T(8,128)(2,1)S(1)}, bf16[2,512,256]{2,1,0:T(8,128)(2,1)S(1)}, bf16[2,512,256]{2,1,0:T(8...) custom-call(f32[256,256]{1,0:T(8,128)S(1)} %add.23.refs_0_.refs_1_, ...), custom_call_target="tpu_custom_call" | custom-call | tf_op jit(solution)/shard_map/pallas_call | solution.py:118
  38.6 2.9 %shard_map.84 = (f32[512,256]{1,0:T(8,128)S(1)}, f32[512,256]{1,0:T(8,128)S(1)}) custom-call(f32[512,256]{1,0:T(8,128)S(1)} %get-tuple-element.95.refs_0_, f32[256,256]{1,0:T(8,128)S(1)} %add.23.refs_0_.refs_1_, f32[128,256]{1,0:T(8,128)S(1)} %collective-permute-done.12.refs_2_, f32[128,256]{1,0:T(8,128)S(1)} %collective-permute-done.13.refs_3_, ...), custom_call_target="tpu_custom_call" | custom-call | tf_op jit(solution)/shard_map/pallas_call | solution.py:118
  42.0 1.1 %collective-permute-done.15.refs_3_.refs_4_ = f32[256,256]{1,0:T(8,128)S(1)} collective-permute-done((f32[256,256]{1,0:T(8,128)S(1)}, f32[256,256]{1,0:T(8,128)S(1)}, u32[]{:S(2)}, u32[]{:S(2)}) %collective-permute-start.15) | collective-permute-done | bytes 262176 | tf_op jit(solution)/shard_map/ppermute | solution.py:24
  43.9 1.1 %collective-permute-done.16 = f32[256,256]{1,0:T(8,128)S(1)} collective-permute-done((f32[256,256]{1,0:T(8,128)S(1)}, f32[256,256]{1,0:T(8,128)S(1)}, u32[]{:S(2)}, u32[]{:S(2)}) %collective-permute-start.16) | collective-permute-done | bytes 262176 | tf_op jit(solution)/shard_map/ppermute | solution.py:24
  45.1 1.1 %collective-permute-start.17 = (f32[256,256]{1,0:T(8,128)S(1)}, f32[256,256]{1,0:T(8,128)S(1)}, u32[]{:S(2)}, u32[]{:S(2)}) collective-permute-start(f32[256,256]{1,0:T(8,128)S(1)} %add.24.refs_0_), channel_id=1, source_target_pairs={{0,2},{1,3},{2,0},{3,1},{4,6},{5,7},{6,4},{7,5},{8,10},{9,11},{10,... | collective-permute-start | bytes 786440 | tf_op jit(solution)/shard_map/ppermute | solution.py:24
  46.2 4.8 %shard_map.88 = (bf16[512,512]{1,0:T(8,128)(2,1)S(1)}, bf16[512,512]{1,0:T(8,128)(2,1)S(1)}, bf16[2,512,256]{2,1,0:T(8,128)(2,1)S(1)}, bf16[2,512,256]{2,1,0:T(8...) custom-call(f32[256,256]{1,0:T(8,128)S(1)} %add.24.refs_0_, ...), custom_call_target="tpu_custom_call" | custom-call | tf_op jit(solution)/shard_map/pallas_call | solution.py:118
  51.0 0.6 shard_map.89.refs_0_
  51.6 1.9 %collective-permute-done.17 = f32[256,256]{1,0:T(8,128)S(1)} collective-permute-done((f32[256,256]{1,0:T(8,128)S(1)}, f32[256,256]{1,0:T(8,128)S(1)}, u32[]{:S(2)}, u32[]{:S(2)}) %collective-permute-start.17) | collective-permute-done | bytes 262176 | tf_op jit(solution)/shard_map/ppermute | solution.py:24
  53.5 1.6 %collective-permute-start.21 = (f32[256,256]{1,0:T(8,128)S(1)}, f32[256,256]{1,0:T(8,128)S(1)}, u32[]{:S(2)}, u32[]{:S(2)}) collective-permute-start(f32[256,256]{1,0:T(8,128)S(1)} %add.25.refs_1_), channel_id=1, source_target_pairs={{0,4},{1,5},{2,6},{3,7},{4,0},{5,1},{6,2},{7,3},{8,12},{9,13},{10,... | collective-permute-start | bytes 786440 | tf_op jit(solution)/shard_map/ppermute | solution.py:24
  55.7 0.8 collective-permute-done.18.refs_2_
  56.7 1.7 %shard_map.90 = (f32[512,256]{1,0:T(8,128)S(1)}, f32[256,256]{1,0:T(8,128)S(1)}, f32[256,256]{1,0:T(8,128)S(1)}) custom-call(f32[512,256]{1,0:T(8,128)S(1)} %shard_map.89.refs_0_, f32[256,256]{1,0:T(8,128)S(1)} %add.25.refs_1_, f32[128,256]{1,0:T(8,128)S(1)} %collective-permute-done.18.refs_2_, f32[128,256]{1,0:T(8,128)S(1)} %collective-permute-done.19.refs_3_, ...), custom_call_target="tpu_custom_call" | custom-call | tf_op jit(solution)/shard_map/pallas_call | solution.py:118
  58.6 2.5 %collective-permute-done.21.refs_3_ = f32[256,256]{1,0:T(8,128)S(1)} collective-permute-done((f32[256,256]{1,0:T(8,128)S(1)}, f32[256,256]{1,0:T(8,128)S(1)}, u32[]{:S(2)}, u32[]{:S(2)}) %collective-permute-start.21) | collective-permute-done | bytes 262176 | tf_op jit(solution)/shard_map/ppermute | solution.py:24
  61.9 0.7 collective-permute-done.22.refs_1_
  63.3 1.6 %collective-permute-start.26 = (f32[128,256]{1,0:T(8,128)S(1)}, f32[128,256]{1,0:T(8,128)S(1)}, u32[]{:S(2)}, u32[]{:S(2)}) collective-permute-start(f32[128,256]{1,0:T(8,128)S(1)} %get-tuple-element.141), channel_id=1, source_target_pairs={{0,4},{1,3},{2,6},{3,1},{4,0},{5,7},{6,2},{7,5},{8,12},{9,11},{10,... | collective-permute-start | bytes 393224 | tf_op jit(solution)/shard_map/ppermute | solution.py:24
  64.9 0.5 collective-permute-start.24
  65.4 3.2 %shard_map.94 = (bf16[512,512]{1,0:T(8,128)(2,1)S(1)}, bf16[512,512]{1,0:T(8,128)(2,1)S(1)}, bf16[2,512,256]{2,1,0:T(8,128)(2,1)S(1)}, bf16[2,512,256]{2,1,0:T(8...) custom-call(f32[256,256]{1,0:T(8,128)S(1)} %shard_map.93.refs_0_, f32[4,512,512]{2,1,0:T(8,128)} %refs_1_.13, ...), custom_call_target="tpu_custom_call" | custom-call | tf_op jit(solution)/shard_map/pallas_call | solution.py:118
  68.6 0.6 shard_map.95.refs_0_
  69.2 0.7 collective-permute-done.24
  69.9 1.1 %collective-permute-start.25 = (f32[128,256]{1,0:T(8,128)S(1)}, f32[128,256]{1,0:T(8,128)S(1)}, u32[]{:S(2)}, u32[]{:S(2)}) collective-permute-start(f32[128,256]{1,0:T(8,128)S(1)} %get-tuple-element.140), channel_id=1, source_target_pairs={{0,2},{1,5},{2,0},{3,7},{4,6},{5,1},{6,4},{7,3},{8,10},{9,13},{10,... | collective-permute-start | bytes 393224 | tf_op jit(solution)/shard_map/ppermute | solution.py:24
  71.0 1.0 %collective-permute-start.27 = (f32[128,256]{1,0:T(8,128)S(1)}, f32[128,256]{1,0:T(8,128)S(1)}, u32[]{:S(2)}, u32[]{:S(2)}) collective-permute-start(f32[128,256]{1,0:T(8,128)S(1)} %get-tuple-element.139), channel_id=1, source_target_pairs={{0,2},{1,5},{2,0},{3,7},{4,6},{5,1},{6,4},{7,3},{8,10},{9,13},{10,... | collective-permute-start | bytes 393224 | tf_op jit(solution)/shard_map/ppermute | solution.py:24
  72.0 2.9 %collective-permute-done.25 = f32[128,256]{1,0:T(8,128)S(1)} collective-permute-done((f32[128,256]{1,0:T(8,128)S(1)}, f32[128,256]{1,0:T(8,128)S(1)}, u32[]{:S(2)}, u32[]{:S(2)}) %collective-permute-start.25) | collective-permute-done | bytes 131104 | tf_op jit(solution)/shard_map/ppermute | solution.py:24
  75.0 1.9 %collective-permute-start.32 = (f32[128,256]{1,0:T(8,128)S(1)}, f32[128,256]{1,0:T(8,128)S(1)}, u32[]{:S(2)}, u32[]{:S(2)}) collective-permute-start(f32[128,256]{1,0:T(8,128)S(1)} %add.27.refs_1_), channel_id=1, source_target_pairs={{0,8},{1,9},{2,10},{3,11},{4,12},{5,13},{6,14},{7,15},{8,0},{9,1},... | collective-permute-start | bytes 393224 | tf_op jit(solution)/shard_map/ppermute | solution.py:24
  77.0 1.4 %collective-permute-start.33 = (f32[128,256]{1,0:T(8,128)S(1)}, f32[128,256]{1,0:T(8,128)S(1)}, u32[]{:S(2)}, u32[]{:S(2)}) collective-permute-start(f32[128,256]{1,0:T(8,128)S(1)} %add.29.refs_2_), channel_id=1, source_target_pairs={{0,8},{1,9},{2,10},{3,11},{4,12},{5,13},{6,14},{7,15},{8,0},{9,1},... | collective-permute-start | bytes 393224 | tf_op jit(solution)/shard_map/ppermute | solution.py:24
  79.1 0.6 collective-permute-done.29.refs_4_
  80.2 1.2 %shard_map.96.refs_0_ = f32[512,256]{1,0:T(8,128)S(1)} custom-call(f32[512,256]{1,0:T(8,128)S(1)} %shard_map.95.refs_0_, f32[128,256]{1,0:T(8,128)S(1)} %add.27.refs_1_, f32[128,256]{1,0:T(8,128)S(1)} %add.29.refs_2_, f32[64,256]{1,0:T(8,128)S(1)} %collective-permute-done.28.refs_3_, f32[64,256]{1,0:T(8,128)S(1)} %collective-permute-done.29.refs_4_, ...), custom_call_target="tpu_custom_call" | custom-call | tf_op jit(solution)/shard_map/pallas_call | solution.py:118
  81.4 1.5 %collective-permute-done.33.refs_4_ = f32[128,256]{1,0:T(8,128)S(1)} collective-permute-done((f32[128,256]{1,0:T(8,128)S(1)}, f32[128,256]{1,0:T(8,128)S(1)}, u32[]{:S(2)}, u32[]{:S(2)}) %collective-permute-start.33) | collective-permute-done | bytes 131104 | tf_op jit(solution)/shard_map/ppermute | solution.py:24
  84.5 1.1 %shard_map.98 = f32[512,256]{1,0:T(8,128)} custom-call(f32[512,256]{1,0:T(8,128)S(1)} %shard_map.97.base, bf16[2,512,256]{2,1,0:T(8,128)(2,1)S(1)} %get-tuple-element.128.refs_1_.factor_high, bf16[2,512,256]{2,1,0:T(8,128)(2,1)S(1)} %get-tuple-element.129.refs_2_.factor_low, f32[128,256]{1,0:T(8,128)S(1)} %collective-permute-done.34.refs_0_, ...), custom_call_target="tpu_custom_call" | custom-call | tf_op jit(solution)/shard_map/pallas_call | solution.py:414
  (71 shorter events, 9.0 us)
Async XLA Ops:
  0.7 1.0 %copy-start.1 = (f32[512,256]{1,0:T(8,128)S(1)}, f32[512,256]{1,0:T(8,128)}, u32[]{:S(2)}) copy-start(f32[512,256]{1,0:T(8,128)} %refs_1_.8) | copy-start | bytes 1572868
  1.8 10.3 %collective-permute-start.2 = (f32[264,256]{1,0:T(8,128)S(1)}, f32[264,256]{1,0:T(8,128)S(1)}, u32[]{:S(2)}, u32[]{:S(2)}) collective-permute-start(f32[264,256]{1,0:T(8,128)S(1)} %shard_map.73.refs_2_), channel_id=1, source_target_pairs={{0,2},{1,3},{2,0},{3,1},{4,6},{5,7},{6,4},{7,5},{8,10},{9,11},{10,... | collective-permute-start | bytes 811016 | tf_op jit(solution)/shard_map/ppermute | solution.py:24
  4.9 11.3 %collective-permute-start.5 = (f32[264,256]{1,0:T(8,128)S(1)}, f32[264,256]{1,0:T(8,128)S(1)}, u32[]{:S(2)}, u32[]{:S(2)}) collective-permute-start(f32[264,256]{1,0:T(8,128)S(1)} %shard_map.74.refs_3_), channel_id=1, source_target_pairs={{2,6},{3,7},{4,0},{5,1},{6,10},{7,11},{8,4},{9,5},{10,14},{11,15},... | collective-permute-start | bytes 811016 | tf_op jit(solution)/shard_map/ppermute | solution.py:24
  6.2 14.2 %collective-permute-start.3 = (f32[264,256]{1,0:T(8,128)S(1)}, f32[264,256]{1,0:T(8,128)S(1)}, u32[]{:S(2)}, u32[]{:S(2)}) collective-permute-start(f32[264,256]{1,0:T(8,128)S(1)} %shard_map.74.refs_3_), channel_id=1, source_target_pairs={{0,2},{1,3},{2,0},{3,1},{4,6},{5,7},{6,4},{7,5},{8,10},{9,11},{10,... | collective-permute-start | bytes 811016 | tf_op jit(solution)/shard_map/ppermute | solution.py:24
  8.9 0.7 copy-start.2
  11.3 9.0 %collective-permute-start = (f32[264,256]{1,0:T(8,128)S(1)}, f32[264,256]{1,0:T(8,128)S(1)}, u32[]{:S(2)}, u32[]{:S(2)}) collective-permute-start(f32[264,256]{1,0:T(8,128)S(1)} %shard_map.73.refs_2_), channel_id=1, source_target_pairs={{0,1},{1,0},{2,3},{3,2},{4,5},{5,4},{6,7},{7,6},{8,9},{9,8},{10,11... | collective-permute-start | bytes 811016 | tf_op jit(solution)/shard_map/ppermute | solution.py:24
  11.4 9.0 %collective-permute-start.1 = (f32[264,256]{1,0:T(8,128)S(1)}, f32[264,256]{1,0:T(8,128)S(1)}, u32[]{:S(2)}, u32[]{:S(2)}) collective-permute-start(f32[264,256]{1,0:T(8,128)S(1)} %shard_map.74.refs_3_), channel_id=1, source_target_pairs={{0,1},{1,0},{2,3},{3,2},{4,5},{5,4},{6,7},{7,6},{8,9},{9,8},{10,11... | collective-permute-start | bytes 811016 | tf_op jit(solution)/shard_map/ppermute | solution.py:24
  12.1 9.9 %collective-permute-start.4 = (f32[264,256]{1,0:T(8,128)S(1)}, f32[264,256]{1,0:T(8,128)S(1)}, u32[]{:S(2)}, u32[]{:S(2)}) collective-permute-start(f32[264,256]{1,0:T(8,128)S(1)} %collective-permute-done.2.refs_5_), channel_id=1, source_target_pairs={{0,4},{1,5},{4,8},{5,9},{6,2},{7,3},{8,12},{9,13},{10,6},{11,7},{1... | collective-permute-start | bytes 811016 | tf_op jit(solution)/shard_map/ppermute | solution.py:24
  16.1 7.4 %collective-permute-start.6 = (f32[264,256]{1,0:T(8,128)S(1)}, f32[264,256]{1,0:T(8,128)S(1)}, u32[]{:S(2)}, u32[]{:S(2)}) collective-permute-start(f32[264,256]{1,0:T(8,128)S(1)} %collective-permute-done.5), channel_id=1, source_target_pairs={{0,2},{1,3},{2,0},{3,1},{4,6},{5,7},{6,4},{7,5},{8,10},{9,11},{10,... | collective-permute-start | bytes 811016 | tf_op jit(solution)/shard_map/ppermute | solution.py:24
  20.3 7.5 %copy-start = (bf16[512,1024]{1,0:T(8,128)(2,1)S(1)}, bf16[512,1024]{1,0:T(8,128)(2,1)}, u32[]{:S(2)}) copy-start(bf16[512,1024]{1,0:T(8,128)(2,1)} %get-tuple-element.83.refs_6_.refs_4_) | copy-start | bytes 3145732
  23.6 1.6 %collective-permute-start.7 = (f32[264,256]{1,0:T(8,128)S(1)}, f32[264,256]{1,0:T(8,128)S(1)}, u32[]{:S(2)}, u32[]{:S(2)}) collective-permute-start(f32[264,256]{1,0:T(8,128)S(1)} %broadcast_select_fusion), channel_id=1, source_target_pairs={{0,1},{1,0},{2,3},{3,2},{4,5},{5,4},{6,7},{7,6},{8,9},{9,8},{10,11... | collective-permute-start | bytes 811016 | tf_op jit(solution)/shard_map/ppermute | solution.py:24
  23.7 2.7 %collective-permute-start.9 = (f32[136,256]{1,0:T(8,128)S(1)}, f32[136,256]{1,0:T(8,128)S(1)}, u32[]{:S(2)}, u32[]{:S(2)}) collective-permute-start(f32[136,256]{1,0:T(8,128)S(1)} %slice_select_fusion), channel_id=1, source_target_pairs={{0,1},{1,0},{2,3},{3,2},{4,5},{5,4},{6,7},{7,6},{8,9},{9,8},{10,11... | collective-permute-start | bytes 417800 | tf_op jit(solution)/shard_map/ppermute | solution.py:24
  24.3 2.1 %collective-permute-start.8 = (f32[128,256]{1,0:T(8,128)S(1)}, f32[128,256]{1,0:T(8,128)S(1)}, u32[]{:S(2)}, u32[]{:S(2)}) collective-permute-start(f32[128,256]{1,0:T(8,128)S(1)} %slice_select_fusion.1), channel_id=1, source_target_pairs={{0,1},{1,0},{2,3},{3,2},{4,5},{5,4},{6,7},{7,6},{8,9},{9,8},{10,11... | collective-permute-start | bytes 393224 | tf_op jit(solution)/shard_map/ppermute | solution.py:24
  27.7 2.0 %collective-permute-start.10 = (f32[512,256]{1,0:T(8,128)S(1)}, f32[512,256]{1,0:T(8,128)S(1)}, u32[]{:S(2)}, u32[]{:S(2)}) collective-permute-start(f32[512,256]{1,0:T(8,128)S(1)} %get-tuple-element.91.refs_2_), channel_id=1, source_target_pairs={{0,1},{1,0},{2,3},{3,2},{4,5},{5,4},{6,7},{7,6},{8,9},{9,8},{10,11... | collective-permute-start | bytes 1572872 | tf_op jit(solution)/shard_map/ppermute | solution.py:24
  31.3 1.6 %collective-permute-start.11 = (f32[256,256]{1,0:T(8,128)S(1)}, f32[256,256]{1,0:T(8,128)S(1)}, u32[]{:S(2)}, u32[]{:S(2)}) collective-permute-start(f32[256,256]{1,0:T(8,128)S(1)} %get-tuple-element.97), channel_id=1, source_target_pairs={{0,1},{1,0},{2,3},{3,2},{4,5},{5,4},{6,7},{7,6},{8,9},{9,8},{10,11... | collective-permute-start | bytes 786440 | tf_op jit(solution)/shard_map/ppermute | solution.py:24
  33.0 8.5 %collective-permute-start.14 = (f32[256,256]{1,0:T(8,128)S(1)}, f32[256,256]{1,0:T(8,128)S(1)}, u32[]{:S(2)}, u32[]{:S(2)}) collective-permute-start(f32[256,256]{1,0:T(8,128)S(1)} %add.23.refs_0_.refs_1_), channel_id=1, source_target_pairs={{0,2},{1,3},{2,0},{3,1},{4,6},{5,7},{6,4},{7,5},{8,10},{9,11},{10,... | collective-permute-start | bytes 786440 | tf_op jit(solution)/shard_map/ppermute | solution.py:24
  34.3 4.2 %collective-permute-start.12 = (f32[128,256]{1,0:T(8,128)S(1)}, f32[128,256]{1,0:T(8,128)S(1)}, u32[]{:S(2)}, u32[]{:S(2)}) collective-permute-start(f32[128,256]{1,0:T(8,128)S(1)} %get-tuple-element.146), channel_id=1, source_target_pairs={{0,1},{1,0},{2,3},{3,2},{4,5},{5,4},{6,7},{7,6},{8,9},{9,8},{10,11... | collective-permute-start | bytes 393224 | tf_op jit(solution)/shard_map/ppermute | solution.py:24
  34.4 4.2 %collective-permute-start.13 = (f32[128,256]{1,0:T(8,128)S(1)}, f32[128,256]{1,0:T(8,128)S(1)}, u32[]{:S(2)}, u32[]{:S(2)}) collective-permute-start(f32[128,256]{1,0:T(8,128)S(1)} %get-tuple-element.145), channel_id=1, source_target_pairs={{0,1},{1,0},{2,3},{3,2},{4,5},{5,4},{6,7},{7,6},{8,9},{9,8},{10,11... | collective-permute-start | bytes 393224 | tf_op jit(solution)/shard_map/ppermute | solution.py:24
  41.5 1.6 %collective-permute-start.15 = (f32[256,256]{1,0:T(8,128)S(1)}, f32[256,256]{1,0:T(8,128)S(1)}, u32[]{:S(2)}, u32[]{:S(2)}) collective-permute-start(f32[256,256]{1,0:T(8,128)S(1)} %collective-permute-done.14.refs_3_), channel_id=1, source_target_pairs={{0,1},{1,0},{2,3},{3,2},{4,5},{5,4},{6,7},{7,6},{8,9},{9,8},{10,11... | collective-permute-start | bytes 786440 | tf_op jit(solution)/shard_map/ppermute | solution.py:24
  43.4 1.6 %collective-permute-start.16 = (f32[256,256]{1,0:T(8,128)S(1)}, f32[256,256]{1,0:T(8,128)S(1)}, u32[]{:S(2)}, u32[]{:S(2)}) collective-permute-start(f32[256,256]{1,0:T(8,128)S(1)} %shard_map.87), channel_id=1, source_target_pairs={{0,1},{1,0},{2,3},{3,2},{4,5},{5,4},{6,7},{7,6},{8,9},{9,8},{10,11... | collective-permute-start | bytes 786440 | tf_op jit(solution)/shard_map/ppermute | solution.py:24
  45.1 8.4 %collective-permute-start.17 = (f32[256,256]{1,0:T(8,128)S(1)}, f32[256,256]{1,0:T(8,128)S(1)}, u32[]{:S(2)}, u32[]{:S(2)}) collective-permute-start(f32[256,256]{1,0:T(8,128)S(1)} %add.24.refs_0_), channel_id=1, source_target_pairs={{0,2},{1,3},{2,0},{3,1},{4,6},{5,7},{6,4},{7,5},{8,10},{9,11},{10,... | collective-permute-start | bytes 786440 | tf_op jit(solution)/shard_map/ppermute | solution.py:24
  50.9 7.5 %collective-permute-start.20 = (f32[256,512]{1,0:T(8,128)S(1)}, f32[256,512]{1,0:T(8,128)S(1)}, u32[]{:S(2)}, u32[]{:S(2)}) collective-permute-start(f32[256,512]{1,0:T(8,128)S(1)} %get-tuple-element.117), channel_id=1, source_target_pairs={{0,1},{1,0},{2,3},{3,2},{4,5},{5,4},{6,7},{7,6},{8,9},{9,8},{10,11... | collective-permute-start | bytes 1572872 | tf_op jit(solution)/shard_map/ppermute | solution.py:24
  53.5 7.6 %collective-permute-start.21 = (f32[256,256]{1,0:T(8,128)S(1)}, f32[256,256]{1,0:T(8,128)S(1)}, u32[]{:S(2)}, u32[]{:S(2)}) collective-permute-start(f32[256,256]{1,0:T(8,128)S(1)} %add.25.refs_1_), channel_id=1, source_target_pairs={{0,4},{1,5},{2,6},{3,7},{4,0},{5,1},{6,2},{7,3},{8,12},{9,13},{10,... | collective-permute-start | bytes 786440 | tf_op jit(solution)/shard_map/ppermute | solution.py:24
  55.1 1.4 %collective-permute-start.18 = (f32[128,256]{1,0:T(8,128)S(1)}, f32[128,256]{1,0:T(8,128)S(1)}, u32[]{:S(2)}, u32[]{:S(2)}) collective-permute-start(f32[128,256]{1,0:T(8,128)S(1)} %get-tuple-element.144), channel_id=1, source_target_pairs={{0,1},{1,0},{2,3},{3,2},{4,5},{5,4},{6,7},{7,6},{8,9},{9,8},{10,11... | collective-permute-start | bytes 393224 | tf_op jit(solution)/shard_map/ppermute | solution.py:24
  55.2 1.5 %collective-permute-start.19 = (f32[128,256]{1,0:T(8,128)S(1)}, f32[128,256]{1,0:T(8,128)S(1)}, u32[]{:S(2)}, u32[]{:S(2)}) collective-permute-start(f32[128,256]{1,0:T(8,128)S(1)} %get-tuple-element.143), channel_id=1, source_target_pairs={{0,1},{1,0},{2,3},{3,2},{4,5},{5,4},{6,7},{7,6},{8,9},{9,8},{10,11... | collective-permute-start | bytes 393224 | tf_op jit(solution)/shard_map/ppermute | solution.py:24
  61.1 1.5 %collective-permute-start.22 = (f32[256,256]{1,0:T(8,128)S(1)}, f32[256,256]{1,0:T(8,128)S(1)}, u32[]{:S(2)}, u32[]{:S(2)}) collective-permute-start(f32[256,256]{1,0:T(8,128)S(1)} %get-tuple-element.127), channel_id=1, source_target_pairs={{0,1},{1,0},{2,3},{3,2},{4,5},{5,4},{6,7},{7,6},{8,9},{9,8},{10,11... | collective-permute-start | bytes 786440 | tf_op jit(solution)/shard_map/ppermute | solution.py:24
  61.1 1.9 %collective-permute-start.23 = (f32[256,256]{1,0:T(8,128)S(1)}, f32[256,256]{1,0:T(8,128)S(1)}, u32[]{:S(2)}, u32[]{:S(2)}) collective-permute-start(f32[256,256]{1,0:T(8,128)S(1)} %collective-permute-done.21.refs_3_), channel_id=1, source_target_pairs={{0,1},{1,0},{2,3},{3,2},{4,5},{5,4},{6,7},{7,6},{8,9},{9,8},{10,11... | collective-permute-start | bytes 786440 | tf_op jit(solution)/shard_map/ppermute | solution.py:24
  63.3 5.9 %collective-permute-start.26 = (f32[128,256]{1,0:T(8,128)S(1)}, f32[128,256]{1,0:T(8,128)S(1)}, u32[]{:S(2)}, u32[]{:S(2)}) collective-permute-start(f32[128,256]{1,0:T(8,128)S(1)} %get-tuple-element.141), channel_id=1, source_target_pairs={{0,4},{1,3},{2,6},{3,1},{4,0},{5,7},{6,2},{7,5},{8,12},{9,11},{10,... | collective-permute-start | bytes 393224 | tf_op jit(solution)/shard_map/ppermute | solution.py:24
  64.9 5.0 %collective-permute-start.24 = (f32[128,256]{1,0:T(8,128)S(1)}, f32[128,256]{1,0:T(8,128)S(1)}, u32[]{:S(2)}, u32[]{:S(2)}) collective-permute-start(f32[128,256]{1,0:T(8,128)S(1)} %get-tuple-element.142), channel_id=1, source_target_pairs={{0,4},{1,3},{2,6},{3,1},{4,0},{5,7},{6,2},{7,5},{8,12},{9,11},{10,... | collective-permute-start | bytes 393224 | tf_op jit(solution)/shard_map/ppermute | solution.py:24
  69.9 5.0 %collective-permute-start.25 = (f32[128,256]{1,0:T(8,128)S(1)}, f32[128,256]{1,0:T(8,128)S(1)}, u32[]{:S(2)}, u32[]{:S(2)}) collective-permute-start(f32[128,256]{1,0:T(8,128)S(1)} %get-tuple-element.140), channel_id=1, source_target_pairs={{0,2},{1,5},{2,0},{3,7},{4,6},{5,1},{6,4},{7,3},{8,10},{9,13},{10,... | collective-permute-start | bytes 393224 | tf_op jit(solution)/shard_map/ppermute | solution.py:24
  71.0 5.9 %collective-permute-start.27 = (f32[128,256]{1,0:T(8,128)S(1)}, f32[128,256]{1,0:T(8,128)S(1)}, u32[]{:S(2)}, u32[]{:S(2)}) collective-permute-start(f32[128,256]{1,0:T(8,128)S(1)} %get-tuple-element.139), channel_id=1, source_target_pairs={{0,2},{1,5},{2,0},{3,7},{4,6},{5,1},{6,4},{7,3},{8,10},{9,13},{10,... | collective-permute-start | bytes 393224 | tf_op jit(solution)/shard_map/ppermute | solution.py:24
  75.0 6.4 %collective-permute-start.32 = (f32[128,256]{1,0:T(8,128)S(1)}, f32[128,256]{1,0:T(8,128)S(1)}, u32[]{:S(2)}, u32[]{:S(2)}) collective-permute-start(f32[128,256]{1,0:T(8,128)S(1)} %add.27.refs_1_), channel_id=1, source_target_pairs={{0,8},{1,9},{2,10},{3,11},{4,12},{5,13},{6,14},{7,15},{8,0},{9,1},... | collective-permute-start | bytes 393224 | tf_op jit(solution)/shard_map/ppermute | solution.py:24
  76.9 2.0 %collective-permute-start.28 = (f32[64,256]{1,0:T(8,128)S(1)}, f32[64,256]{1,0:T(8,128)S(1)}, u32[]{:S(2)}, u32[]{:S(2)}) collective-permute-start(f32[64,256]{1,0:T(8,128)S(1)} %get-tuple-element.150), channel_id=1, source_target_pairs={{0,1},{1,0},{2,3},{3,2},{4,5},{5,4},{6,7},{7,6},{8,9},{9,8},{10,11... | collective-permute-start | bytes 196616 | tf_op jit(solution)/shard_map/ppermute | solution.py:24
  77.0 5.9 %collective-permute-start.33 = (f32[128,256]{1,0:T(8,128)S(1)}, f32[128,256]{1,0:T(8,128)S(1)}, u32[]{:S(2)}, u32[]{:S(2)}) collective-permute-start(f32[128,256]{1,0:T(8,128)S(1)} %add.29.refs_2_), channel_id=1, source_target_pairs={{0,8},{1,9},{2,10},{3,11},{4,12},{5,13},{6,14},{7,15},{8,0},{9,1},... | collective-permute-start | bytes 393224 | tf_op jit(solution)/shard_map/ppermute | solution.py:24
  78.4 1.3 %collective-permute-start.29 = (f32[64,256]{1,0:T(8,128)S(1)}, f32[64,256]{1,0:T(8,128)S(1)}, u32[]{:S(2)}, u32[]{:S(2)}) collective-permute-start(f32[64,256]{1,0:T(8,128)S(1)} %get-tuple-element.149), channel_id=1, source_target_pairs={{0,1},{1,0},{2,3},{3,2},{4,5},{5,4},{6,7},{7,6},{8,9},{9,8},{10,11... | collective-permute-start | bytes 196616 | tf_op jit(solution)/shard_map/ppermute | solution.py:24
  78.6 1.3 %collective-permute-start.30 = (f32[64,256]{1,0:T(8,128)S(1)}, f32[64,256]{1,0:T(8,128)S(1)}, u32[]{:S(2)}, u32[]{:S(2)}) collective-permute-start(f32[64,256]{1,0:T(8,128)S(1)} %get-tuple-element.148), channel_id=1, source_target_pairs={{0,1},{1,0},{2,3},{3,2},{4,5},{5,4},{6,7},{7,6},{8,9},{9,8},{10,11... | collective-permute-start | bytes 196616 | tf_op jit(solution)/shard_map/ppermute | solution.py:24
  79.0 1.3 %collective-permute-start.31 = (f32[64,256]{1,0:T(8,128)S(1)}, f32[64,256]{1,0:T(8,128)S(1)}, u32[]{:S(2)}, u32[]{:S(2)}) collective-permute-start(f32[64,256]{1,0:T(8,128)S(1)} %get-tuple-element.147), channel_id=1, source_target_pairs={{0,1},{1,0},{2,3},{3,2},{4,5},{5,4},{6,7},{7,6},{8,9},{9,8},{10,11... | collective-permute-start | bytes 196616 | tf_op jit(solution)/shard_map/ppermute | solution.py:24
  82.9 1.3 %collective-permute-start.34 = (f32[128,256]{1,0:T(8,128)S(1)}, f32[128,256]{1,0:T(8,128)S(1)}, u32[]{:S(2)}, u32[]{:S(2)}) collective-permute-start(f32[128,256]{1,0:T(8,128)S(1)} %collective-permute-done.32.refs_3_), channel_id=1, source_target_pairs={{0,1},{1,0},{2,3},{3,2},{4,5},{5,4},{6,7},{7,6},{8,9},{9,8},{10,11... | collective-permute-start | bytes 393224 | tf_op jit(solution)/shard_map/ppermute | solution.py:24
  82.9 1.5 %collective-permute-start.35 = (f32[128,256]{1,0:T(8,128)S(1)}, f32[128,256]{1,0:T(8,128)S(1)}, u32[]{:S(2)}, u32[]{:S(2)}) collective-permute-start(f32[128,256]{1,0:T(8,128)S(1)} %collective-permute-done.33.refs_4_), channel_id=1, source_target_pairs={{0,1},{1,0},{2,3},{3,2},{4,5},{5,4},{6,7},{7,6},{8,9},{9,8},{10,11... | collective-permute-start | bytes 393224 | tf_op jit(solution)/shard_map/ppermute | solution.py:24
